TPU v7x, 32 devices: a whole 2x2x4 slice. The times are simulated.
32 devices in a mesh: groups: 2 (over y), rows: 4 (over x, core), cols: 4 (over z).
Axes of the slice: x: 2, y: 2, z: 4, core: 2. Of those that a mesh axis runs over, the one named last changes fastest.
Arguments:
- iterate: float32 [8192, 8192], P(('groups', 'rows'), 'cols'), parts along dimension 0, may hold values from -1 to 1
Outputs:
- update: float32 [8192, 8192], P(('groups', 'rows'), 'cols'), parts along dimension 0
There are 2 independent parts, one for each index of `groups`. A program takes and returns all parts, laid end to end along the dimension named above; each array names one. Nothing has to cross between parts.
All inputs are finite; a program needn't handle non-finite values.
Results may differ from a plain program's by a relative error of at most 0.0042.
Values may be sent and summed in bfloat16 or wider, within the bound.
No kernel may reach another device: no remote copies, remote signals or barrier semaphores. Data moves between devices by JAX's collectives and lax.ppermute only.
A program may use at most 128 MiB of HBM per device.

v0:
```python
import math

import jax
import jax.numpy as jnp
from jax import lax
from jax.sharding import PartitionSpec as P

HEIGHT = 4096
BREADTH = 8192


coef_a = 3.4445
coef_b = -4.775
coef_c = 2.0315


def on_device(iterate):
    x_local = iterate.astype(jnp.bfloat16)
    partial_gram = lax.dot_general(
        x_local,
        lax.all_gather(x_local, "rows", axis=0, tiled=True),
        (((1,), (1,)), ((), ())),
        preferred_element_type=jnp.float32,
    )
    gram_block = lax.psum_scatter(partial_gram, "cols", scatter_dimension=1, tiled=True)
    block_half = gram_block.astype(jnp.bfloat16)
    row_half = lax.all_gather(block_half, "cols", axis=1, tiled=True)
    left_part = row_half
    square = jnp.dot(
        left_part,
        lax.all_gather(block_half, "rows", axis=0, tiled=True),
        preferred_element_type=jnp.float32,
    )
    poly_block = (coef_b * gram_block + coef_c * square).astype(jnp.bfloat16)
    poly_rows = lax.all_gather(poly_block, "cols", axis=1, tiled=True)
    left_part = poly_rows
    applied = jnp.dot(
        left_part,
        lax.all_gather(x_local, "rows", axis=0, tiled=True),
        preferred_element_type=jnp.float32,
    )
    factor = 0.2 * math.sqrt(max(HEIGHT, BREADTH))
    return factor * (coef_a * iterate + applied)


def solution(mesh):
    return jax.shard_map(
        on_device,
        mesh=mesh,
        in_specs=(P(("groups", "rows"), "cols"),),
        out_specs=P(("groups", "rows"), "cols"),
        check_vma=False,
    )
```

profile of v0, /device:TPU:0, one launch (start us, length us, event | category | flops | bytes accessed | tf_op | source)
XLA Modules:
  0.0 834.3 jit_solution(8380458705238469455)
XLA Ops:
  6.5 0.0 all-gather.5.cloned.1.call-start
  6.5 6.0 convert_element_type.9
  12.6 0.0 all-gather.5.cloned.1.call-update
  12.6 0.0 reduce-scatter.2.cloned.1.call-start
  12.7 108.7 %all-gather.5.cloned.1.call-done = bf16[4096,2048]{1,0:T(8,128)(2,1)} async-done(((bf16[1024,2048]{1,0:T(8,128)(2,1)}), bf16[4096,2048]{1,0:T(8,128)(2,1)}) %all-gather.5.cloned.1.call-update) | async-done | bytes 16777232 | tf_op jit(solution)/shard_map/all_gather | solution.py:21
  121.4 23.6 %fusion = f32[1024,4096]{1,0:T(8,128)} fusion(bf16[1024,2048]{1,0:T(8,128)(2,1)} %convert_element_type.9, bf16[4096,2048]{1,0:T(8,128)(2,1)} %all-gather.5.cloned.1.call-done), kind=kOutput, calls=%fused_computation.2 | convolution fusion | flops 17179869184 | bytes 37748736 | tf_op jit(solution)/shard_map/dot_general | solution.py:19
  145.0 0.0 reduce-scatter.2.cloned.1.call-update
  145.0 0.0 all-gather.7.cloned.1.call-start
  145.0 280.4 %reduce-scatter.2.cloned.1.call-done = f32[1024,1024]{1,0:T(8,128)} async-done(((f32[1024,4096]{1,0:T(8,128)}), f32[1024,1024]{1,0:T(8,128)}) %reduce-scatter.2.cloned.1.call-update) | async-done | bytes 4194320 | tf_op jit(solution)/shard_map/reduce_scatter | solution.py:25
  425.4 3.8 convert_element_type.10
  429.3 0.0 all-gather.7.cloned.1.call-update
  429.3 0.0 all-gather.9.cloned.1.call-start
  429.3 0.5 all-gather.9.cloned.1.call-update
  429.9 0.0 all-gather.11.cloned.1.call-start
  429.9 149.9 %all-gather.7.cloned.1.call-done = bf16[1024,4096]{1,0:T(8,128)(2,1)} async-done(((bf16[1024,1024]{1,0:T(8,128)(2,1)}), bf16[1024,4096]{1,0:T(8,128)(2,1)}) %all-gather.7.cloned.1.call-update) | async-done | bytes 8388624 | tf_op jit(solution)/shard_map/all_gather | solution.py:27
  579.8 58.0 %all-gather.9.cloned.1.call-done = bf16[4096,1024]{1,0:T(8,128)(2,1)} async-done(((bf16[1024,1024]{1,0:T(8,128)(2,1)}), bf16[4096,1024]{1,0:T(8,128)(2,1)}) %all-gather.9.cloned.1.call-update) | async-done | bytes 8388624 | tf_op jit(solution)/shard_map/all_gather | solution.py:31
  637.8 15.3 %add_convert_fusion = bf16[1024,1024]{1,0:T(8,128)(2,1)} fusion(f32[1024,1024]{1,0:T(8,128)} %reduce-scatter.2.cloned.1.call-done, bf16[1024,4096]{1,0:T(8,128)(2,1)} %all-gather.7.cloned.1.call-done, bf16[4096,1024]{1,0:T(8,128)(2,1)} %all-gather.9.cloned.1.call-done), kind=kOutput, calls=%fused_computation.1 | convolution fusion | flops 8594128896 | bytes 23068672 | tf_op jit(solution)/shard_map/dot_general | solution.py:29
  653.2 0.0 all-gather.11.cloned.1.call-update
  653.2 149.8 %all-gather.11.cloned.1.call-done = bf16[1024,4096]{1,0:T(8,128)(2,1)} async-done(((bf16[1024,1024]{1,0:T(8,128)(2,1)}), bf16[1024,4096]{1,0:T(8,128)(2,1)}) %all-gather.11.cloned.1.call-update) | async-done | bytes 8388624 | tf_op jit(solution)/shard_map/all_gather | solution.py:35
  803.0 24.8 %add_multiply_fusion = f32[1024,2048]{1,0:T(8,128)} fusion(f32[1024,2048]{1,0:T(8,128)} %param.1, bf16[1024,4096]{1,0:T(8,128)(2,1)} %all-gather.11.cloned.1.call-done, bf16[4096,2048]{1,0:T(8,128)(2,1)} %all-gather.5.cloned.1.call-done), kind=kOutput, calls=%fused_computation | convolution fusion | flops 17186160640 | bytes 41943040 | tf_op jit(solution)/shard_map/dot_general | solution.py:37
Async XLA Ops:
  6.5 114.9 %all-gather.5.cloned.1.call-start = ((), (), s32[]{:S(2)}) async-start(), calls=%async_computation.1 | async-start | bytes 20971520 | tf_op jit(solution)/shard_map/all_gather | solution.py:21
  12.6 412.8 %reduce-scatter.2.cloned.1.call-start = ((), (), s32[]{:S(2)}) async-start(), calls=%async_computation.2 | async-start | bytes 20971520 | tf_op jit(solution)/shard_map/reduce_scatter | solution.py:25
  145.0 434.8 %all-gather.7.cloned.1.call-start = ((), (), s32[]{:S(2)}) async-start(), calls=%async_computation.3 | async-start | bytes 10485760 | tf_op jit(solution)/shard_map/all_gather | solution.py:27
  429.3 208.5 %all-gather.9.cloned.1.call-start = ((), (), s32[]{:S(2)}) async-start(), calls=%async_computation.4 | async-start | bytes 10485760 | tf_op jit(solution)/shard_map/all_gather | solution.py:31
  429.9 373.1 %all-gather.11.cloned.1.call-start = ((), (), s32[]{:S(2)}) async-start(), calls=%async_computation.5 | async-start | bytes 10485760 | tf_op jit(solution)/shard_map/all_gather | solution.py:35
Sparse Core Ops, SparseCore 0:
  12.7 108.6 all-gather.4
  145.1 280.2 reduce-scatter.1
  429.4 150.3 all-gather.6
  581.3 56.4 all-gather.8
  653.3 149.6 all-gather.10
where the time goes:
time: 834 us
  waiting for transfers between devices  747 us (90%)
  matrix products  63.7 us (8%)
  between operations  13.1 us (2%)
  other arithmetic  9.88 us (1%)
    reduce_scatter x1, waiting for transfers between devices, on_device(): lax.psum_scatter(partial_gram, 'cols', scatter_dimension=1, tiled=True)  280 us
    all_gather x1, waiting for transfers between devices, on_device(): row_half = lax.all_gather(block_half, 'cols', axis=1, tiled=True)  150 us
    all_gather x1, waiting for transfers between devices, on_device(): poly_rows = lax.all_gather(poly_block, 'cols', axis=1, tiled=True)  150 us
    all_gather x1, waiting for transfers between devices, on_device(): lax.all_gather(x_local, 'rows', axis=0, tiled=True)  109 us
    all_gather x1, waiting for transfers between devices, on_device(): lax.all_gather(block_half, 'rows', axis=0, tiled=True)  58 us
    dot_general x1, matrix products, on_device(): jnp.dot(left_part, lax.all_gather(x_local, 'rows', axis=0, tiled=True), p...  24.8 us
    dot_general x1, matrix products, on_device(): lax.dot_general(x_local, lax.all_gather(x_local, 'rows', axis=0, tiled=Tr...  23.6 us
  transfers between devices with their start and end apart: 5, of which 5 were waited for; matrix products, arithmetic and copies ran while one was open for 0% of the time, Pallas kernels for 0%

commit v1 on v0

v1 whole, which is shorter than its diff:
```python
import math

import jax
import jax.numpy as jnp
from jax import lax
from jax.sharding import PartitionSpec as P

HEIGHT = 4096
BREADTH = 8192

coef_a = 3.4445
coef_b = -4.775
coef_c = 2.0315

WIDTH = 256
SKEW = 1

NT = (((1,), (1,)), ((), ()))


def solution(mesh):
    rows = mesh.shape["rows"]
    cols = mesh.shape["cols"]

    def swap(value, mask):
        return lax.ppermute(value, "rows", [(i, i ^ mask) for i in range(rows)])

    def shift(value, by):
        pairs = [(i, i + by) for i in range(cols) if 0 <= i + by < cols]
        return lax.ppermute(value, "cols", pairs)

    def after(value, *others):
        return lax.optimization_barrier((value, *others))[0]

    def nt(a, b):
        return lax.dot_general(a, b, NT, preferred_element_type=jnp.float32)

    def dot(a, b):
        return jnp.dot(a, b, preferred_element_type=jnp.float32)

    def choose(index, options):
        out = None
        for k, o in enumerate(options):
            if o is None:
                continue
            out = jnp.where(index == k, o, jnp.zeros_like(o) if out is None else out)
        return out

    def on_device(iterate):
        m, n = iterate.shape
        pieces = max(1, m // WIDTH)
        w = m // pieces
        z = lax.axis_index("cols")
        zz = cols - 1 - z
        x0 = iterate.astype(jnp.bfloat16)

        parts = {}
        for i in range(pieces):
            parts[0, i] = x0[i * w : (i + 1) * w]
            parts[1, i] = swap(parts[0, i], 1)
        order = [(t, i) for t in (0, 1) for i in range(pieces)]
        crossed = []
        for t in range(2, rows, 2):
            for i in range(pieces):
                piece = parts[0, i]
                if len(crossed) >= 2:
                    piece = after(piece, crossed[-2])
                parts[t, i] = swap(piece, t)
                crossed.append(parts[t, i])
                parts[t + 1, i] = swap(parts[t, i], 1)
                order += [(t, i), (t + 1, i)]

        own = [nt(x0, parts[k]).astype(jnp.bfloat16) for k in order]
        count = len(order)

        def at(values, j):
            return values[j] if 0 <= j < len(values) else None

        got_r, got_l = [], []
        whole, rest = {}, {}
        sib, far = {}, {}

        def finish(j):
            total = own[j].astype(jnp.float32)
            for index, got in ((z, got_r), (zz, got_l)):
                came = choose(
                    index,
                    [None] + [at(got, j + SKEW * (k - 1)) for k in range(1, cols)],
                )
                total = total + came.astype(jnp.float32)
            key = order[j]
            whole[key] = total.astype(jnp.bfloat16)
            rest[key] = (total - whole[key].astype(jnp.float32)).astype(jnp.bfloat16)
            sib[key] = swap(whole[key], 1)
            v, i = key
            for t in range(2, rows, 2):
                if (t ^ v) >= 2:
                    piece = whole[key]
                    piece = after(piece, crossed[-2])
                    far[t, v, i] = swap(piece, t)
                    crossed.append(far[t, v, i])
                    far[t + 1, v, i] = swap(far[t, v, i], 1)

        for s in range(count + SKEW * (cols - 2)):
            for index, got, by in ((z, got_r, 1), (zz, got_l, -1)):
                mine = choose(index, [at(own, s - SKEW * k) for k in range(cols - 1)])
                before = at(got, s - SKEW)
                if before is not None:
                    mine = mine.astype(jnp.float32) + before.astype(jnp.float32)
                got.append(shift(mine.astype(jnp.bfloat16), by))
            if s >= SKEW * (cols - 2):
                finish(s - SKEW * (cols - 2))

        def joined(pick):
            return jnp.concatenate([pick(i) for i in range(pieces)], axis=1)

        mine = [joined(lambda i: whole[t, i]) for t in range(rows)]
        beside = [joined(lambda i: sib[t, i]) for t in range(rows)]

        def block(t, u):
            if t == 0:
                return mine[u]
            if t == 1:
                return beside[u ^ 1]
            return joined(lambda i: far[t, t ^ u, i])

        poly = []
        for u in range(rows):
            square = None
            for t in range(rows):
                term = nt(mine[t], block(u, t)) if u < 2 else dot(mine[t], block(t, u))
                square = term if square is None else square + term
            gram = joined(
                lambda i: whole[u, i].astype(jnp.float32)
                + rest[u, i].astype(jnp.float32)
            )
            poly.append((coef_b * gram + coef_c * square).astype(jnp.bfloat16))
        applied = None
        for u in range(rows):
            there = jnp.concatenate([parts[u, i] for i in range(pieces)], axis=0)
            term = dot(poly[u], there)
            applied = term if applied is None else applied + term
        factor = 0.2 * math.sqrt(max(HEIGHT, BREADTH))
        return factor * (coef_a * iterate + applied)

    return jax.shard_map(
        on_device,
        mesh=mesh,
        in_specs=(P(("groups", "rows"), "cols"),),
        out_specs=P(("groups", "rows"), "cols"),
        check_vma=False,
    )
```

time: 834 us -> 530 us (0.64); the launches traced: 834 us -> 520 us
  waiting for transfers between devices: 747 us -> 153 us
  starting transfers between devices: 0.17 us -> 133 us
  matrix products: 63.7 us -> 193 us
  other arithmetic: 9.88 us -> 36.3 us
  between operations: 13.1 us -> 1.72 us
    all_gather x4 -> x0, waiting for transfers between devices: 466 us -> none  [the longest x1 150 us: on_device(): row_half = lax.all_gather(block_half, 'cols', axis=1, tiled=True)]
    reduce_scatter x1 -> x0, waiting for transfers between devices: 280 us -> none  [on_device(): lax.psum_scatter(partial_gram, 'cols', scatter_dimension=1, tiled=True)]
    ppermute x0 -> x80, waiting for transfers between devices: none -> 153 us  [the longest x36 81.6 us: shift(): return lax.ppermute(value, 'cols', pairs)]
    ppermute x0 -> x80, starting transfers between devices: none -> 133 us  [the longest x36 115 us: shift(): return lax.ppermute(value, 'cols', pairs)]
    dot_general x3 -> x32, matrix products: 63.7 us -> 193 us  [the longest x10 117 us: dot(): return jnp.dot(a, b, preferred_element_type=jnp.float32)]
    add x0 -> x8, other arithmetic: none -> 22.8 us  [on_device(): whole[u, i].astype(jnp.float32) + rest[u, i].astype(jnp.float32)]
  transfers between devices with their start and end apart: 5 -> 80, of which waited for: 5 -> 31; matrix products, arithmetic and copies ran while one was open for 0% -> 32% of each run, Pallas kernels for 0% -> 0%
where the time goes in v1:
time: 530 us; the launch traced here: 520 us
  matrix products  193 us (36%)
  waiting for transfers between devices  153 us (29%)
  starting transfers between devices  133 us (25%)
  other arithmetic  36.3 us (7%)
    dot_general x10, matrix products, dot(): return jnp.dot(a, b, preferred_element_type=jnp.float32)  117 us
    ppermute x36, starting transfers between devices, shift(): return lax.ppermute(value, 'cols', pairs)  115 us
    ppermute x36, waiting for transfers between devices, shift(): return lax.ppermute(value, 'cols', pairs)  81.6 us
    dot_general x22, matrix products, nt(): return lax.dot_general(a, b, NT, preferred_element_type=jnp.float32)  75.9 us
    ppermute x44, waiting for transfers between devices, swap(): return lax.ppermute(value, 'rows', [(i, i ^ mask) for i in range(rows)])  71.4 us
    add x8, other arithmetic, on_device(): whole[u, i].astype(jnp.float32) + rest[u, i].astype(jnp.float32)  22.8 us
    ppermute x44, starting transfers between devices, swap(): return lax.ppermute(value, 'rows', [(i, i ^ mask) for i in range(rows)])  17.5 us
  transfers between devices with their start and end apart: 80, of which 31 were waited for; matrix products, arithmetic and copies ran while one was open for 32% of the time, Pallas kernels for 0%

profile of v1, /device:TPU:0, one launch (start us, length us, event | category | flops | bytes accessed | tf_op | source)
XLA Modules:
  0.0 519.6 jit_solution(16668977056691725463)
XLA Ops:
  0.0 6.0 %convert_element_type.748 = bf16[1024,2048]{1,0:T(8,128)(2,1)} convert(f32[1024,2048]{1,0:T(8,128)} %param.1) | non-fusion elementwise | flops 2097152 | bytes 12582912 | tf_op jit(solution)/shard_map/convert_element_type | solution.py:55
  16.7 9.9 %collective-permute-done.3 = bf16[1024,256]{0,1:T(8,128)(2,1)S(1)} collective-permute-done((bf16[1024,256]{0,1:T(8,128)(2,1)S(1)}, bf16[1024,256]{0,1:T(8,128)(2,1)S(1)}, u32[]{:S(2)}, u32[]{:S(2)}) %collective-permute-start.3) | collective-permute-done | bytes 524320 | tf_op jit(solution)/shard_map/ppermute | solution.py:30
  39.3 9.3 %collective-permute-done.4 = bf16[1024,256]{0,1:T(8,128)(2,1)S(1)} collective-permute-done((bf16[1024,256]{0,1:T(8,128)(2,1)}, bf16[1024,256]{0,1:T(8,128)(2,1)S(1)}, u32[]{:S(2)}, u32[]{:S(2)}) %collective-permute-start.4) | collective-permute-done | bytes 524320 | tf_op jit(solution)/shard_map/ppermute | solution.py:30
  62.2 6.3 %collective-permute-done.5 = bf16[1024,256]{0,1:T(8,128)(2,1)S(1)} collective-permute-done((bf16[1024,256]{0,1:T(8,128)(2,1)S(1)}, bf16[1024,256]{0,1:T(8,128)(2,1)S(1)}, u32[]{:S(2)}, u32[]{:S(2)}) %collective-permute-start.5) | collective-permute-done | bytes 524320 | tf_op jit(solution)/shard_map/ppermute | solution.py:30
  77.9 7.1 %collective-permute-done.7 = bf16[1024,256]{0,1:T(8,128)(2,1)S(1)} collective-permute-done((bf16[1024,256]{0,1:T(8,128)(2,1)S(1)}, bf16[1024,256]{0,1:T(8,128)(2,1)S(1)}, u32[]{:S(2)}, u32[]{:S(2)}) %collective-permute-start.7) | collective-permute-done | bytes 524320 | tf_op jit(solution)/shard_map/ppermute | solution.py:30
  94.5 6.2 %collective-permute-done.10 = bf16[1024,256]{0,1:T(8,128)(2,1)S(1)} collective-permute-done((bf16[1024,256]{0,1:T(8,128)(2,1)S(1)}, bf16[1024,256]{0,1:T(8,128)(2,1)S(1)}, u32[]{:S(2)}, u32[]{:S(2)}) %collective-permute-start.10) | collective-permute-done | bytes 524320 | tf_op jit(solution)/shard_map/ppermute | solution.py:30
  126.7 10.0 %collective-permute-done.26 = bf16[256,2048]{1,0:T(8,128)(2,1)} collective-permute-done((bf16[256,2048]{1,0:T(8,128)(2,1)}, bf16[256,2048]{1,0:T(8,128)(2,1)}, u32[]{:S(2)}, u32[]{:S(2)}) %collective-permute-start.26) | collective-permute-done | bytes 1048608 | tf_op jit(solution)/shard_map/ppermute | solution.py:26
  137.1 22.1 %collective-permute-done.20 = bf16[256,2048]{1,0:T(8,128)(2,1)} collective-permute-done((bf16[256,2048]{1,0:T(8,128)(2,1)}, bf16[256,2048]{1,0:T(8,128)(2,1)}, u32[]{:S(2)}, u32[]{:S(2)}) %collective-permute-start.20) | collective-permute-done | bytes 1048608 | tf_op jit(solution)/shard_map/ppermute | solution.py:26
  175.4 25.7 %collective-permute-done.30 = bf16[256,2048]{1,0:T(8,128)(2,1)S(1)} collective-permute-done((bf16[256,2048]{1,0:T(8,128)(2,1)}, bf16[256,2048]{1,0:T(8,128)(2,1)S(1)}, u32[]{:S(2)}, u32[]{:S(2)}) %collective-permute-start.30) | collective-permute-done | bytes 1048608 | tf_op jit(solution)/shard_map/ppermute | solution.py:26
  221.7 6.2 %collective-permute-start.24 = (bf16[1024,256]{0,1:T(8,128)(2,1)S(1)}, bf16[1024,256]{0,1:T(8,128)(2,1)S(1)}, u32[]{:S(2)}, u32[]{:S(2)}) collective-permute-start(bf16[1024,256]{0,1:T(8,128)(2,1)S(1)} %get-tuple-element.120), channel_id=1, source_target_pairs={{0,1},{1,2},{2,3},{4,5},{5,6},{6,7},{8,9},{9,10},{10,11},{12,13},{... | collective-permute-start | bytes 1572872 | tf_op jit(solution)/shard_map/ppermute | solution.py:30
  247.7 6.5 %fusion.179 = f32[1024,1024]{0,1:T(8,128)} fusion(bf16[1024,256]{0,1:T(8,128)(2,1)} %fusion.136, bf16[1024,256]{0,1:T(8,128)(2,1)} %fusion.135, bf16[1024,256]{0,1:T(8,128)(2,1)} %fusion.134, bf16[1024,256]{0,1:T(8,128)(2,1)} %fusion.133), kind=kOutput, calls=%fused_computation.318 | convolution fusion | flops 2155872256 | bytes 6291456 | tf_op jit(solution)/shard_map/dot_general | solution.py:36
  263.7 6.4 %collective-permute-done.68 = bf16[1024,256]{0,1:T(8,128)(2,1)} collective-permute-done((bf16[1024,256]{0,1:T(8,128)(2,1)S(1)}, bf16[1024,256]{0,1:T(8,128)(2,1)}, u32[]{:S(2)}, u32[]{:S(2)}) %collective-permute-start.68) | collective-permute-done | bytes 524320 | tf_op jit(solution)/shard_map/ppermute | solution.py:26
  311.0 6.0 %fusion.39 = f32[1024,1024]{0,1:T(8,128)} fusion(bf16[1024,256]{0,1:T(8,128)(2,1)S(1)} %collective-permute-done.51, bf16[1024,256]{0,1:T(8,128)(2,1)S(1)} %collective-permute-done.50, bf16[1024,256]{0,1:T(8,128)(2,1)S(1)} %collective-permute-done.49, bf16[1024,256]{0,1:T(8,128)(2,1)S(1)} %collective-permute-done.48, bf16[1024,256]{0,1:T(8,128)(2,1)} %fusion.136, ...), kind=kOutput, calls=%fused_computation.42 | convolution fusion | flops 2164260864 | bytes 8388608 | tf_op jit(solution)/shard_map/dot_general | solution.py:36
  333.3 6.5 %collective-permute-done.42 = bf16[1024,256]{0,1:T(8,128)(2,1)S(1)} collective-permute-done((bf16[1024,256]{0,1:T(8,128)(2,1)S(1)}, bf16[1024,256]{0,1:T(8,128)(2,1)S(1)}, u32[]{:S(2)}, u32[]{:S(2)}) %collective-permute-start.42) | collective-permute-done | bytes 524320 | tf_op jit(solution)/shard_map/ppermute | solution.py:30
  369.5 7.1 %collective-permute-done.74 = bf16[1024,256]{0,1:T(8,128)(2,1)} collective-permute-done((bf16[1024,256]{0,1:T(8,128)(2,1)S(1)}, bf16[1024,256]{0,1:T(8,128)(2,1)}, u32[]{:S(2)}, u32[]{:S(2)}) %collective-permute-start.74) | collective-permute-done | bytes 524320 | tf_op jit(solution)/shard_map/ppermute | solution.py:26
  382.1 6.1 %fusion.177 = f32[1024,1024]{0,1:T(8,128)} fusion(bf16[1024,256]{0,1:T(8,128)(2,1)} %fusion.136, bf16[1024,256]{0,1:T(8,128)(2,1)} %fusion.135, bf16[1024,256]{0,1:T(8,128)(2,1)} %fusion.134, bf16[1024,256]{0,1:T(8,128)(2,1)} %fusion.133, bf16[1024,256]{0,1:T(8,128)(2,1)S(1)} %get-tuple-element.89, bf16[1024,256]{0,1:T(8,128)(2,1)S(1)} %get-tuple-element.86, ...), kind=kOutput, calls=%fused_computation.316 | convolution fusion | flops 2164260864 | bytes 8388608 | tf_op jit(solution)/shard_map/dot_general | solution.py:39
  393.3 6.1 %fusion.178 = f32[1024,1024]{0,1:T(8,128)} fusion(bf16[1024,256]{0,1:T(8,128)(2,1)} %fusion.136, bf16[1024,256]{0,1:T(8,128)(2,1)} %fusion.135, bf16[1024,256]{0,1:T(8,128)(2,1)} %fusion.134, bf16[1024,256]{0,1:T(8,128)(2,1)} %fusion.133, bf16[1024,256]{0,1:T(8,128)(2,1)S(1)} %fusion.148, bf16[1024,256]{0,1:T(8,128)(2,1)S(1)} %fusion.147, ...), kind=kOutput, calls=%fused_computation.317 | convolution fusion | flops 2164260864 | bytes 8388608 | tf_op jit(solution)/shard_map/dot_general | solution.py:39
  399.4 19.6 %fusion.37 = f32[1024,2048]{1,0:T(8,128)} fusion(bf16[1024,2048]{1,0:T(8,128)(2,1)} %convert_element_type.748, f32[1024,256]{0,1:T(8,128)} %get-tuple-element.101, f32[1024,256]{0,1:T(8,128)} %get-tuple-element.98, f32[1024,256]{0,1:T(8,128)} %get-tuple-element.95, f32[1024,256]{0,1:T(8,128)} %get-tuple-element.49, f32[1024,1024]{0,1:T(8,128)} %fusion.182, ...), kind=kOutput, calls=%fused_computation.37 | convolution fusion | flops 6461325312 | bytes 31457280 | tf_op jit(solution)/shard_map/dot_general | solution.py:39
  419.1 6.6 %fusion.55 = f32[1024,1024]{0,1:T(8,128)} fusion(bf16[1024,256]{0,1:T(8,128)(2,1)} %copy-done.76, bf16[1024,256]{0,1:T(8,128)(2,1)} %copy-done.74, bf16[1024,256]{0,1:T(8,128)(2,1)} %copy-done.72, bf16[1024,256]{0,1:T(8,128)(2,1)} %copy-done.70, bf16[1024,256]{0,1:T(8,128)(2,1)} %copy-done.47, bf16[1024,256]{0,1:T(8,128)(2,1)} %copy-done.60, ...), kind=kOutput, calls=%fused_computation.58 | convolution fusion | flops 2164260864 | bytes 8388608 | tf_op jit(solution)/shard_map/dot_general | solution.py:39
  425.8 6.0 %fusion.71 = f32[1024,1024]{0,1:T(8,128)} fusion(bf16[1024,256]{0,1:T(8,128)(2,1)} %collective-permute-done.74, bf16[1024,256]{0,1:T(8,128)(2,1)} %collective-permute-done.72, bf16[1024,256]{0,1:T(8,128)(2,1)} %collective-permute-done.70, bf16[1024,256]{0,1:T(8,128)(2,1)} %collective-permute-done.68, bf16[1024,256]{0,1:T(8,128)(2,1)S(1)} %copy-done.48, ...), kind=kOutput, calls=%fused_computation.74 | convolution fusion | flops 2164260864 | bytes 8388608 | tf_op jit(solution)/shard_map/dot_general | solution.py:39
  451.1 18.7 %fusion.14 = f32[1024,2048]{1,0:T(8,128)} fusion(bf16[256,2048]{1,0:T(8,128)(2,1)} %copy-done.68, bf16[256,2048]{1,0:T(8,128)(2,1)} %copy-done.69, bf16[256,2048]{1,0:T(8,128)(2,1)} %collective-permute-done.26, bf16[256,2048]{1,0:T(8,128)(2,1)} %collective-permute-done.20, f32[1024,256]{0,1:T(8,128)} %convert_add_fusion.4, ...), kind=kOutput, calls=%fused_computation.18 | convolution fusion | flops 6478102528 | bytes 33554432 | tf_op jit(solution)/shard_map/dot_general | solution.py:39
  469.8 6.1 %fusion.180 = f32[1024,1024]{0,1:T(8,128)} fusion(bf16[1024,1024]{0,1:T(8,128)(2,1)S(1)} %constant_dynamic-update-slice_fusion.4, bf16[1024,256]{0,1:T(8,128)(2,1)} %copy-done.54, bf16[1024,256]{0,1:T(8,128)(2,1)} %copy-done.56, bf16[1024,256]{0,1:T(8,128)(2,1)} %copy-done.51, bf16[1024,256]{0,1:T(8,128)(2,1)} %copy-done.49), kind=kOutput, calls=%fused_computation.319 | convolution fusion | flops 2155872256 | bytes 8388608 | tf_op jit(solution)/shard_map/dot_general | solution.py:36
  475.9 19.6 %fusion.4 = f32[1024,2048]{1,0:T(8,128)} fusion(bf16[256,2048]{1,0:T(8,128)(2,1)} %collective-permute-done.17, bf16[256,2048]{1,0:T(8,128)(2,1)} %copy-done.67, bf16[256,2048]{1,0:T(8,128)(2,1)} %copy-done.66, bf16[256,2048]{1,0:T(8,128)(2,1)} %copy-done.65, f32[1024,256]{0,1:T(8,128)} %get-tuple-element.80, f32[1024,256]{0,1:T(8,128)} %get-tuple-element.135, ...), kind=kOutput, calls=%fused_computation.7 | convolution fusion | flops 6486491136 | bytes 33554432 | tf_op jit(solution)/shard_map/dot_general | solution.py:39
  495.5 23.9 %add_multiply_fusion = f32[1024,2048]{1,0:T(8,128)} fusion(f32[1024,2048]{1,0:T(8,128)} %fusion.14, f32[1024,2048]{1,0:T(8,128)} %fusion.37, f32[1024,2048]{1,0:T(8,128)} %fusion.4, f32[1024,2048]{1,0:T(8,128)} %param.1, bf16[256,2048]{1,0:T(8,128)(2,1)} %copy-done.25, bf16[256,2048]{1,0:T(8,128)(2,1)} %copy-done.24, bf16[256,2048]{1,0:T(8,128)(2,1)} %copy-done.23, ...), kind=kOutput, calls=%fused_computation | convolution fusion | flops 6490685440 | bytes 67108864 | tf_op jit(solution)/shard_map/dot_general | solution.py:39
  (356 shorter events, 263.7 us)
Async XLA Ops:
  110.2 26.5 %collective-permute-start.26 = (bf16[256,2048]{1,0:T(8,128)(2,1)}, bf16[256,2048]{1,0:T(8,128)(2,1)}, u32[]{:S(2)}, u32[]{:S(2)}) collective-permute-start(bf16[256,2048]{1,0:T(8,128)(2,1)} %get-tuple-element.76), channel_id=1, source_target_pairs={{0,8},{4,12},{8,0},{12,4},{1,9},{5,13},{9,1},{13,5},{2,10},{6,14},... | collective-permute-start | bytes 3145736 | tf_op jit(solution)/shard_map/ppermute | solution.py:26
  110.6 48.5 %collective-permute-start.20 = (bf16[256,2048]{1,0:T(8,128)(2,1)}, bf16[256,2048]{1,0:T(8,128)(2,1)}, u32[]{:S(2)}, u32[]{:S(2)}) collective-permute-start(bf16[256,2048]{1,0:T(8,128)(2,1)} %get-tuple-element.73), channel_id=1, source_target_pairs={{0,8},{4,12},{8,0},{12,4},{1,9},{5,13},{9,1},{13,5},{2,10},{6,14},... | collective-permute-start | bytes 3145736 | tf_op jit(solution)/shard_map/ppermute | solution.py:26
  112.3 47.2 %collective-permute-start.17 = (bf16[256,2048]{1,0:T(8,128)(2,1)}, bf16[256,2048]{1,0:T(8,128)(2,1)}, u32[]{:S(2)}, u32[]{:S(2)}) collective-permute-start(bf16[256,2048]{1,0:T(8,128)(2,1)} %get-tuple-element.16), channel_id=1, source_target_pairs={{0,4},{4,0},{8,12},{12,8},{1,5},{5,1},{9,13},{13,9},{2,6},{6,2},{1... | collective-permute-start | bytes 3145736 | tf_op jit(solution)/shard_map/ppermute | solution.py:26
  119.6 40.0 %collective-permute-start.16 = (bf16[1024,256]{0,1:T(8,128)(2,1)}, bf16[1024,256]{0,1:T(8,128)(2,1)S(1)}, u32[]{:S(2)}, u32[]{:S(2)}) collective-permute-start(bf16[1024,256]{0,1:T(8,128)(2,1)} %get-tuple-element.125), channel_id=1, source_target_pairs={{1,0},{2,1},{3,2},{5,4},{6,5},{7,6},{9,8},{10,9},{11,10},{13,12},{... | collective-permute-start | bytes 1572872 | tf_op jit(solution)/shard_map/ppermute | solution.py:30
  120.9 38.7 %collective-permute-start.15 = (bf16[1024,256]{0,1:T(8,128)(2,1)}, bf16[1024,256]{0,1:T(8,128)(2,1)}, u32[]{:S(2)}, u32[]{:S(2)}) collective-permute-start(bf16[1024,256]{0,1:T(8,128)(2,1)} %get-tuple-element.126), channel_id=1, source_target_pairs={{0,1},{1,2},{2,3},{4,5},{5,6},{6,7},{8,9},{9,10},{10,11},{12,13},{... | collective-permute-start | bytes 1572872 | tf_op jit(solution)/shard_map/ppermute | solution.py:30
  136.7 75.3 %collective-permute-start.36 = (bf16[256,2048]{1,0:T(8,128)(2,1)}, bf16[256,2048]{1,0:T(8,128)(2,1)S(1)}, u32[]{:S(2)}, u32[]{:S(2)}) collective-permute-start(bf16[256,2048]{1,0:T(8,128)(2,1)} %get-tuple-element.16), channel_id=1, source_target_pairs={{0,8},{4,12},{8,0},{12,4},{1,9},{5,13},{9,1},{13,5},{2,10},{6,14},... | collective-permute-start | bytes 3145736 | tf_op jit(solution)/shard_map/ppermute | solution.py:26
  159.2 41.9 %collective-permute-start.30 = (bf16[256,2048]{1,0:T(8,128)(2,1)}, bf16[256,2048]{1,0:T(8,128)(2,1)S(1)}, u32[]{:S(2)}, u32[]{:S(2)}) collective-permute-start(bf16[256,2048]{1,0:T(8,128)(2,1)} %copy-done.26), channel_id=1, source_target_pairs={{0,8},{4,12},{8,0},{12,4},{1,9},{5,13},{9,1},{13,5},{2,10},{6,14},... | collective-permute-start | bytes 3145736 | tf_op jit(solution)/shard_map/ppermute | solution.py:26
  159.5 54.1 %collective-permute-start.23 = (bf16[256,2048]{1,0:T(8,128)(2,1)}, bf16[256,2048]{1,0:T(8,128)(2,1)S(1)}, u32[]{:S(2)}, u32[]{:S(2)}) collective-permute-start(bf16[256,2048]{1,0:T(8,128)(2,1)} %collective-permute-done.20), channel_id=1, source_target_pairs={{0,4},{4,0},{8,12},{12,8},{1,5},{5,1},{9,13},{13,9},{2,6},{6,2},{1... | collective-permute-start | bytes 3145736 | tf_op jit(solution)/shard_map/ppermute | solution.py:26
  164.3 37.0 %collective-permute-start.19 = (bf16[1024,256]{0,1:T(8,128)(2,1)S(1)}, bf16[1024,256]{0,1:T(8,128)(2,1)S(1)}, u32[]{:S(2)}, u32[]{:S(2)}) collective-permute-start(bf16[1024,256]{0,1:T(8,128)(2,1)S(1)} %get-tuple-element.123), channel_id=1, source_target_pairs={{1,0},{2,1},{3,2},{5,4},{6,5},{7,6},{9,8},{10,9},{11,10},{13,12},{... | collective-permute-start | bytes 1572872 | tf_op jit(solution)/shard_map/ppermute | solution.py:30
  165.7 35.7 %collective-permute-start.18 = (bf16[1024,256]{0,1:T(8,128)(2,1)S(1)}, bf16[1024,256]{0,1:T(8,128)(2,1)S(1)}, u32[]{:S(2)}, u32[]{:S(2)}) collective-permute-start(bf16[1024,256]{0,1:T(8,128)(2,1)S(1)} %get-tuple-element.124), channel_id=1, source_target_pairs={{0,1},{1,2},{2,3},{4,5},{5,6},{6,7},{8,9},{9,10},{10,11},{12,13},{... | collective-permute-start | bytes 1572872 | tf_op jit(solution)/shard_map/ppermute | solution.py:30
  212.1 42.2 %collective-permute-start.29 = (bf16[256,2048]{1,0:T(8,128)(2,1)}, bf16[256,2048]{1,0:T(8,128)(2,1)S(1)}, u32[]{:S(2)}, u32[]{:S(2)}) collective-permute-start(bf16[256,2048]{1,0:T(8,128)(2,1)} %collective-permute-done.26), channel_id=1, source_target_pairs={{0,4},{4,0},{8,12},{12,8},{1,5},{5,1},{9,13},{13,9},{2,6},{6,2},{1... | collective-permute-start | bytes 3145736 | tf_op jit(solution)/shard_map/ppermute | solution.py:26
  213.3 69.6 %collective-permute-start.35 = (bf16[256,2048]{1,0:T(8,128)(2,1)S(1)}, bf16[256,2048]{1,0:T(8,128)(2,1)S(1)}, u32[]{:S(2)}, u32[]{:S(2)}) collective-permute-start(bf16[256,2048]{1,0:T(8,128)(2,1)S(1)} %collective-permute-done.30), channel_id=1, source_target_pairs={{0,4},{4,0},{8,12},{12,8},{1,5},{5,1},{9,13},{13,9},{2,6},{6,2},{1... | collective-permute-start | bytes 3145736 | tf_op jit(solution)/shard_map/ppermute | solution.py:26
  263.3 53.7 %collective-permute-start.41 = (bf16[256,2048]{1,0:T(8,128)(2,1)S(1)}, bf16[256,2048]{1,0:T(8,128)(2,1)S(1)}, u32[]{:S(2)}, u32[]{:S(2)}) collective-permute-start(bf16[256,2048]{1,0:T(8,128)(2,1)S(1)} %collective-permute-done.36), channel_id=1, source_target_pairs={{0,4},{4,0},{8,12},{12,8},{1,5},{5,1},{9,13},{13,9},{2,6},{6,2},{1... | collective-permute-start | bytes 3145736 | tf_op jit(solution)/shard_map/ppermute | solution.py:26
  281.5 22.5 %collective-permute-start.49 = (bf16[1024,256]{0,1:T(8,128)(2,1)S(1)}, bf16[1024,256]{0,1:T(8,128)(2,1)S(1)}, u32[]{:S(2)}, u32[]{:S(2)}) collective-permute-start(bf16[1024,256]{0,1:T(8,128)(2,1)S(1)} %fusion.138), channel_id=1, source_target_pairs={{0,4},{4,0},{8,12},{12,8},{1,5},{5,1},{9,13},{13,9},{2,6},{6,2},{1... | collective-permute-start | bytes 1572872 | tf_op jit(solution)/shard_map/ppermute | solution.py:26
  304.0 46.7 %collective-permute-start.56 = (bf16[1024,256]{0,1:T(8,128)(2,1)S(1)}, bf16[1024,256]{0,1:T(8,128)(2,1)S(1)}, u32[]{:S(2)}, u32[]{:S(2)}) collective-permute-start(bf16[1024,256]{0,1:T(8,128)(2,1)S(1)} %fusion.143), channel_id=1, source_target_pairs={{0,4},{4,0},{8,12},{12,8},{1,5},{5,1},{9,13},{13,9},{2,6},{6,2},{1... | collective-permute-start | bytes 1572872 | tf_op jit(solution)/shard_map/ppermute | solution.py:26
  304.6 46.7 %collective-permute-start.60 = (bf16[1024,256]{0,1:T(8,128)(2,1)S(1)}, bf16[1024,256]{0,1:T(8,128)(2,1)S(1)}, u32[]{:S(2)}, u32[]{:S(2)}) collective-permute-start(bf16[1024,256]{0,1:T(8,128)(2,1)S(1)} %get-tuple-element.77), channel_id=1, source_target_pairs={{0,4},{4,0},{8,12},{12,8},{1,5},{5,1},{9,13},{13,9},{2,6},{6,2},{1... | collective-permute-start | bytes 1572872 | tf_op jit(solution)/shard_map/ppermute | solution.py:26
  368.8 107.1 %collective-permute-start.54 = (bf16[1024,256]{0,1:T(8,128)(2,1)}, bf16[1024,256]{0,1:T(8,128)(2,1)}, u32[]{:S(2)}, u32[]{:S(2)}) collective-permute-start(bf16[1024,256]{0,1:T(8,128)(2,1)} %fusion.135), channel_id=1, source_target_pairs={{0,4},{4,0},{8,12},{12,8},{1,5},{5,1},{9,13},{13,9},{2,6},{6,2},{1... | collective-permute-start | bytes 1572872 | tf_op jit(solution)/shard_map/ppermute | solution.py:26
  369.1 62.7 %collective-permute-start.69 = (bf16[1024,256]{0,1:T(8,128)(2,1)}, bf16[1024,256]{0,1:T(8,128)(2,1)}, u32[]{:S(2)}, u32[]{:S(2)}) collective-permute-start(bf16[1024,256]{0,1:T(8,128)(2,1)} %collective-permute-done.68), channel_id=1, source_target_pairs={{0,4},{4,0},{8,12},{12,8},{1,5},{5,1},{9,13},{13,9},{2,6},{6,2},{1... | collective-permute-start | bytes 1572872 | tf_op jit(solution)/shard_map/ppermute | solution.py:26
  376.6 55.8 %collective-permute-start.71 = (bf16[1024,256]{0,1:T(8,128)(2,1)}, bf16[1024,256]{0,1:T(8,128)(2,1)}, u32[]{:S(2)}, u32[]{:S(2)}) collective-permute-start(bf16[1024,256]{0,1:T(8,128)(2,1)} %collective-permute-done.70), channel_id=1, source_target_pairs={{0,4},{4,0},{8,12},{12,8},{1,5},{5,1},{9,13},{13,9},{2,6},{6,2},{1... | collective-permute-start | bytes 1572872 | tf_op jit(solution)/shard_map/ppermute | solution.py:26
  377.2 55.2 %collective-permute-start.73 = (bf16[1024,256]{0,1:T(8,128)(2,1)}, bf16[1024,256]{0,1:T(8,128)(2,1)}, u32[]{:S(2)}, u32[]{:S(2)}) collective-permute-start(bf16[1024,256]{0,1:T(8,128)(2,1)} %collective-permute-done.72), channel_id=1, source_target_pairs={{0,4},{4,0},{8,12},{12,8},{1,5},{5,1},{9,13},{13,9},{2,6},{6,2},{1... | collective-permute-start | bytes 1572872 | tf_op jit(solution)/shard_map/ppermute | solution.py:26
  378.3 54.5 %collective-permute-start.75 = (bf16[1024,256]{0,1:T(8,128)(2,1)}, bf16[1024,256]{0,1:T(8,128)(2,1)}, u32[]{:S(2)}, u32[]{:S(2)}) collective-permute-start(bf16[1024,256]{0,1:T(8,128)(2,1)} %collective-permute-done.74), channel_id=1, source_target_pairs={{0,4},{4,0},{8,12},{12,8},{1,5},{5,1},{9,13},{13,9},{2,6},{6,2},{1... | collective-permute-start | bytes 1572872 | tf_op jit(solution)/shard_map/ppermute | solution.py:26
  438.8 37.0 %collective-permute-start.53 = (bf16[1024,256]{0,1:T(8,128)(2,1)}, bf16[1024,256]{0,1:T(8,128)(2,1)}, u32[]{:S(2)}, u32[]{:S(2)}) collective-permute-start(bf16[1024,256]{0,1:T(8,128)(2,1)} %fusion.134), channel_id=1, source_target_pairs={{0,4},{4,0},{8,12},{12,8},{1,5},{5,1},{9,13},{13,9},{2,6},{6,2},{1... | collective-permute-start | bytes 1572872 | tf_op jit(solution)/shard_map/ppermute | solution.py:26
  439.3 36.5 %collective-permute-start.52 = (bf16[1024,256]{0,1:T(8,128)(2,1)}, bf16[1024,256]{0,1:T(8,128)(2,1)}, u32[]{:S(2)}, u32[]{:S(2)}) collective-permute-start(bf16[1024,256]{0,1:T(8,128)(2,1)} %fusion.133), channel_id=1, source_target_pairs={{0,4},{4,0},{8,12},{12,8},{1,5},{5,1},{9,13},{13,9},{2,6},{6,2},{1... | collective-permute-start | bytes 1572872 | tf_op jit(solution)/shard_map/ppermute | solution.py:26
  445.9 29.9 %collective-permute-start.55 = (bf16[1024,256]{0,1:T(8,128)(2,1)}, bf16[1024,256]{0,1:T(8,128)(2,1)}, u32[]{:S(2)}, u32[]{:S(2)}) collective-permute-start(bf16[1024,256]{0,1:T(8,128)(2,1)} %fusion.136), channel_id=1, source_target_pairs={{0,4},{4,0},{8,12},{12,8},{1,5},{5,1},{9,13},{13,9},{2,6},{6,2},{1... | collective-permute-start | bytes 1572872 | tf_op jit(solution)/shard_map/ppermute | solution.py:26
  (134 other events, 2428.3 us)

commit v2 on v0

v2 whole, which is shorter than its diff:
```python
import functools
import math

import jax
import jax.numpy as jnp
from jax import lax
from jax.experimental import pallas as pl
from jax.experimental.pallas import tpu as pltpu
from jax.sharding import PartitionSpec as P

HEIGHT = 4096
BREADTH = 8192

coef_a = 3.4445
coef_b = -4.775
coef_c = 2.0315

PIECES = 2
WIDTH = 256
SKEW = 2
TILE = 256
STRIPE = 512

NN = (((1,), (0,)), ((), ()))
NT = (((1,), (1,)), ((), ()))


def dots_body(flips, scales, out_scale, height, *refs):
    count = len(flips)
    pairs, adds, out = refs[: 2 * count], refs[2 * count : -1], refs[-1]
    for start in range(0, out.shape[0], height):
        here = pl.ds(start, height)
        total = None
        for k in range(count):
            term = lax.dot_general(
                pairs[2 * k][here, :],
                pairs[2 * k + 1][...],
                NT if flips[k] else NN,
                preferred_element_type=jnp.float32,
            )
            total = term if total is None else total + term
        if scales[0] != 1.0:
            total = scales[0] * total
        for scale, add in zip(scales[1:], adds):
            value = add[here, :].astype(jnp.float32)
            total = total + (value if scale == 1.0 else scale * value)
        if out_scale != 1.0:
            total = out_scale * total
        out[here, :] = total.astype(out.dtype)


def dots(pairs, width, tile, dot_scale, adds, out_dtype, out_scale=1.0):
    m = pairs[0][0].shape[0]
    operands, specs, flips = [], [], []
    flops = 0
    for left, column, depth, right, where in pairs:
        operands += [left, right]
        specs.append(
            pl.BlockSpec(
                (m, depth),
                functools.partial(lambda c, j: (0, c), column),
                pipeline_mode=pl.Buffered(1),
            )
        )
        flip = callable(where)
        if flip:
            specs.append(
                pl.BlockSpec(
                    (tile, depth), functools.partial(lambda f, j: (f(j), 0), where)
                )
            )
        else:
            specs.append(
                pl.BlockSpec(
                    (depth, tile), functools.partial(lambda b, j: (b, j), where)
                )
            )
        flips.append(flip)
        flops += 2 * m * depth * width
    for _, add in adds:
        operands.append(add)
        specs.append(pl.BlockSpec((m, tile), lambda j: (0, j)))
    moved = sum(o.size * o.dtype.itemsize for o in operands)
    return pl.pallas_call(
        functools.partial(
            dots_body,
            tuple(flips),
            (dot_scale,) + tuple(s for s, _ in adds),
            out_scale,
            min(STRIPE, m),
        ),
        out_shape=jax.ShapeDtypeStruct((m, width), out_dtype),
        grid=(width // tile,),
        in_specs=specs,
        out_specs=pl.BlockSpec((m, tile), lambda j: (0, j)),
        compiler_params=pltpu.CompilerParams(vmem_limit_bytes=36 * 1024 * 1024),
        cost_estimate=pl.CostEstimate(
            flops=flops, bytes_accessed=moved, transcendentals=0
        ),
    )(*operands)


def gate_body(*refs):
    pass


def gate(values):
    anywhere = pl.BlockSpec(memory_space=pl.ANY)
    return list(
        pl.pallas_call(
            gate_body,
            out_shape=[jax.ShapeDtypeStruct(v.shape, v.dtype) for v in values],
            in_specs=[anywhere] * len(values),
            out_specs=[anywhere] * len(values),
            input_output_aliases={k: k for k in range(len(values))},
            cost_estimate=pl.CostEstimate(flops=0, bytes_accessed=0, transcendentals=0),
        )(*values)
    )


def solution(mesh):
    rows = mesh.shape["rows"]
    cols = mesh.shape["cols"]
    chips = rows // 2

    def swap(value, mask):
        return lax.ppermute(value, "rows", [(i, i ^ mask) for i in range(rows)])

    def side(value):
        pairs = [[2 * i, 2 * i + 1] for i in range(chips)]
        return lax.all_gather(
            value, "rows", axis=0, tiled=True, axis_index_groups=pairs
        )

    def trade(value, start):
        pairs = []
        for i in range(start, cols - 1, 2):
            pairs += [(i, i + 1), (i + 1, i)]
        return lax.ppermute(value, "cols", pairs)

    def choose(index, options):
        out = None
        for k, o in options:
            out = o if out is None else jnp.where(index == k, o, out)
        return out

    def wide(value):
        return value.astype(jnp.float32)

    def on_device(iterate):
        m, n = iterate.shape
        mp = m // PIECES
        w = min(WIDTH, 2 * mp)
        q = 2 * mp // w
        tile = min(TILE, mp)
        z = lax.axis_index("cols")
        even = jnp.where(z % 2 == 0, z, cols - 1 - z)
        odd = cols - 1 - even
        x0 = iterate.astype(jnp.bfloat16)
        zero = jnp.zeros((m, w), jnp.bfloat16)

        groups = [(d, p) for d in range(chips) for p in range(PIECES)]
        order = [(g, i) for g in groups for i in range(q)]
        count = len(order)
        lag = SKEW * (cols - 2)
        steps = count + lag
        ready = {
            g: order.index((g, q - 1)) + lag + SKEW for g in groups
        }

        held = {}
        passing = {s: [] for s in range(steps + 1)}
        follow = {s: [] for s in range(steps + 1)}

        def hold(key, value, s):
            held[key] = value
            if 0 <= s < steps:
                passing[s].append(key)

        def then(s, action):
            if 0 <= s < steps:
                follow[s].append(action)
            else:
                late.append(action)

        late = []
        blocks = {}

        def cross(key):
            d, p = key
            held["x", key] = swap(held.pop(("x0", key)), 2 * d)

        def settle(key):
            blocks[key] = side(held.pop(("x", key)))

        for g in groups:
            d, p = g
            piece = x0[p * mp : (p + 1) * mp]
            if d == 0:
                blocks[g] = side(piece)
                continue
            i = (d - 1) * PIECES + p
            begin, end = i * q - 1, (i + 1) * q
            hold(("x0", g), piece, begin)
            if begin < 0:
                cross(g)
            else:
                then(begin, functools.partial(cross, g))
            passing[end].append(("x", g))
            then(end, functools.partial(settle, g))

        own, got_e, got_o, chunks = [], {}, {}, {}
        strip, chip, far = {}, {}, {}

        def at(values, j):
            if isinstance(values, dict):
                return values.get(j, zero)
            return values[j] if 0 <= j < len(values) else zero

        def finish(j):
            came_e = choose(
                even,
                [
                    (k, at(got_e, j + SKEW * (cols - 2 - k)))
                    for k in range(0, cols - 1, 2)
                ],
            )
            came_o = choose(
                even,
                [(0, zero)]
                + [(k, at(got_o, j + SKEW * (k - 1))) for k in range(2, cols - 1, 2)],
            )
            chunks[order[j]] = (wide(own[j]) + wide(came_e) + wide(came_o)).astype(
                jnp.bfloat16
            )

        def launch(g, s):
            d0, p = g
            strip[g] = held.pop(("s", g))
            chip[g] = side(strip[g])
            for d in range(1, chips):
                e = d ^ d0
                if e == 0:
                    continue
                over = swap(strip[g], 2 * d)
                if s + q < steps:
                    hold(("f", d, e, p), over, s + q)
                    then(s + q, functools.partial(land, d, e, p))
                else:
                    far[d, e, p] = side(over)

        def land(d, e, p):
            far[d, e, p] = side(held.pop(("f", d, e, p)))

        def complete(g, s):
            held["s", g] = jnp.concatenate([chunks[g, i] for i in range(q)], axis=1)
            if s < steps:
                passing[s].append(("s", g))
                follow[s].append(functools.partial(launch, g, s))
            else:
                launch(g, s)

        poly, others = {}, {}

        def turned(p):
            per = mp // tile
            return lambda j: (j // per * PIECES + p) * per + j % per

        def poly_first(p):
            poly[p] = dots(
                [
                    (strip[0, r], 0, 2 * mp, chip[0, r], turned(p))
                    for r in range(PIECES)
                ],
                2 * mp,
                tile,
                coef_c,
                [(coef_b, strip[0, p])],
                jnp.float32,
            )

        def poly_next(r, p):
            poly[p] = dots(
                [
                    (strip[d, r], 0, 2 * mp, chip[d, r], turned(p))
                    for d in range(1, chips)
                ],
                2 * mp,
                tile,
                coef_c,
                [(1.0, poly[p])],
                jnp.bfloat16 if r == PIECES - 1 else jnp.float32,
            )

        def others_next(r, e, p):
            pairs = [
                (strip[d, r], c, mp, far[d, e, p], c * PIECES + r)
                for d in range(1, chips)
                for c in range(2)
            ]
            adds = [] if r == 0 else [(1.0, others[e, p])]
            if r == p:
                pairs += [
                    (strip[0, t], c, mp, chip[e, p], c * PIECES + t)
                    for t in range(PIECES)
                    for c in range(2)
                ]
                adds += [(coef_b, strip[e, p])]
            others[e, p] = dots(
                pairs,
                2 * mp,
                tile,
                coef_c,
                adds,
                jnp.bfloat16 if r == PIECES - 1 else jnp.float32,
            )

        def early(p, s):
            poly_first(p)
            if s + 1 < steps:
                held["poly", p] = poly[p]
                passing[s + 1].append(("poly", p))
                follow[s + 1].insert(0, functools.partial(regain, p))

        def regain(p):
            poly[p] = held.pop(("poly", p))

        first_at = ready[0, PIECES - 1] + 2
        for p in range(PIECES):
            then(first_at + p, functools.partial(early, p, first_at + p))

        token = jnp.zeros((8, 128), jnp.float32)
        for s in range(steps):
            if s < count:
                g, i = order[s]
                own.append(
                    lax.dot_general(
                        x0,
                        blocks[g][i * w : (i + 1) * w],
                        NT,
                        preferred_element_type=jnp.float32,
                    ).astype(jnp.bfloat16)
                )
            for g in groups:
                if ready[g] == s:
                    for i in range(q):
                        finish(order.index((g, i)))
                    complete(g, s)
            last_e, last_o = at(got_e, s - SKEW), at(got_o, s - SKEW)
            mine_e = choose(
                even, [(k, at(own, s - SKEW * k)) for k in range(0, cols - 1, 2)]
            )
            carry = jnp.where(even == 0, zero, last_o)
            sends = [(wide(mine_e) + wide(carry)).astype(jnp.bfloat16)]
            if SKEW <= s < count + SKEW * (cols - 3):
                mine_o = choose(
                    odd, [(k, at(own, s - SKEW * k)) for k in range(1, cols - 1, 2)]
                )
                sends.append((wide(mine_o) + wide(last_e)).astype(jnp.bfloat16))
            keys = passing[s]
            out = gate(sends + [held[k] for k in keys] + [token])
            token = out[-1]
            got_e[s] = trade(out[0], 0)
            if len(sends) > 1:
                got_o[s] = trade(out[1], 1)
            for k, v in zip(keys, out[len(sends) : -1]):
                held[k] = v
            for action in follow[s]:
                action()
        for action in late:
            action()

        for r in range(PIECES):
            wanted = [(d, r) for d in range(chips)] if chips == 2 else groups
            for g in wanted:
                if g not in strip:
                    for i in range(q):
                        finish(order.index((g, i)))
                    complete(g, steps)
            for e in range(1, chips):
                for p in range(PIECES):
                    if p != r:
                        others_next(r, e, p)
            for p in range(PIECES):
                poly_next(r, p)
            for e in range(1, chips):
                others_next(r, e, r)
            if r < PIECES - 1 and chips == 2:
                keys = [("p", p) for p in range(PIECES)]
                keys += [(e, p) for e in range(1, chips) for p in range(PIECES)]
                values = [poly[p] if e == "p" else others[e, p] for e, p in keys]
                out = gate(values + [got_e[steps - 1], token])
                got_e[steps - 1], token = out[-2:]
                for (e, p), v in zip(keys, out):
                    if e == "p":
                        poly[p] = v
                    else:
                        others[e, p] = v

        factor = 0.2 * math.sqrt(max(HEIGHT, BREADTH))
        return dots(
            [
                (poly[p] if e == 0 else others[e, p], 0, 2 * mp, blocks[e, p], 0)
                for e in range(chips)
                for p in range(PIECES)
            ],
            n,
            tile,
            1.0,
            [(coef_a, iterate)],
            jnp.float32,
            factor,
        )

    return jax.shard_map(
        on_device,
        mesh=mesh,
        in_specs=(P(("groups", "rows"), "cols"),),
        out_specs=P(("groups", "rows"), "cols"),
        check_vma=False,
    )
```

time: 834 us -> 476 us (0.57); the launches traced: 834 us -> 466 us
  waiting for transfers between devices: 747 us -> 65.1 us
  starting transfers between devices: 0.17 us -> 105 us
  Pallas kernels: 0 us -> 75.5 us
  local copies, waits for them, and re-layouts: 0 us -> 68.9 us
  other arithmetic: 9.88 us -> 58 us
  matrix products: 63.7 us -> 79.4 us
    all_gather x4 -> x10, waiting for transfers between devices: 466 us -> 15.2 us  [side(): lax.all_gather(value, 'rows', axis=0, tiled=True, axis_index_groups=pairs)]
    reduce_scatter x1 -> x0, waiting for transfers between devices: 280 us -> none  [on_device(): lax.psum_scatter(partial_gram, 'cols', scatter_dimension=1, tiled=True)]
    ppermute x0 -> x40, starting transfers between devices: none -> 104 us  [the longest x36 96.8 us: trade(): return lax.ppermute(value, 'cols', pairs)]
    pallas_call x0 -> x32, Pallas kernels: none -> 75.5 us  [the longest x11 75.5 us: dots(): pl.pallas_call(functools.partial(dots_body, tuple(flips), (dot_scale,) +...]
    unnamed x0 -> x188, local copies, waits for them, and re-layouts: none -> 65.6 us
    ppermute x0 -> x40, waiting for transfers between devices: none -> 47.8 us  [the longest x36 47.7 us: trade(): return lax.ppermute(value, 'cols', pairs)]
    convert_element_type x2 -> x25, other arithmetic: 9.88 us -> 49.9 us  [the longest x12 28.4 us: finish(): (wide(own[j]) + wide(came_e) + wide(came_o)).astype(jnp.bfloat16)]
    dot_general x3 -> x16, matrix products: 63.7 us -> 79.4 us  [on_device(): lax.dot_general(x0, blocks[g][i * w:(i + 1) * w], NT, preferred_element_t...]
  transfers between devices with their start and end apart: 5 -> 50, of which waited for: 5 -> 13; matrix products, arithmetic and copies ran while one was open for 0% -> 28% of each run, Pallas kernels for 0% -> 8%
where the time goes in v2:
time: 476 us; the launch traced here: 466 us
  starting transfers between devices  105 us (22%)
  matrix products  79.4 us (17%)
  Pallas kernels  75.5 us (16%)
  local copies, waits for them, and re-layouts  68.9 us (14%)
  waiting for transfers between devices  65.1 us (14%)
  other arithmetic  58 us (12%)
  between operations  14.7 us (3%)
    ppermute x36, starting transfers between devices, trade(): return lax.ppermute(value, 'cols', pairs)  96.8 us
    dot_general x16, matrix products, on_device(): lax.dot_general(x0, blocks[g][i * w:(i + 1) * w], NT, preferred_element_t...  79.4 us
    pallas_call x11, Pallas kernels, dots(): pl.pallas_call(functools.partial(dots_body, tuple(flips), (dot_scale,) +...  75.5 us
    unnamed x188, local copies, waits for them, and re-layouts  65.6 us
    ppermute x36, waiting for transfers between devices, trade(): return lax.ppermute(value, 'cols', pairs)  47.7 us
    convert_element_type x12, other arithmetic, finish(): (wide(own[j]) + wide(came_e) + wide(came_o)).astype(jnp.bfloat16)  28.4 us
    all_gather x10, waiting for transfers between devices, side(): lax.all_gather(value, 'rows', axis=0, tiled=True, axis_index_groups=pairs)  15.2 us
    convert_element_type x8, other arithmetic, on_device(): sends.append((wide(mine_o) + wide(last_e)).astype(jnp.bfloat16))  13.5 us
  transfers between devices with their start and end apart: 50, of which 13 were waited for; matrix products, arithmetic and copies ran while one was open for 28% of the time, Pallas kernels for 8%

profile of v2, /device:TPU:0, one launch (start us, length us, event | category | flops | bytes accessed | tf_op | source)
XLA Modules:
  0.0 466.2 jit_solution(15235439444533625274)
XLA Ops:
  17.9 12.7 %all-gather.13.cloned.1.call-done.refs_1_ = bf16[1024,2048]{1,0:T(8,128)(2,1)} async-done(((bf16[512,2048]{1,0:T(8,128)(2,1)}), bf16[1024,2048]{1,0:T(8,128)(2,1)}) %all-gather.13.cloned.1.call-update) | async-done | bytes 4194320 | tf_op jit(solution)/shard_map/all_gather | solution.py:131
  37.5 5.0 %broadcast_select_fusion.1 = (bf16[1024,256]{1,0:T(8,128)(2,1)}, bf16[1024,256]{1,0:T(8,128)(2,1)S(1)}) fusion(pred[]{:T(512)S(6)} %eq.9, bf16[1024,2048]{1,0:T(8,128)(2,1)} %copy-done.38, bf16[1024,2048]{1,0:T(8,128)(2,1)} %all-gather.13.cloned.1.call-done.refs_1_), kind=kOutput, calls=%fused_computation.141 | convolution fusion | flops 1074266112 | bytes 6291457 | tf_op jit(solution)/shard_map/dot_general | solution.py:337
  42.5 5.4 %broadcast_select_fusion.3 = (bf16[1024,256]{1,0:T(8,128)(2,1)}, bf16[1024,256]{1,0:T(8,128)(2,1)S(1)}) fusion(pred[]{:T(512)S(6)} %eq.9, bf16[1024,2048]{1,0:T(8,128)(2,1)} %copy-done.38, bf16[1024,2048]{1,0:T(8,128)(2,1)} %all-gather.13.cloned.1.call-done.refs_1_), kind=kOutput, calls=%fused_computation.143 | convolution fusion | flops 1074266112 | bytes 6291457 | tf_op jit(solution)/shard_map/dot_general | solution.py:337
  53.5 4.8 %broadcast_select_fusion = (bf16[1024,256]{1,0:T(8,128)(2,1)}, bf16[1024,256]{1,0:T(8,128)(2,1)}) fusion(pred[]{:T(512)S(6)} %eq.9, bf16[1024,2048]{1,0:T(8,128)(2,1)} %copy-done.38, bf16[1024,2048]{1,0:T(8,128)(2,1)} %all-gather.13.cloned.1.call-done.refs_1_), kind=kOutput, calls=%fused_computation.140 | convolution fusion | flops 1074266112 | bytes 6291457 | tf_op jit(solution)/shard_map/dot_general | solution.py:337
  63.0 9.7 %collective-permute-done.2 = bf16[1024,256]{1,0:T(8,128)(2,1)} collective-permute-done((bf16[1024,256]{1,0:T(8,128)(2,1)}, bf16[1024,256]{1,0:T(8,128)(2,1)}, u32[]{:S(2)}, u32[]{:S(2)}) %collective-permute-start.2) | collective-permute-done | bytes 524320 | tf_op jit(solution)/shard_map/ppermute | solution.py:139
  89.6 5.7 %add_convert_fusion.13 = (bf16[1024,256]{1,0:T(8,128)(2,1)}, bf16[1024,256]{1,0:T(8,128)(2,1)}) fusion(bf16[1024,256]{1,0:T(8,128)(2,1)S(1)} %collective-permute-done.7, bf16[1024,256]{1,0:T(8,128)(2,1)} %copy-done.57, pred[]{:T(512)S(6)} %eq.10, pred[]{:T(512)S(6)} %eq.9, bf16[1024,2048]{1,0:T(8,128)(2,1)} %copy-done.38, ...), kind=kOutput, calls=%fused_computation.137 | convolution fusion | flops 1075576832 | bytes 7340034 | tf_op jit(solution)/shard_map/dot_general | solution.py:337
  101.0 7.5 %collective-permute-start.13 = (bf16[1024,256]{1,0:T(8,128)(2,1)}, bf16[1024,256]{1,0:T(8,128)(2,1)}, u32[]{:S(2)}, u32[]{:S(2)}) collective-permute-start(bf16[1024,256]{1,0:T(8,128)(2,1)} %get-tuple-element.95), channel_id=1, source_target_pairs={{0,1},{1,0},{2,3},{3,2},{4,5},{5,4},{6,7},{7,6},{8,9},{9,8},{10,11... | collective-permute-start | bytes 1572872 | tf_op jit(solution)/shard_map/ppermute | solution.py:139
  121.0 4.8 %add_convert_fusion.11 = (bf16[1024,256]{1,0:T(8,128)(2,1)}, bf16[1024,256]{1,0:T(8,128)(2,1)}) fusion(bf16[1024,256]{1,0:T(8,128)(2,1)} %collective-permute-done.12, bf16[1024,256]{1,0:T(8,128)(2,1)} %get-tuple-element.181, pred[]{:T(512)S(6)} %eq.10, pred[]{:T(512)S(6)} %eq.9, bf16[1024,2048]{1,0:T(8,128)(2,1)} %copy-done.38, ...), kind=kOutput, calls=%fused_computation.135 | convolution fusion | flops 1075576832 | bytes 7340034 | tf_op jit(solution)/shard_map/dot_general | solution.py:337
  144.2 9.5 %collective-permute-done.17 = bf16[1024,256]{1,0:T(8,128)(2,1)S(1)} collective-permute-done((bf16[1024,256]{1,0:T(8,128)(2,1)}, bf16[1024,256]{1,0:T(8,128)(2,1)S(1)}, u32[]{:S(2)}, u32[]{:S(2)}) %collective-permute-start.17) | collective-permute-done | bytes 524320 | tf_op jit(solution)/shard_map/ppermute | solution.py:139
  156.2 5.0 %add_convert_fusion.9 = (bf16[1024,256]{1,0:T(8,128)(2,1)}, bf16[1024,256]{1,0:T(8,128)(2,1)}) fusion(bf16[1024,256]{1,0:T(8,128)(2,1)S(1)} %collective-permute-done.16, bf16[1024,256]{1,0:T(8,128)(2,1)S(1)} %copy-done.70, pred[]{:T(512)S(6)} %eq.10, pred[]{:T(512)S(6)} %eq.9, bf16[1024,2048]{1,0:T(8,128)(2,1)} %copy-done.38, ...), kind=kOutput, calls=%fused_computation.133 | convolution fusion | flops 1075576832 | bytes 7340034 | tf_op jit(solution)/shard_map/dot_general | solution.py:337
  170.1 6.1 %collective-permute-start.21 = (bf16[1024,256]{1,0:T(8,128)(2,1)}, bf16[1024,256]{1,0:T(8,128)(2,1)}, u32[]{:S(2)}, u32[]{:S(2)}) collective-permute-start(bf16[1024,256]{1,0:T(8,128)(2,1)} %get-tuple-element.108), channel_id=1, source_target_pairs={{0,1},{1,0},{2,3},{3,2},{4,5},{5,4},{6,7},{7,6},{8,9},{9,8},{10,11... | collective-permute-start | bytes 1572872 | tf_op jit(solution)/shard_map/ppermute | solution.py:139
  176.2 5.5 %add_convert_fusion.10 = (bf16[1024,256]{1,0:T(8,128)(2,1)}, bf16[1024,256]{1,0:T(8,128)(2,1)}) fusion(bf16[1024,256]{1,0:T(8,128)(2,1)S(1)} %collective-permute-done.14, bf16[1024,256]{1,0:T(8,128)(2,1)S(1)} %copy-done.68, pred[]{:T(512)S(6)} %eq.10, pred[]{:T(512)S(6)} %eq.9, bf16[1024,2048]{1,0:T(8,128)(2,1)} %copy-done.38, ...), kind=kOutput, calls=%fused_computation.134 | convolution fusion | flops 1075576832 | bytes 7340034 | tf_op jit(solution)/shard_map/dot_general | solution.py:337
  181.7 8.1 %collective-permute-start.19 = (bf16[1024,256]{1,0:T(8,128)(2,1)}, bf16[1024,256]{1,0:T(8,128)(2,1)}, u32[]{:S(2)}, u32[]{:S(2)}) collective-permute-start(bf16[1024,256]{1,0:T(8,128)(2,1)} %get-tuple-element.106), channel_id=1, source_target_pairs={{0,1},{1,0},{2,3},{3,2},{4,5},{5,4},{6,7},{7,6},{8,9},{9,8},{10,11... | collective-permute-start | bytes 1572872 | tf_op jit(solution)/shard_map/ppermute | solution.py:139
  189.9 4.8 %add_convert_fusion.7 = (bf16[1024,256]{1,0:T(8,128)(2,1)}, bf16[1024,256]{1,0:T(8,128)(2,1)}) fusion(bf16[1024,256]{1,0:T(8,128)(2,1)} %collective-permute-done.20, bf16[1024,256]{1,0:T(8,128)(2,1)} %get-tuple-element.189, pred[]{:T(512)S(6)} %eq.10, pred[]{:T(512)S(6)} %eq.9, bf16[1024,2048]{1,0:T(8,128)(2,1)} %copy-done.38, ...), kind=kOutput, calls=%fused_computation.131 | convolution fusion | flops 1075576832 | bytes 7340034 | tf_op jit(solution)/shard_map/dot_general | solution.py:337
  232.7 5.8 %add_convert_fusion.6 = (bf16[1024,256]{1,0:T(8,128)(2,1)}, bf16[1024,256]{1,0:T(8,128)(2,1)}) fusion(bf16[1024,256]{1,0:T(8,128)(2,1)S(1)} %collective-permute-done.23, bf16[1024,256]{1,0:T(8,128)(2,1)} %get-tuple-element.195, pred[]{:T(512)S(6)} %eq.10, pred[]{:T(512)S(6)} %eq.9, bf16[1024,2048]{1,0:T(8,128)(2,1)} %copy-done.38, ...), kind=kOutput, calls=%fused_computation.130 | convolution fusion | flops 1075576832 | bytes 7340034 | tf_op jit(solution)/shard_map/dot_general | solution.py:337
  244.0 6.5 %collective-permute-start.28 = (bf16[1024,256]{1,0:T(8,128)(2,1)}, bf16[1024,256]{1,0:T(8,128)(2,1)}, u32[]{:S(2)}, u32[]{:S(2)}) collective-permute-start(bf16[1024,256]{1,0:T(8,128)(2,1)} %get-tuple-element.119), channel_id=1, source_target_pairs={{0,1},{1,0},{2,3},{3,2},{4,5},{5,4},{6,7},{7,6},{8,9},{9,8},{10,11... | collective-permute-start | bytes 1572872 | tf_op jit(solution)/shard_map/ppermute | solution.py:139
  251.3 4.8 %add_convert_fusion.3 = (bf16[1024,256]{1,0:T(8,128)(2,1)}, bf16[1024,256]{1,0:T(8,128)(2,1)}) fusion(bf16[1024,256]{1,0:T(8,128)(2,1)S(1)} %collective-permute-done.29, bf16[1024,256]{1,0:T(8,128)(2,1)S(1)} %copy-done.74, pred[]{:T(512)S(6)} %eq.10, pred[]{:T(512)S(6)} %eq.9, bf16[1024,2048]{1,0:T(8,128)(2,1)} %copy-done.38, ...), kind=kOutput, calls=%fused_computation.127 | convolution fusion | flops 1075576832 | bytes 7340034 | tf_op jit(solution)/shard_map/dot_general | solution.py:337
  281.4 5.8 %shard_map.32.refs_2_ = f32[1024,1024]{1,0:T(8,128)S(1)} custom-call(bf16[1024,1024]{1,0:T(8,128)(2,1)S(1)} %copy-done.1, bf16[2048,1024]{1,0:T(8,128)(2,1)S(1)} %copy-done.29, bf16[1024,1024]{1,0:T(8,128)(2,1)S(1)} %copy-done, bf16[2048,1024]{1,0:T(8,128)(2,1)S(1)} %copy-done.31, bf16[1024,1024]{1,0:T(8,128)(2,1)S(1)} %copy-done.1), custom_call_target="tpu_custom_call" | custom-call | flops 4294967296 | bytes 14680064 | tf_op jit(solution)/shard_map/pallas_call | solution.py:84
  299.1 5.9 %shard_map.35.refs_3_ = f32[1024,1024]{1,0:T(8,128)S(1)} custom-call(bf16[1024,1024]{1,0:T(8,128)(2,1)S(1)} %copy-done.2, bf16[2048,1024]{1,0:T(8,128)(2,1)S(1)} %copy-done.30, bf16[1024,1024]{1,0:T(8,128)(2,1)S(1)} %copy-done, bf16[2048,1024]{1,0:T(8,128)(2,1)S(1)} %copy-done.32, bf16[1024,1024]{1,0:T(8,128)(2,1)S(1)} %copy-done), custom_call_target="tpu_custom_call" | custom-call | flops 4294967296 | bytes 14680064 | tf_op jit(solution)/shard_map/pallas_call | solution.py:84
  313.1 5.5 %collective-permute-start.35 = (bf16[1024,256]{1,0:T(8,128)(2,1)}, bf16[1024,256]{1,0:T(8,128)(2,1)}, u32[]{:S(2)}, u32[]{:S(2)}) collective-permute-start(bf16[1024,256]{1,0:T(8,128)(2,1)} %get-tuple-element.129), channel_id=1, source_target_pairs={{0,1},{1,0},{2,3},{3,2},{4,5},{5,4},{6,7},{7,6},{8,9},{9,8},{10,11... | collective-permute-start | bytes 1572872 | tf_op jit(solution)/shard_map/ppermute | solution.py:139
  320.4 11.0 %collective-permute-start.37 = (bf16[1024,256]{1,0:T(8,128)(2,1)}, bf16[1024,256]{1,0:T(8,128)(2,1)}, u32[]{:S(2)}, u32[]{:S(2)}) collective-permute-start(bf16[1024,256]{1,0:T(8,128)(2,1)} %get-tuple-element.132), channel_id=1, source_target_pairs={{0,1},{1,0},{2,3},{3,2},{4,5},{5,4},{6,7},{7,6},{8,9},{9,8},{10,11... | collective-permute-start | bytes 1572872 | tf_op jit(solution)/shard_map/ppermute | solution.py:139
  378.5 9.2 %shard_map.40.refs_2_ = f32[1024,1024]{1,0:T(8,128)S(1)} custom-call(bf16[1024,1024]{1,0:T(8,128)(2,1)S(1)} %copy-done.7, bf16[2048,1024]{1,0:T(8,128)(2,1)S(1)} %copy-done.16, bf16[1024,1024]{1,0:T(8,128)(2,1)S(1)} %copy-done.7, bf16[2048,1024]{1,0:T(8,128)(2,1)S(1)} %copy-done.16, bf16[1024,1024]{1,0:T(8,128)(2,1)S(1)} %copy-done.3, ...), custom_call_target="tpu_custom_call" | custom-call | flops 6442450944 | bytes 39845888 | tf_op jit(solution)/shard_map/pallas_call | solution.py:84
  416.6 9.8 %shard_map.47.refs_6_ = bf16[1024,1024]{1,0:T(8,128)(2,1)S(1)} custom-call(bf16[1024,1024]{1,0:T(8,128)(2,1)S(1)} %copy-done.9, bf16[2048,1024]{1,0:T(8,128)(2,1)S(1)} %copy-done.15, bf16[1024,1024]{1,0:T(8,128)(2,1)S(1)} %copy-done.9, bf16[2048,1024]{1,0:T(8,128)(2,1)S(1)} %copy-done.15, bf16[1024,1024]{1,0:T(8,128)(2,1)S(1)} %copy-done.4, ...), custom_call_target="tpu_custom_call" | custom-call | flops 6442450944 | bytes 44040192 | tf_op jit(solution)/shard_map/pallas_call | solution.py:84
  436.4 22.5 %shard_map.48 = f32[1024,2048]{1,0:T(8,128)} custom-call(bf16[1024,1024]{1,0:T(8,128)(2,1)S(1)} %shard_map.44.refs_0_, bf16[1024,2048]{1,0:T(8,128)(2,1)S(1)} %copy-done.35, bf16[1024,1024]{1,0:T(8,128)(2,1)S(1)} %shard_map.45.refs_2_, bf16[1024,2048]{1,0:T(8,128)(2,1)S(1)} %copy-done.36, bf16[1024,1024]{1,0:T(8,128)(2,1)S(1)} %copy-done.34, ...), custom_call_target="tpu_custom_call" | custom-call | flops 17179869184 | bytes 33554432 | tf_op jit(solution)/shard_map/pallas_call | solution.py:84
  (353 shorter events, 269.9 us)
Async XLA Ops:
  6.5 24.1 %all-gather.13.cloned.1.call-start = ((), (), s32[]{:S(2)}) async-start(), calls=%async_computation.1 | async-start | bytes 6291456 | tf_op jit(solution)/shard_map/all_gather | solution.py:131
  14.1 48.9 %all-gather.11.cloned.1.call-start = ((), (), s32[]{:S(2)}) async-start(), calls=%async_computation | async-start | bytes 6291456 | tf_op jit(solution)/shard_map/all_gather | solution.py:131
  14.8 118.7 %all-gather.15.cloned.1.call-start = ((), (), s32[]{:S(2)}) async-start(), calls=%async_computation.2 | async-start | bytes 6291456 | tf_op jit(solution)/shard_map/all_gather | solution.py:131
  14.9 65.2 %collective-permute-start.3 = (bf16[512,2048]{1,0:T(8,128)(2,1)}, bf16[512,2048]{1,0:T(8,128)(2,1)}, u32[]{:S(2)}, u32[]{:S(2)}) collective-permute-start(bf16[512,2048]{1,0:T(8,128)(2,1)} %get-tuple-element.148), channel_id=1, source_target_pairs={{0,8},{4,12},{8,0},{12,4},{1,9},{5,13},{9,1},{13,5},{2,10},{6,14},... | collective-permute-start | bytes 6291464 | tf_op jit(solution)/shard_map/ppermute | solution.py:127
  80.1 133.3 %all-gather.17.cloned.1.call-start = ((), (), s32[]{:S(2)}) async-start(), calls=%async_computation.3 | async-start | bytes 6291456 | tf_op jit(solution)/shard_map/all_gather | solution.py:131
  85.5 52.7 %collective-permute-start.11 = (bf16[512,2048]{1,0:T(8,128)(2,1)S(1)}, bf16[512,2048]{1,0:T(8,128)(2,1)}, u32[]{:S(2)}, u32[]{:S(2)}) collective-permute-start(bf16[512,2048]{1,0:T(8,128)(2,1)S(1)} %copy-done.37), channel_id=1, source_target_pairs={{0,8},{4,12},{8,0},{12,4},{1,9},{5,13},{9,1},{13,5},{2,10},{6,14},... | collective-permute-start | bytes 6291464 | tf_op jit(solution)/shard_map/ppermute | solution.py:127
  87.0 21.6 %collective-permute-start.5 = (bf16[1024,256]{1,0:T(8,128)(2,1)}, bf16[1024,256]{1,0:T(8,128)(2,1)}, u32[]{:S(2)}, u32[]{:S(2)}) collective-permute-start(bf16[1024,256]{1,0:T(8,128)(2,1)} %get-tuple-element.85), channel_id=1, source_target_pairs={{1,2},{2,1},{5,6},{6,5},{9,10},{10,9},{13,14},{14,13},{17,18},{18,... | collective-permute-start | bytes 1572872 | tf_op jit(solution)/shard_map/ppermute | solution.py:139
  88.4 24.8 %collective-permute-start.6 = (bf16[1024,256]{1,0:T(8,128)(2,1)}, bf16[1024,256]{1,0:T(8,128)(2,1)}, u32[]{:S(2)}, u32[]{:S(2)}) collective-permute-start(bf16[1024,256]{1,0:T(8,128)(2,1)} %get-tuple-element.86), channel_id=1, source_target_pairs={{0,1},{1,0},{2,3},{3,2},{4,5},{5,4},{6,7},{7,6},{8,9},{9,8},{10,11... | collective-permute-start | bytes 1572872 | tf_op jit(solution)/shard_map/ppermute | solution.py:139
  101.0 24.8 %collective-permute-start.13 = (bf16[1024,256]{1,0:T(8,128)(2,1)}, bf16[1024,256]{1,0:T(8,128)(2,1)}, u32[]{:S(2)}, u32[]{:S(2)}) collective-permute-start(bf16[1024,256]{1,0:T(8,128)(2,1)} %get-tuple-element.95), channel_id=1, source_target_pairs={{0,1},{1,0},{2,3},{3,2},{4,5},{5,4},{6,7},{7,6},{8,9},{9,8},{10,11... | collective-permute-start | bytes 1572872 | tf_op jit(solution)/shard_map/ppermute | solution.py:139
  138.3 137.2 %all-gather.19.cloned.1.call-start = ((), (), s32[]{:S(2)}) async-start(), calls=%async_computation.4 | async-start | bytes 6291456 | tf_op jit(solution)/shard_map/all_gather | solution.py:131
  166.4 109.0 %all-gather.21.cloned.1.call-start = ((), (), s32[]{:S(2)}) async-start(), calls=%async_computation.5 | async-start | bytes 6291456 | tf_op jit(solution)/shard_map/all_gather | solution.py:131
  167.2 22.7 %collective-permute-start.20 = (bf16[1024,256]{1,0:T(8,128)(2,1)}, bf16[1024,256]{1,0:T(8,128)(2,1)}, u32[]{:S(2)}, u32[]{:S(2)}) collective-permute-start(bf16[1024,256]{1,0:T(8,128)(2,1)} %get-tuple-element.107), channel_id=1, source_target_pairs={{1,2},{2,1},{5,6},{6,5},{9,10},{10,9},{13,14},{14,13},{17,18},{18,... | collective-permute-start | bytes 1572872 | tf_op jit(solution)/shard_map/ppermute | solution.py:139
  168.6 54.0 %collective-permute-start.26 = (bf16[1024,1024]{1,0:T(8,128)(2,1)}, bf16[1024,1024]{1,0:T(8,128)(2,1)S(1)}, u32[]{:S(2)}, u32[]{:S(2)}) collective-permute-start(bf16[1024,1024]{1,0:T(8,128)(2,1)} %get-tuple-element.115.refs_0_.refs_4_.refs_6_), channel_id=1, source_target_pairs={{0,8},{4,12},{8,0},{12,4},{1,9},{5,13},{9,1},{13,5},{2,10},{6,14},... | collective-permute-start | bytes 6291464 | tf_op jit(solution)/shard_map/ppermute | solution.py:127
  170.1 24.6 %collective-permute-start.21 = (bf16[1024,256]{1,0:T(8,128)(2,1)}, bf16[1024,256]{1,0:T(8,128)(2,1)}, u32[]{:S(2)}, u32[]{:S(2)}) collective-permute-start(bf16[1024,256]{1,0:T(8,128)(2,1)} %get-tuple-element.108), channel_id=1, source_target_pairs={{0,1},{1,0},{2,3},{3,2},{4,5},{5,4},{6,7},{7,6},{8,9},{9,8},{10,11... | collective-permute-start | bytes 1572872 | tf_op jit(solution)/shard_map/ppermute | solution.py:139
  223.9 121.3 %all-gather.23.cloned.1.call-start = ((), (), s32[]{:S(2)}) async-start(), calls=%async_computation.6 | async-start | bytes 6291456 | tf_op jit(solution)/shard_map/all_gather | solution.py:131
  229.9 26.3 %collective-permute-start.30 = (bf16[1024,256]{1,0:T(8,128)(2,1)}, bf16[1024,256]{1,0:T(8,128)(2,1)}, u32[]{:S(2)}, u32[]{:S(2)}) collective-permute-start(bf16[1024,256]{1,0:T(8,128)(2,1)} %get-tuple-element.122), channel_id=1, source_target_pairs={{0,1},{1,0},{2,3},{3,2},{4,5},{5,4},{6,7},{7,6},{8,9},{9,8},{10,11... | collective-permute-start | bytes 1572872 | tf_op jit(solution)/shard_map/ppermute | solution.py:139
  259.2 49.9 %collective-permute-start.34 = (bf16[1024,1024]{1,0:T(8,128)(2,1)S(1)}, bf16[1024,1024]{1,0:T(8,128)(2,1)}, u32[]{:S(2)}, u32[]{:S(2)}) collective-permute-start(bf16[1024,1024]{1,0:T(8,128)(2,1)S(1)} %copy-done), channel_id=1, source_target_pairs={{0,8},{4,12},{8,0},{12,4},{1,9},{5,13},{9,1},{13,5},{2,10},{6,14},... | collective-permute-start | bytes 6291464 | tf_op jit(solution)/shard_map/ppermute | solution.py:127
  261.4 30.7 %collective-permute-start.32 = (bf16[1024,256]{1,0:T(8,128)(2,1)}, bf16[1024,256]{1,0:T(8,128)(2,1)}, u32[]{:S(2)}, u32[]{:S(2)}) collective-permute-start(bf16[1024,256]{1,0:T(8,128)(2,1)} %get-tuple-element.126), channel_id=1, source_target_pairs={{1,2},{2,1},{5,6},{6,5},{9,10},{10,9},{13,14},{14,13},{17,18},{18,... | collective-permute-start | bytes 1572872 | tf_op jit(solution)/shard_map/ppermute | solution.py:139
  309.2 54.6 %all-gather.27.cloned.1.call-start = ((), (), s32[]{:S(2)}) async-start(), calls=%async_computation.8 | async-start | bytes 6291456 | tf_op jit(solution)/shard_map/all_gather | solution.py:131
  309.9 63.2 %all-gather.25.cloned.1.call-start = ((), (), s32[]{:S(2)}) async-start(), calls=%async_computation.7 | async-start | bytes 6291456 | tf_op jit(solution)/shard_map/all_gather | solution.py:131
  310.6 98.4 %all-gather.29.cloned.1.call-start = ((), (), s32[]{:S(2)}) async-start(), calls=%async_computation.9 | async-start | bytes 6291456 | tf_op jit(solution)/shard_map/all_gather | solution.py:131
  313.1 23.4 %collective-permute-start.35 = (bf16[1024,256]{1,0:T(8,128)(2,1)}, bf16[1024,256]{1,0:T(8,128)(2,1)}, u32[]{:S(2)}, u32[]{:S(2)}) collective-permute-start(bf16[1024,256]{1,0:T(8,128)(2,1)} %get-tuple-element.129), channel_id=1, source_target_pairs={{0,1},{1,0},{2,3},{3,2},{4,5},{5,4},{6,7},{7,6},{8,9},{9,8},{10,11... | collective-permute-start | bytes 1572872 | tf_op jit(solution)/shard_map/ppermute | solution.py:139
  320.4 22.5 %collective-permute-start.37 = (bf16[1024,256]{1,0:T(8,128)(2,1)}, bf16[1024,256]{1,0:T(8,128)(2,1)}, u32[]{:S(2)}, u32[]{:S(2)}) collective-permute-start(bf16[1024,256]{1,0:T(8,128)(2,1)} %get-tuple-element.132), channel_id=1, source_target_pairs={{0,1},{1,0},{2,3},{3,2},{4,5},{5,4},{6,7},{7,6},{8,9},{9,8},{10,11... | collective-permute-start | bytes 1572872 | tf_op jit(solution)/shard_map/ppermute | solution.py:139
  332.5 57.3 %collective-permute-start.39 = (bf16[1024,256]{1,0:T(8,128)(2,1)}, bf16[1024,256]{1,0:T(8,128)(2,1)}, u32[]{:S(2)}, u32[]{:S(2)}) collective-permute-start(bf16[1024,256]{1,0:T(8,128)(2,1)} %get-tuple-element.140), channel_id=1, source_target_pairs={{0,1},{1,0},{2,3},{3,2},{4,5},{5,4},{6,7},{7,6},{8,9},{9,8},{10,11... | collective-permute-start | bytes 1572872 | tf_op jit(solution)/shard_map/ppermute | solution.py:139
  (120 other events, 1036.3 us)
Sparse Core Ops, SparseCore 0:
  14.2 16.3 all-gather.12
  32.2 14.8 all-gather.10
  80.2 14.8 all-gather.14
  138.4 13.5 all-gather.16
  166.5 13.5 all-gather.18
  224.1 13.9 all-gather.20
  309.3 13.1 all-gather.22
  324.0 14.8 all-gather.26
  340.4 14.8 all-gather.24
  395.3 13.6 all-gather.28

commit v3 on v2

--- a/solution.py
+++ b/solution.py
@@ -20,6 +20,9 @@
 SKEW = 2
 TILE = 256
 STRIPE = 512
+VMEM = 60 * 1024 * 1024
+SMALL = VMEM
+PARTS = 4
 
 NN = (((1,), (0,)), ((), ()))
 NT = (((1,), (1,)), ((), ()))
@@ -93,11 +96,132 @@
         grid=(width // tile,),
         in_specs=specs,
         out_specs=pl.BlockSpec((m, tile), lambda j: (0, j)),
-        compiler_params=pltpu.CompilerParams(vmem_limit_bytes=36 * 1024 * 1024),
+        compiler_params=pltpu.CompilerParams(vmem_limit_bytes=VMEM),
         cost_estimate=pl.CostEstimate(
-            flops=flops, bytes_accessed=moved, transcendentals=0
+            flops=flops, bytes_accessed=0, transcendentals=0
         ),
     )(*operands)
+
+
+def gram_body(where, left, right, out):
+    out[0] = lax.dot_general(
+        left[...], right[...], NT, preferred_element_type=jnp.float32
+    ).astype(out.dtype)
+
+
+def gram(left, right, where, count, width):
+    m, n = left.shape
+    return pl.pallas_call(
+        gram_body,
+        out_shape=jax.ShapeDtypeStruct((count, m, width), jnp.bfloat16),
+        grid_spec=pltpu.PrefetchScalarGridSpec(
+            num_scalar_prefetch=1,
+            grid=(count,),
+            in_specs=[
+                pl.BlockSpec(
+                    (m, n), lambda j, where: (0, 0), pipeline_mode=pl.Buffered(1)
+                ),
+                pl.BlockSpec((width, n), lambda j, where: (where[0] + j, 0)),
+            ],
+            out_specs=pl.BlockSpec((1, m, width), lambda j, where: (j, 0, 0)),
+        ),
+        compiler_params=pltpu.CompilerParams(vmem_limit_bytes=VMEM),
+        cost_estimate=pl.CostEstimate(
+            flops=2 * m * n * width * count,
+            bytes_accessed=0,
+            transcendentals=0,
+        ),
+    )(where, left, right)
+
+
+def mix_body(top, plan, where, *refs):
+    outs = refs[-len(plan) :]
+    for out, choices in zip(outs, plan):
+        total = None
+        for flip, options in choices:
+            here = top - where[0] if flip else where[0]
+            value = None
+            for k, slot in options:
+                if slot is None:
+                    new = jnp.zeros(out.shape, jnp.float32)
+                else:
+                    new = refs[slot][...].reshape(out.shape).astype(jnp.float32)
+                value = new if value is None else jnp.where(here == k, new, value)
+            total = value if total is None else total + value
+        out[...] = total.astype(out.dtype)
+
+
+def mix_all(top, plan, count, idle, where, *refs):
+    ins, outs = refs[:count], refs[count + idle :]
+    mix_body(top, plan, where, *ins, *outs[: len(plan)])
+
+
+def mix(where, top, sums, held, parts):
+    sources, uses, plan = [], [], []
+
+    def slot_of(source, use):
+        if source is None:
+            return None
+        for k, (array, chunk) in enumerate(sources):
+            if array is source[0] and chunk == source[1]:
+                uses[k].append(use)
+                return k
+        sources.append(source)
+        uses.append([use])
+        return len(sources) - 1
+
+    for terms in sums:
+        plan.append(
+            tuple(
+                (
+                    flip,
+                    tuple(
+                        (k, slot_of(source, (flip, k) if len(options) > 1 else None))
+                        for k, source in options
+                    ),
+                )
+                for flip, options in terms
+            )
+        )
+    array, chunk = sources[0]
+    m, w = array.shape[-2:]
+    high = m // parts
+    specs = []
+    for (array, chunk), used in zip(sources, uses):
+
+        def at(j, where, chunk=chunk, used=used):
+            row = j
+            if None not in used:
+                live = False
+                for flip, k in used:
+                    live = live | (where[0] == (top - k if flip else k))
+                row = jnp.where(live, j, 0)
+            return (row, 0) if chunk is None else (chunk, row, 0)
+
+        specs.append(pl.BlockSpec((high, w) if chunk is None else (1, high, w), at))
+    anywhere = pl.BlockSpec(memory_space=pl.ANY)
+    idle, count = len(held), len(sources)
+    return list(
+        pl.pallas_call(
+            functools.partial(mix_all, top, tuple(plan), count, idle),
+            out_shape=[jax.ShapeDtypeStruct((m, w), jnp.bfloat16)] * len(plan)
+            + [jax.ShapeDtypeStruct(v.shape, v.dtype) for v in held],
+            grid_spec=pltpu.PrefetchScalarGridSpec(
+                num_scalar_prefetch=1,
+                grid=(parts,),
+                in_specs=specs + [anywhere] * idle,
+                out_specs=[pl.BlockSpec((high, w), lambda j, where: (j, 0))] * len(plan)
+                + [anywhere] * idle,
+            ),
+            input_output_aliases={
+                1 + count + k: len(plan) + k for k in range(idle)
+            },
+            compiler_params=pltpu.CompilerParams(vmem_limit_bytes=SMALL),
+            cost_estimate=pl.CostEstimate(
+                flops=10**10, bytes_accessed=0, transcendentals=0
+            ),
+        )(where, *[a for a, _ in sources], *held)
+    )
 
 
 def gate_body(*refs):
@@ -113,6 +237,7 @@
             in_specs=[anywhere] * len(values),
             out_specs=[anywhere] * len(values),
             input_output_aliases={k: k for k in range(len(values))},
+            compiler_params=pltpu.CompilerParams(vmem_limit_bytes=VMEM),
             cost_estimate=pl.CostEstimate(flops=0, bytes_accessed=0, transcendentals=0),
         )(*values)
     )
@@ -138,26 +263,17 @@
             pairs += [(i, i + 1), (i + 1, i)]
         return lax.ppermute(value, "cols", pairs)
 
-    def choose(index, options):
-        out = None
-        for k, o in options:
-            out = o if out is None else jnp.where(index == k, o, out)
-        return out
-
-    def wide(value):
-        return value.astype(jnp.float32)
-
     def on_device(iterate):
         m, n = iterate.shape
         mp = m // PIECES
-        w = min(WIDTH, 2 * mp)
+        w = min(WIDTH, mp)
         q = 2 * mp // w
         tile = min(TILE, mp)
         z = lax.axis_index("cols")
+        core = lax.axis_index("rows") % 2
         even = jnp.where(z % 2 == 0, z, cols - 1 - z)
-        odd = cols - 1 - even
+        where = jnp.reshape(even, (1,)).astype(jnp.int32)
         x0 = iterate.astype(jnp.bfloat16)
-        zero = jnp.zeros((m, w), jnp.bfloat16)
 
         groups = [(d, p) for d in range(chips) for p in range(PIECES)]
         order = [(g, i) for g in groups for i in range(q)]
@@ -209,30 +325,31 @@
             passing[end].append(("x", g))
             then(end, functools.partial(settle, g))
 
-        own, got_e, got_o, chunks = [], {}, {}, {}
+        own, sent, got_e, got_o, chunks = [], {}, {}, {}, {}
         strip, chip, far = {}, {}, {}
 
         def at(values, j):
             if isinstance(values, dict):
-                return values.get(j, zero)
-            return values[j] if 0 <= j < len(values) else zero
-
-        def finish(j):
-            came_e = choose(
-                even,
-                [
-                    (k, at(got_e, j + SKEW * (cols - 2 - k)))
-                    for k in range(0, cols - 1, 2)
-                ],
-            )
-            came_o = choose(
-                even,
-                [(0, zero)]
-                + [(k, at(got_o, j + SKEW * (k - 1))) for k in range(2, cols - 1, 2)],
-            )
-            chunks[order[j]] = (wide(own[j]) + wide(came_e) + wide(came_o)).astype(
-                jnp.bfloat16
-            )
+                return (values[j], None) if j in values else None
+            return values[j] if 0 <= j < len(values) else None
+
+        def at_row(chunk):
+            return jnp.full((1,), chunk, jnp.int32)
+
+        def final(j):
+            return [
+                (
+                    False,
+                    [(k, at(sent, j + SKEW * k)) for k in range(0, cols - 1, 2)],
+                ),
+                (
+                    False,
+                    [
+                        (k, at(got_e, j + SKEW * (cols - 2 - k)))
+                        for k in range(0, cols - 1, 2)
+                    ],
+                ),
+            ]
 
         def launch(g, s):
             d0, p = g
@@ -253,12 +370,13 @@
             far[d, e, p] = side(held.pop(("f", d, e, p)))
 
         def complete(g, s):
-            held["s", g] = jnp.concatenate([chunks[g, i] for i in range(q)], axis=1)
-            if s < steps:
-                passing[s].append(("s", g))
-                follow[s].append(functools.partial(launch, g, s))
-            else:
-                launch(g, s)
+            parts = [chunks[g, i] for i in range(q)]
+            if g[0] == 0:
+                near, beside = parts[: q // 2], parts[q // 2 :]
+                parts = [jnp.where(core == 0, a, b) for a, b in zip(near, beside)]
+                parts += [jnp.where(core == 0, b, a) for a, b in zip(near, beside)]
+            held["s", g] = jnp.concatenate(parts, axis=1)
+            launch(g, s)
 
         poly, others = {}, {}
 
@@ -333,38 +451,50 @@
         for s in range(steps):
             if s < count:
                 g, i = order[s]
-                own.append(
-                    lax.dot_general(
-                        x0,
-                        blocks[g][i * w : (i + 1) * w],
-                        NT,
-                        preferred_element_type=jnp.float32,
-                    ).astype(jnp.bfloat16)
+                d, p = g
+                near = q // 2
+                made = None
+                if d == 0 and i == 0:
+                    made = gram(x0, x0, at_row(p * near), near, w)
+                elif d == 0 and i == near:
+                    made = gram(x0, blocks[g], at_row((1 - core) * near), near, w)
+                elif d > 0 and i == 0:
+                    made = gram(x0, blocks[g], at_row(0), q, w)
+                if made is not None:
+                    own += [(made, c) for c in range(made.shape[0])]
+            evens, odds = range(0, cols - 1, 2), range(1, cols - 1, 2)
+            last_e, last_o = at(got_e, s - SKEW), at(got_o, s - SKEW)
+            sums = [
+                [
+                    (False, [(k, at(own, s - SKEW * k)) for k in evens]),
+                    (False, [(k, last_o if k else None) for k in evens]),
+                ]
+            ]
+            if SKEW <= s < count + SKEW * (cols - 3):
+                sums.append(
+                    [
+                        (True, [(k, at(own, s - SKEW * k)) for k in odds]),
+                        (True, [(cols, last_e)]),
+                    ]
                 )
+            sends = len(sums)
+            j = s - lag - SKEW
+            if j >= 0:
+                sums.append(final(j))
+            keys = passing[s]
+            out = mix(where, cols - 1, sums, [held[k] for k in keys] + [token], PARTS)
+            if j >= 0:
+                chunks[order[j]] = out[sends]
+            token = out[-1]
+            sent[s] = out[0]
+            got_e[s] = trade(out[0], 0)
+            if sends > 1:
+                got_o[s] = trade(out[1], 1)
+            for k, v in zip(keys, out[len(sums) : -1]):
+                held[k] = v
             for g in groups:
                 if ready[g] == s:
-                    for i in range(q):
-                        finish(order.index((g, i)))
                     complete(g, s)
-            last_e, last_o = at(got_e, s - SKEW), at(got_o, s - SKEW)
-            mine_e = choose(
-                even, [(k, at(own, s - SKEW * k)) for k in range(0, cols - 1, 2)]
-            )
-            carry = jnp.where(even == 0, zero, last_o)
-            sends = [(wide(mine_e) + wide(carry)).astype(jnp.bfloat16)]
-            if SKEW <= s < count + SKEW * (cols - 3):
-                mine_o = choose(
-                    odd, [(k, at(own, s - SKEW * k)) for k in range(1, cols - 1, 2)]
-                )
-                sends.append((wide(mine_o) + wide(last_e)).astype(jnp.bfloat16))
-            keys = passing[s]
-            out = gate(sends + [held[k] for k in keys] + [token])
-            token = out[-1]
-            got_e[s] = trade(out[0], 0)
-            if len(sends) > 1:
-                got_o[s] = trade(out[1], 1)
-            for k, v in zip(keys, out[len(sends) : -1]):
-                held[k] = v
             for action in follow[s]:
                 action()
         for action in late:
@@ -375,7 +505,9 @@
             for g in wanted:
                 if g not in strip:
                     for i in range(q):
-                        finish(order.index((g, i)))
+                        if (g, i) not in chunks:
+                            j = order.index((g, i))
+                            chunks[g, i] = mix(where, cols - 1, [final(j)], [], PARTS)[0]
                     complete(g, steps)
             for e in range(1, chips):
                 for p in range(PIECES):

time: 476 us -> 423 us (0.89); the launches traced: 466 us -> 419 us
  Pallas kernels: 75.5 us -> 239 us
  matrix products: 79.4 us -> 0 us
  other arithmetic: 58 us -> 12.1 us
  local copies, waits for them, and re-layouts: 68.9 us -> 27.7 us
  starting transfers between devices: 105 us -> 75.9 us
  waiting for transfers between devices: 65.1 us -> 50.9 us
    pallas_call x0 -> x28, Pallas kernels: none -> 128 us  [the longest x22 85.1 us: mix(): pl.pallas_call(functools.partial(mix_all, top, tuple(plan), count, idle),...]
    dot_general x16 -> x0, matrix products: 79.4 us -> none  [on_device(): lax.dot_general(x0, blocks[g][i * w:(i + 1) * w], NT, preferred_element_t...]
    convert_element_type x24 -> x0, other arithmetic: 45.9 us -> none  [the longest x12 28.4 us: finish(): (wide(own[j]) + wide(came_e) + wide(came_o)).astype(jnp.bfloat16)]
    unnamed x188 -> x97, local copies, waits for them, and re-layouts: 65.6 us -> 22.6 us
    pallas_call x11, Pallas kernels: 75.5 us -> 111 us  [dots(): pl.pallas_call(functools.partial(dots_body, tuple(flips), (dot_scale,) +...]
    ppermute x36, starting transfers between devices: 96.8 us -> 71.3 us  [trade(): return lax.ppermute(value, 'cols', pairs)]
    ppermute x36, waiting for transfers between devices: 47.7 us -> 38.1 us  [trade(): return lax.ppermute(value, 'cols', pairs)]
    all_gather x10, waiting for transfers between devices: 15.2 us -> 5.95 us  [side(): lax.all_gather(value, 'rows', axis=0, tiled=True, axis_index_groups=pairs)]
  transfers between devices with their start and end apart: 50 -> 50, of which waited for: 13 -> 12; matrix products, arithmetic and copies ran while one was open for 28% -> 3% of each run, Pallas kernels for 8% -> 41%
where the time goes in v3:
time: 423 us; the launch traced here: 419 us
  Pallas kernels  239 us (57%)
  starting transfers between devices  75.9 us (18%)
  waiting for transfers between devices  50.9 us (12%)
  local copies, waits for them, and re-layouts  27.7 us (7%)
  between operations  14 us (3%)
  other arithmetic  12.1 us (3%)
    pallas_call x11, Pallas kernels, dots(): pl.pallas_call(functools.partial(dots_body, tuple(flips), (dot_scale,) +...  111 us
    pallas_call x22, Pallas kernels, mix(): pl.pallas_call(functools.partial(mix_all, top, tuple(plan), count, idle),...  85.1 us
    ppermute x36, starting transfers between devices, trade(): return lax.ppermute(value, 'cols', pairs)  71.3 us
    pallas_call x6, Pallas kernels, gram(): pl.pallas_call(gram_body, out_shape=jax.ShapeDtypeStruct((count, m, width...  42.6 us
    ppermute x36, waiting for transfers between devices, trade(): return lax.ppermute(value, 'cols', pairs)  38.1 us
    unnamed x97, local copies, waits for them, and re-layouts  22.6 us
  transfers between devices with their start and end apart: 50, of which 12 were waited for; matrix products, arithmetic and copies ran while one was open for 3% of the time, Pallas kernels for 41%

profile of v3, /device:TPU:0, one launch (start us, length us, event | category | flops | bytes accessed | tf_op | source)
XLA Modules:
  0.0 419.3 jit_solution(9420607159623933005)
XLA Ops:
  18.6 6.1 %shard_map.18.refs_0_.refs_1_ = bf16[2,1024,256]{2,1,0:T(8,128)(2,1)} custom-call(s32[1]{0:T(128)} %constant.30.clone.1.where, bf16[1024,2048]{1,0:T(8,128)(2,1)} %copy-done, bf16[1024,2048]{1,0:T(8,128)(2,1)} %copy-done), custom_call_target="tpu_custom_call" | custom-call | flops 2147483648 | tf_op jit(solution)/shard_map/pallas_call | solution.py:114
  32.9 5.9 %shard_map.17.refs_0_.refs_3_.refs_1_ = bf16[2,1024,256]{2,1,0:T(8,128)(2,1)} custom-call(s32[1]{0:T(128)} %constant.31.clone.1.where, bf16[1024,2048]{1,0:T(8,128)(2,1)} %copy-done, bf16[1024,2048]{1,0:T(8,128)(2,1)} %copy-done), custom_call_target="tpu_custom_call" | custom-call | flops 2147483648 | tf_op jit(solution)/shard_map/pallas_call | solution.py:114
  38.8 6.6 %shard_map.19.refs_0_.refs_3_.refs_1_ = bf16[2,1024,256]{2,1,0:T(8,128)(2,1)} custom-call(s32[1]{0:T(128)} %bitcast.1.where, bf16[1024,2048]{1,0:T(8,128)(2,1)} %copy-done, bf16[1024,2048]{1,0:T(8,128)(2,1)} %all-gather.11.cloned.1.call-done.right.refs_1_), custom_call_target="tpu_custom_call" | custom-call | flops 2147483648 | tf_op jit(solution)/shard_map/pallas_call | solution.py:114
  59.7 4.7 %collective-permute-done.3.refs_5_ = bf16[512,2048]{1,0:T(8,128)(2,1)} collective-permute-done((bf16[512,2048]{1,0:T(8,128)(2,1)S(1)}, bf16[512,2048]{1,0:T(8,128)(2,1)}, u32[]{:S(2)}, u32[]{:S(2)}) %collective-permute-start.3) | collective-permute-done | bytes 2097184 | tf_op jit(solution)/shard_map/ppermute | solution.py:252
  76.0 6.6 %shard_map.26.refs_0_.refs_3_.refs_1_ = bf16[2,1024,256]{2,1,0:T(8,128)(2,1)} custom-call(s32[1]{0:T(128)} %bitcast.1.where, bf16[1024,2048]{1,0:T(8,128)(2,1)} %copy-done, bf16[1024,2048]{1,0:T(8,128)(2,1)} %all-gather.15.cloned.1.call-done.right.refs_3_), custom_call_target="tpu_custom_call" | custom-call | flops 2147483648 | tf_op jit(solution)/shard_map/pallas_call | solution.py:114
  115.3 8.7 %shard_map.25.refs_0_.refs_3_.refs_1_ = bf16[4,1024,256]{2,1,0:T(8,128)(2,1)} custom-call(s32[1]{0:T(128)} %constant.30.clone.1.where, bf16[1024,2048]{1,0:T(8,128)(2,1)} %copy-done, bf16[1024,2048]{1,0:T(8,128)(2,1)} %all-gather.13.cloned.1.call-done.right.refs_5_), custom_call_target="tpu_custom_call" | custom-call | flops 4294967296 | tf_op jit(solution)/shard_map/pallas_call | solution.py:114
  130.5 4.6 %collective-permute-start.17 = (bf16[1024,256]{1,0:T(8,128)(2,1)S(1)}, bf16[1024,256]{1,0:T(8,128)(2,1)S(1)}, u32[]{:S(2)}, u32[]{:S(2)}) collective-permute-start(bf16[1024,256]{1,0:T(8,128)(2,1)S(1)} %copy-done.20), channel_id=1, source_target_pairs={{0,1},{1,0},{2,3},{3,2},{4,5},{5,4},{6,7},{7,6},{8,9},{9,8},{10,11... | collective-permute-start | bytes 1572872 | tf_op jit(solution)/shard_map/ppermute | solution.py:264
  137.8 10.2 %collective-permute-done.17.refs_4_.refs_7_ = bf16[1024,256]{1,0:T(8,128)(2,1)S(1)} collective-permute-done((bf16[1024,256]{1,0:T(8,128)(2,1)S(1)}, bf16[1024,256]{1,0:T(8,128)(2,1)S(1)}, u32[]{:S(2)}, u32[]{:S(2)}) %collective-permute-start.17) | collective-permute-done | bytes 524320 | tf_op jit(solution)/shard_map/ppermute | solution.py:264
  160.8 4.3 %shard_map.33 = (bf16[1024,256]{1,0:T(8,128)(2,1)}, bf16[1024,256]{1,0:T(8,128)(2,1)}, bf16[1024,256]{1,0:T(8,128)(2,1)}, f32[8,128]{1,0:T(8,128)}) custom-call(s32[1]{0:T(128)} %bitcast.where, bf16[4,1024,256]{2,1,0:T(8,128)(2,1)} %shard_map.25.refs_0_.refs_3_.refs_1_, ...), custom_call_target="tpu_custom_call", output_to_operand_aliasing={{3}: (9, {})} | custom-call | flops 10000000000 | tf_op jit(solution)/shard_map/pallas_call | solution.py:205
  181.1 8.7 %shard_map.31.refs_0_.refs_3_.refs_2_ = bf16[4,1024,256]{2,1,0:T(8,128)(2,1)} custom-call(s32[1]{0:T(128)} %constant.30.clone.1.where, bf16[1024,2048]{1,0:T(8,128)(2,1)} %copy-done, bf16[1024,2048]{1,0:T(8,128)(2,1)} %all-gather.17.cloned.1.call-done.right.refs_7_), custom_call_target="tpu_custom_call" | custom-call | flops 4294967296 | tf_op jit(solution)/shard_map/pallas_call | solution.py:114
  210.7 5.4 %collective-permute-done.23.refs_4_.refs_5_ = bf16[1024,256]{1,0:T(8,128)(2,1)S(1)} collective-permute-done((bf16[1024,256]{1,0:T(8,128)(2,1)S(1)}, bf16[1024,256]{1,0:T(8,128)(2,1)S(1)}, u32[]{:S(2)}, u32[]{:S(2)}) %collective-permute-start.23) | collective-permute-done | bytes 524320 | tf_op jit(solution)/shard_map/ppermute | solution.py:264
  239.7 9.7 %shard_map.38.refs_7_ = f32[1024,1024]{1,0:T(8,128)} custom-call(bf16[1024,1024]{1,0:T(8,128)(2,1)} %copy-done.1, bf16[2048,1024]{1,0:T(8,128)(2,1)} %all-gather.19.cloned.1.call-done.refs_1_, bf16[1024,1024]{1,0:T(8,128)(2,1)} %pad_maximum_fusion.1.refs_2_.refs_4_.refs_8_.refs_10_, bf16[2048,1024]{1,0:T(8,128)(2,1)} %all-gather.21.cloned.1.call-done.refs_3_, ...), custom_call_target="tpu_custom_call" | custom-call | flops 4294967296 | tf_op jit(solution)/shard_map/pallas_call | solution.py:87
  255.3 9.6 %shard_map.41.refs_8_ = f32[1024,1024]{1,0:T(8,128)} custom-call(bf16[1024,1024]{1,0:T(8,128)(2,1)} %copy-done.1, bf16[2048,1024]{1,0:T(8,128)(2,1)} %all-gather.19.cloned.1.call-done.refs_1_, bf16[1024,1024]{1,0:T(8,128)(2,1)} %pad_maximum_fusion.1.refs_2_.refs_4_.refs_8_.refs_10_, bf16[2048,1024]{1,0:T(8,128)(2,1)} %all-gather.21.cloned.1.call-done.refs_3_, ...), custom_call_target="tpu_custom_call" | custom-call | flops 4294967296 | tf_op jit(solution)/shard_map/pallas_call | solution.py:87
  280.3 8.9 %collective-permute-done.32.refs_4_ = bf16[1024,256]{1,0:T(8,128)(2,1)S(1)} collective-permute-done((bf16[1024,256]{1,0:T(8,128)(2,1)S(1)}, bf16[1024,256]{1,0:T(8,128)(2,1)S(1)}, u32[]{:S(2)}, u32[]{:S(2)}) %collective-permute-start.32) | collective-permute-done | bytes 524320 | tf_op jit(solution)/shard_map/ppermute | solution.py:264
  307.5 7.8 %shard_map.47.refs_1_ = f32[1024,1024]{1,0:T(8,128)} custom-call(bf16[1024,1024]{1,0:T(8,128)(2,1)} %constant_dynamic-update-slice_fusion.refs_0_.refs_2_.refs_12_, bf16[2048,1024]{1,0:T(8,128)(2,1)} %all-gather.23.cloned.1.call-done.refs_1_.refs_5_.refs_7_.refs_9_.refs_11_, f32[1024,1024]{1,0:T(8,128)} %get-tuple-element.160.refs_2_), custom_call_target="tpu_custom_call" | custom-call | flops 2147483648 | tf_op jit(solution)/shard_map/pallas_call | solution.py:87
  315.4 7.3 %shard_map.46.refs_0_ = f32[1024,1024]{1,0:T(8,128)} custom-call(bf16[1024,1024]{1,0:T(8,128)(2,1)} %constant_dynamic-update-slice_fusion.refs_0_.refs_2_.refs_12_, bf16[2048,1024]{1,0:T(8,128)(2,1)} %all-gather.23.cloned.1.call-done.refs_1_.refs_5_.refs_7_.refs_9_.refs_11_, f32[1024,1024]{1,0:T(8,128)} %get-tuple-element.159.refs_2_), custom_call_target="tpu_custom_call" | custom-call | flops 2147483648 | tf_op jit(solution)/shard_map/pallas_call | solution.py:87
  322.7 6.3 %shard_map.49.refs_3_ = f32[1024,1024]{1,0:T(8,128)} custom-call(bf16[1024,1024]{1,0:T(8,128)(2,1)} %constant_dynamic-update-slice_fusion.refs_0_.refs_2_.refs_12_, bf16[2048,1024]{1,0:T(8,128)(2,1)} %all-gather.27.cloned.1.call-done.refs_1_.refs_3_, bf16[1024,1024]{1,0:T(8,128)(2,1)} %constant_dynamic-update-slice_fusion.refs_0_.refs_2_.refs_12_, ...), custom_call_target="tpu_custom_call" | custom-call | flops 2147483648 | tf_op jit(solution)/shard_map/pallas_call | solution.py:87
  329.0 12.1 %shard_map.48.refs_2_ = f32[1024,1024]{1,0:T(8,128)} custom-call(bf16[1024,1024]{1,0:T(8,128)(2,1)} %constant_dynamic-update-slice_fusion.refs_0_.refs_2_.refs_12_, bf16[2048,1024]{1,0:T(8,128)(2,1)} %all-gather.25.cloned.1.call-done.refs_1_.refs_3_, bf16[1024,1024]{1,0:T(8,128)(2,1)} %constant_dynamic-update-slice_fusion.refs_0_.refs_2_.refs_12_, ...), custom_call_target="tpu_custom_call" | custom-call | flops 6442450944 | tf_op jit(solution)/shard_map/pallas_call | solution.py:87
  348.3 7.0 %shard_map.54.refs_4_ = bf16[1024,1024]{1,0:T(8,128)(2,1)} custom-call(bf16[1024,1024]{1,0:T(8,128)(2,1)} %pad_maximum_fusion.2.refs_0_.refs_2_.refs_13_, bf16[2048,1024]{1,0:T(8,128)(2,1)} %all-gather.25.cloned.1.call-done.refs_1_.refs_3_, bf16[1024,1024]{1,0:T(8,128)(2,1)} %pad_maximum_fusion.2.refs_0_.refs_2_.refs_13_, ...), custom_call_target="tpu_custom_call" | custom-call | flops 2147483648 | tf_op jit(solution)/shard_map/pallas_call | solution.py:87
  355.3 5.9 %all-gather.29.cloned.1.call-done.refs_1_.refs_5_.refs_7_.refs_9_.refs_11_ = bf16[2048,1024]{1,0:T(8,128)(2,1)} async-done(((bf16[1024,1024]{1,0:T(8,128)(2,1)}), bf16[2048,1024]{1,0:T(8,128)(2,1)}) %all-gather.29.cloned.1.call-update) | async-done | bytes 4194320 | tf_op jit(solution)/shard_map/all_gather | solution.py:256
  361.2 12.5 %shard_map.55.refs_6_ = bf16[1024,1024]{1,0:T(8,128)(2,1)} custom-call(bf16[1024,1024]{1,0:T(8,128)(2,1)} %pad_maximum_fusion.2.refs_0_.refs_2_.refs_13_, bf16[2048,1024]{1,0:T(8,128)(2,1)} %all-gather.27.cloned.1.call-done.refs_1_.refs_3_, bf16[1024,1024]{1,0:T(8,128)(2,1)} %pad_maximum_fusion.2.refs_0_.refs_2_.refs_13_, ...), custom_call_target="tpu_custom_call" | custom-call | flops 6442450944 | tf_op jit(solution)/shard_map/pallas_call | solution.py:87
  373.8 7.0 %shard_map.53.refs_2_ = bf16[1024,1024]{1,0:T(8,128)(2,1)} custom-call(bf16[1024,1024]{1,0:T(8,128)(2,1)} %pad_maximum_fusion.2.refs_0_.refs_2_.refs_13_, bf16[2048,1024]{1,0:T(8,128)(2,1)} %all-gather.29.cloned.1.call-done.refs_1_.refs_5_.refs_7_.refs_9_.refs_11_, f32[1024,1024]{1,0:T(8,128)} %get-tuple-element.166.refs_2_), custom_call_target="tpu_custom_call" | custom-call | flops 2147483648 | tf_op jit(solution)/shard_map/pallas_call | solution.py:87
  380.8 6.9 %shard_map.52.refs_0_ = bf16[1024,1024]{1,0:T(8,128)(2,1)} custom-call(bf16[1024,1024]{1,0:T(8,128)(2,1)} %pad_maximum_fusion.2.refs_0_.refs_2_.refs_13_, bf16[2048,1024]{1,0:T(8,128)(2,1)} %all-gather.29.cloned.1.call-done.refs_1_.refs_5_.refs_7_.refs_9_.refs_11_, f32[1024,1024]{1,0:T(8,128)} %get-tuple-element.165.refs_2_), custom_call_target="tpu_custom_call" | custom-call | flops 2147483648 | tf_op jit(solution)/shard_map/pallas_call | solution.py:87
  387.7 24.7 %shard_map.56 = f32[1024,2048]{1,0:T(8,128)} custom-call(bf16[1024,1024]{1,0:T(8,128)(2,1)} %shard_map.52.refs_0_, bf16[1024,2048]{1,0:T(8,128)(2,1)} %all-gather.11.cloned.1.call-done.right.refs_1_, bf16[1024,1024]{1,0:T(8,128)(2,1)} %shard_map.53.refs_2_, bf16[1024,2048]{1,0:T(8,128)(2,1)} %all-gather.15.cloned.1.call-done.right.refs_3_, ...), custom_call_target="tpu_custom_call" | custom-call | flops 17179869184 | tf_op jit(solution)/shard_map/pallas_call | solution.py:87
  (234 shorter events, 207.5 us)
Async XLA Ops:
  6.5 32.3 %all-gather.11.cloned.1.call-start = ((), (), s32[]{:S(2)}) async-start(), calls=%async_computation | async-start | bytes 6291456 | tf_op jit(solution)/shard_map/all_gather | solution.py:256
  14.1 41.2 %all-gather.15.cloned.1.call-start = ((), (), s32[]{:S(2)}) async-start(), calls=%async_computation.2 | async-start | bytes 6291456 | tf_op jit(solution)/shard_map/all_gather | solution.py:256
  14.8 100.4 %all-gather.13.cloned.1.call-start = ((), (), s32[]{:S(2)}) async-start(), calls=%async_computation.1 | async-start | bytes 6291456 | tf_op jit(solution)/shard_map/all_gather | solution.py:256
  15.7 48.7 %collective-permute-start.3 = (bf16[512,2048]{1,0:T(8,128)(2,1)S(1)}, bf16[512,2048]{1,0:T(8,128)(2,1)}, u32[]{:S(2)}, u32[]{:S(2)}) collective-permute-start(bf16[512,2048]{1,0:T(8,128)(2,1)S(1)} %copy-done.3), channel_id=1, source_target_pairs={{0,8},{4,12},{8,0},{12,4},{1,9},{5,13},{9,1},{13,5},{2,10},{6,14},... | collective-permute-start | bytes 6291464 | tf_op jit(solution)/shard_map/ppermute | solution.py:252
  32.4 22.9 %collective-permute-start.4 = (bf16[1024,256]{1,0:T(8,128)(2,1)}, bf16[1024,256]{1,0:T(8,128)(2,1)S(1)}, u32[]{:S(2)}, u32[]{:S(2)}) collective-permute-start(bf16[1024,256]{1,0:T(8,128)(2,1)} %get-tuple-element.92.refs_5_), channel_id=1, source_target_pairs={{0,1},{1,0},{2,3},{3,2},{4,5},{5,4},{6,7},{7,6},{8,9},{9,8},{10,11... | collective-permute-start | bytes 1572872 | tf_op jit(solution)/shard_map/ppermute | solution.py:264
  71.1 110.0 %all-gather.17.cloned.1.call-start = ((), (), s32[]{:S(2)}) async-start(), calls=%async_computation.3 | async-start | bytes 6291456 | tf_op jit(solution)/shard_map/all_gather | solution.py:256
  75.3 48.6 %collective-permute-start.11 = (bf16[512,2048]{1,0:T(8,128)(2,1)S(1)}, bf16[512,2048]{1,0:T(8,128)(2,1)}, u32[]{:S(2)}, u32[]{:S(2)}) collective-permute-start(bf16[512,2048]{1,0:T(8,128)(2,1)S(1)} %copy-done.4), channel_id=1, source_target_pairs={{0,8},{4,12},{8,0},{12,4},{1,9},{5,13},{9,1},{13,5},{2,10},{6,14},... | collective-permute-start | bytes 6291464 | tf_op jit(solution)/shard_map/ppermute | solution.py:252
  128.8 110.8 %all-gather.19.cloned.1.call-start = ((), (), s32[]{:S(2)}) async-start(), calls=%async_computation.4 | async-start | bytes 6291456 | tf_op jit(solution)/shard_map/all_gather | solution.py:256
  135.1 25.7 %collective-permute-start.14 = (bf16[1024,256]{1,0:T(8,128)(2,1)}, bf16[1024,256]{1,0:T(8,128)(2,1)}, u32[]{:S(2)}, u32[]{:S(2)}) collective-permute-start(bf16[1024,256]{1,0:T(8,128)(2,1)} %get-tuple-element.110), channel_id=1, source_target_pairs={{1,2},{2,1},{5,6},{6,5},{9,10},{10,9},{13,14},{14,13},{17,18},{18,... | collective-permute-start | bytes 1572872 | tf_op jit(solution)/shard_map/ppermute | solution.py:264
  136.6 24.2 %collective-permute-start.15 = (bf16[1024,256]{1,0:T(8,128)(2,1)S(1)}, bf16[1024,256]{1,0:T(8,128)(2,1)}, u32[]{:S(2)}, u32[]{:S(2)}) collective-permute-start(bf16[1024,256]{1,0:T(8,128)(2,1)S(1)} %copy-done.15), channel_id=1, source_target_pairs={{0,1},{1,0},{2,3},{3,2},{4,5},{5,4},{6,7},{7,6},{8,9},{9,8},{10,11... | collective-permute-start | bytes 1572872 | tf_op jit(solution)/shard_map/ppermute | solution.py:264
  154.6 41.2 %collective-permute-start.26 = (bf16[1024,1024]{1,0:T(8,128)(2,1)S(1)}, bf16[1024,1024]{1,0:T(8,128)(2,1)}, u32[]{:S(2)}, u32[]{:S(2)}) collective-permute-start(bf16[1024,1024]{1,0:T(8,128)(2,1)S(1)} %pad_maximum_fusion.refs_0_.refs_4_.refs_6_), channel_id=1, source_target_pairs={{0,8},{4,12},{8,0},{12,4},{1,9},{5,13},{9,1},{13,5},{2,10},{6,14},... | collective-permute-start | bytes 6291464 | tf_op jit(solution)/shard_map/ppermute | solution.py:252
  156.0 83.7 %all-gather.21.cloned.1.call-start = ((), (), s32[]{:S(2)}) async-start(), calls=%async_computation.5 | async-start | bytes 6291456 | tf_op jit(solution)/shard_map/all_gather | solution.py:256
  165.1 24.6 %collective-permute-start.18 = (bf16[1024,256]{1,0:T(8,128)(2,1)}, bf16[1024,256]{1,0:T(8,128)(2,1)}, u32[]{:S(2)}, u32[]{:S(2)}) collective-permute-start(bf16[1024,256]{1,0:T(8,128)(2,1)} %get-tuple-element.116), channel_id=1, source_target_pairs={{1,2},{2,1},{5,6},{6,5},{9,10},{10,9},{13,14},{14,13},{17,18},{18,... | collective-permute-start | bytes 1572872 | tf_op jit(solution)/shard_map/ppermute | solution.py:264
  166.6 23.1 %collective-permute-start.19 = (bf16[1024,256]{1,0:T(8,128)(2,1)}, bf16[1024,256]{1,0:T(8,128)(2,1)S(1)}, u32[]{:S(2)}, u32[]{:S(2)}) collective-permute-start(bf16[1024,256]{1,0:T(8,128)(2,1)} %get-tuple-element.117.refs_6_.refs_4_), channel_id=1, source_target_pairs={{0,1},{1,0},{2,3},{3,2},{4,5},{5,4},{6,7},{7,6},{8,9},{9,8},{10,11... | collective-permute-start | bytes 1572872 | tf_op jit(solution)/shard_map/ppermute | solution.py:264
  202.8 104.8 %all-gather.23.cloned.1.call-start = ((), (), s32[]{:S(2)}) async-start(), calls=%async_computation.6 | async-start | bytes 6291456 | tf_op jit(solution)/shard_map/all_gather | solution.py:256
  206.7 58.2 %collective-permute-start.35 = (bf16[1024,1024]{1,0:T(8,128)(2,1)S(1)}, bf16[1024,1024]{1,0:T(8,128)(2,1)}, u32[]{:S(2)}, u32[]{:S(2)}) collective-permute-start(bf16[1024,1024]{1,0:T(8,128)(2,1)S(1)} %copy-done.2), channel_id=1, source_target_pairs={{0,8},{4,12},{8,0},{12,4},{1,9},{5,13},{9,1},{13,5},{2,10},{6,14},... | collective-permute-start | bytes 6291464 | tf_op jit(solution)/shard_map/ppermute | solution.py:252
  221.0 28.3 %collective-permute-start.27 = (bf16[1024,256]{1,0:T(8,128)(2,1)}, bf16[1024,256]{1,0:T(8,128)(2,1)}, u32[]{:S(2)}, u32[]{:S(2)}) collective-permute-start(bf16[1024,256]{1,0:T(8,128)(2,1)} %get-tuple-element.132), channel_id=1, source_target_pairs={{1,2},{2,1},{5,6},{6,5},{9,10},{10,9},{13,14},{14,13},{17,18},{18,... | collective-permute-start | bytes 1572872 | tf_op jit(solution)/shard_map/ppermute | solution.py:264
  222.5 26.9 %collective-permute-start.28 = (bf16[1024,256]{1,0:T(8,128)(2,1)}, bf16[1024,256]{1,0:T(8,128)(2,1)}, u32[]{:S(2)}, u32[]{:S(2)}) collective-permute-start(bf16[1024,256]{1,0:T(8,128)(2,1)} %get-tuple-element.133.refs_5_.refs_0_), channel_id=1, source_target_pairs={{0,1},{1,0},{2,3},{3,2},{4,5},{5,4},{6,7},{7,6},{8,9},{9,8},{10,11... | collective-permute-start | bytes 1572872 | tf_op jit(solution)/shard_map/ppermute | solution.py:264
  232.4 32.6 %collective-permute-start.33 = (bf16[1024,256]{1,0:T(8,128)(2,1)}, bf16[1024,256]{1,0:T(8,128)(2,1)S(1)}, u32[]{:S(2)}, u32[]{:S(2)}) collective-permute-start(bf16[1024,256]{1,0:T(8,128)(2,1)} %get-tuple-element.144), channel_id=1, source_target_pairs={{1,2},{2,1},{5,6},{6,5},{9,10},{10,9},{13,14},{14,13},{17,18},{18,... | collective-permute-start | bytes 1572872 | tf_op jit(solution)/shard_map/ppermute | solution.py:264
  233.0 31.9 %collective-permute-start.34 = (bf16[1024,256]{1,0:T(8,128)(2,1)}, bf16[1024,256]{1,0:T(8,128)(2,1)S(1)}, u32[]{:S(2)}, u32[]{:S(2)}) collective-permute-start(bf16[1024,256]{1,0:T(8,128)(2,1)} %get-tuple-element.145.refs_5_.refs_0_), channel_id=1, source_target_pairs={{0,1},{1,0},{2,3},{3,2},{4,5},{5,4},{6,7},{7,6},{8,9},{9,8},{10,11... | collective-permute-start | bytes 1572872 | tf_op jit(solution)/shard_map/ppermute | solution.py:264
  271.8 50.9 %all-gather.27.cloned.1.call-start = ((), (), s32[]{:S(2)}) async-start(), calls=%async_computation.8 | async-start | bytes 6291456 | tf_op jit(solution)/shard_map/all_gather | solution.py:256
  272.6 56.4 %all-gather.25.cloned.1.call-start = ((), (), s32[]{:S(2)}) async-start(), calls=%async_computation.7 | async-start | bytes 6291456 | tf_op jit(solution)/shard_map/all_gather | solution.py:256
  273.3 87.9 %all-gather.29.cloned.1.call-start = ((), (), s32[]{:S(2)}) async-start(), calls=%async_computation.9 | async-start | bytes 6291456 | tf_op jit(solution)/shard_map/all_gather | solution.py:256
  300.1 41.1 %collective-permute-start.39 = (bf16[1024,256]{1,0:T(8,128)(2,1)}, bf16[1024,256]{1,0:T(8,128)(2,1)S(1)}, u32[]{:S(2)}, u32[]{:S(2)}) collective-permute-start(bf16[1024,256]{1,0:T(8,128)(2,1)} %get-tuple-element.154.refs_1_), channel_id=1, source_target_pairs={{0,1},{1,0},{2,3},{3,2},{4,5},{5,4},{6,7},{7,6},{8,9},{9,8},{10,11... | collective-permute-start | bytes 1572872 | tf_op jit(solution)/shard_map/ppermute | solution.py:264
  (73 other events, 529.9 us)
Sparse Core Ops, SparseCore 0:
  14.2 16.3 all-gather.10
  32.2 14.8 all-gather.14
  71.2 12.9 all-gather.12
  128.9 13.2 all-gather.16
  156.1 13.2 all-gather.18
  202.9 12.8 all-gather.20
  272.0 13.1 all-gather.22
  286.7 14.8 all-gather.26
  303.1 14.8 all-gather.24
  348.5 12.7 all-gather.28

commit v4 on v3

v4 whole, which is shorter than its diff:
```python
import functools
import math

import jax
import jax.numpy as jnp
from jax import lax
from jax.experimental import pallas as pl
from jax.experimental.pallas import tpu as pltpu
from jax.sharding import PartitionSpec as P

HEIGHT = 4096
BREADTH = 8192

coef_a = 3.4445
coef_b = -4.775
coef_c = 2.0315

PIECES = 2
WIDTH = 256
SKEW = 2
TILE = 256
HIGH = 256
VMEM = 60 * 1024 * 1024
SMALL = VMEM
PARTS = 2

NN = (((1,), (0,)), ((), ()))
NT = (((1,), (1,)), ((), ()))


def dots_body(flips, scales, out_scale, height, *refs):
    count = len(flips)
    pairs, adds, out = refs[: 2 * count], refs[2 * count : -1], refs[-1]
    for start in range(0, out.shape[0], height):
        here = pl.ds(start, height)
        total = None
        for k in range(count):
            term = lax.dot_general(
                pairs[2 * k][here, :],
                pairs[2 * k + 1][...],
                NT if flips[k] else NN,
                preferred_element_type=jnp.float32,
            )
            total = term if total is None else total + term
        if scales[0] != 1.0:
            total = scales[0] * total
        for scale, add in zip(scales[1:], adds):
            value = add[here, :].astype(jnp.float32)
            total = total + (value if scale == 1.0 else scale * value)
        if out_scale != 1.0:
            total = out_scale * total
        out[here, :] = total.astype(out.dtype)


def dots(pairs, width, tile, high, dot_scale, adds, out_dtype, out_scale=1.0, stripe=512):
    m = pairs[0][0].shape[0]
    high, once = min(high, m), {}
    if high == m:
        once["pipeline_mode"] = pl.Buffered(1)
    operands, specs, flips = [], [], []
    flops = 0
    for left, column, depth, right, where in pairs:
        operands += [left, right]
        specs.append(
            pl.BlockSpec(
                (high, depth), functools.partial(lambda c, j, i: (i, c), column), **once
            )
        )
        flip = callable(where)
        if flip:
            specs.append(
                pl.BlockSpec(
                    (tile, depth), functools.partial(lambda f, j, i: (f(j), 0), where)
                )
            )
        else:
            specs.append(
                pl.BlockSpec(
                    (depth, tile), functools.partial(lambda b, j, i: (b, j), where)
                )
            )
        flips.append(flip)
        flops += 2 * m * depth * width
    for _, add in adds:
        operands.append(add)
        specs.append(pl.BlockSpec((high, tile), lambda j, i: (i, j)))
    return pl.pallas_call(
        functools.partial(
            dots_body,
            tuple(flips),
            (dot_scale,) + tuple(s for s, _ in adds),
            out_scale,
            min(stripe, high),
        ),
        out_shape=jax.ShapeDtypeStruct((m, width), out_dtype),
        grid=(width // tile, m // high),
        in_specs=specs,
        out_specs=pl.BlockSpec((high, tile), lambda j, i: (i, j)),
        compiler_params=pltpu.CompilerParams(vmem_limit_bytes=VMEM),
        cost_estimate=pl.CostEstimate(
            flops=flops, bytes_accessed=0, transcendentals=0
        ),
    )(*operands)


def gram_body(where, *refs):
    *lefts, right, out = refs
    high = lefts[0].shape[0]
    for k, left in enumerate(lefts):
        out[0, k * high : (k + 1) * high, :] = lax.dot_general(
            left[...], right[...], NT, preferred_element_type=jnp.float32
        ).astype(out.dtype)


def gram(lefts, right, where, count, width):
    high, n = lefts[0].shape
    m = high * len(lefts)
    return pl.pallas_call(
        gram_body,
        out_shape=jax.ShapeDtypeStruct((count, m, width), jnp.bfloat16),
        grid_spec=pltpu.PrefetchScalarGridSpec(
            num_scalar_prefetch=1,
            grid=(count,),
            in_specs=[
                pl.BlockSpec(
                    (high, n), lambda j, where: (0, 0), pipeline_mode=pl.Buffered(1)
                )
            ]
            * len(lefts)
            + [pl.BlockSpec((width, n), lambda j, where: (where[0] + j, 0))],
            out_specs=pl.BlockSpec((1, m, width), lambda j, where: (j, 0, 0)),
        ),
        compiler_params=pltpu.CompilerParams(vmem_limit_bytes=VMEM),
        cost_estimate=pl.CostEstimate(
            flops=2 * m * n * width * count, bytes_accessed=0, transcendentals=0
        ),
    )(where, *lefts, right)


def mix_body(plan, count, idle, where, *refs):
    ins, outs = refs[:count], refs[count + idle :]
    for k, sums in plan:

        @pl.when(where[0] == k)
        def _():
            for out, slots in zip(outs, sums):
                total = None
                for slot in slots:
                    value = ins[slot][...].reshape(out.shape)
                    total = value if total is None else total + value
                if total is not None:
                    out[...] = total


def mix(where, sums, held, parts, strip=None):
    sources, uses = [], []
    kinds = sorted(sums[0])
    plan = []
    for k in kinds:
        row = []
        for terms in sums:
            slots = []
            for source in terms[k]:
                if source is None:
                    continue
                for slot, (array, chunk) in enumerate(sources):
                    if array is source[0] and chunk == source[1]:
                        break
                else:
                    slot = len(sources)
                    sources.append(source)
                    uses.append(set())
                uses[slot].add(k)
                slots.append(slot)
            row.append(tuple(slots))
        plan.append((k, tuple(row)))
    m, w = sources[0][0].shape[-2:]
    high = m // parts
    specs = []
    for (array, chunk), used in zip(sources, uses):

        def at(j, where, chunk=chunk, used=tuple(sorted(used))):
            row = j
            if len(used) < len(kinds):
                live = where[0] == used[0]
                for k in used[1:]:
                    live = live | (where[0] == k)
                row = jnp.where(live, j, 0)
            return (row, 0) if chunk is None else (chunk, row, 0)

        specs.append(pl.BlockSpec((high, w) if chunk is None else (1, high, w), at))
    anywhere = pl.BlockSpec(memory_space=pl.ANY)
    shapes = [jax.ShapeDtypeStruct((m, w), jnp.bfloat16)] * len(sums)
    outs = [pl.BlockSpec((high, w), lambda j, where: (j, 0))] * len(sums)
    passed = list(held)
    alias = [len(sums) + k for k in range(len(held))]
    if strip is not None:
        before, width, column = strip
        shapes[-1] = jax.ShapeDtypeStruct((m, width), jnp.bfloat16)
        outs[-1] = pl.BlockSpec((high, w), lambda j, where: (j, column(where)))
        if before is not None:
            passed.append(before)
            alias.append(len(sums) - 1)
    idle, count = len(passed), len(sources)
    return list(
        pl.pallas_call(
            functools.partial(mix_body, tuple(plan), count, idle),
            out_shape=shapes
            + [jax.ShapeDtypeStruct(v.shape, v.dtype) for v in held],
            grid_spec=pltpu.PrefetchScalarGridSpec(
                num_scalar_prefetch=1,
                grid=(parts,),
                in_specs=specs + [anywhere] * idle,
                out_specs=outs + [anywhere] * len(held),
            ),
            input_output_aliases={1 + count + k: a for k, a in enumerate(alias)},
            compiler_params=pltpu.CompilerParams(vmem_limit_bytes=SMALL),
            cost_estimate=pl.CostEstimate(
                flops=10**10, bytes_accessed=0, transcendentals=0
            ),
        )(where, *[a for a, _ in sources], *passed)
    )


def gate_body(*refs):
    pass


def gate(values, others=()):
    anywhere = pl.BlockSpec(memory_space=pl.ANY)
    return list(
        pl.pallas_call(
            gate_body,
            out_shape=[jax.ShapeDtypeStruct(v.shape, v.dtype) for v in values],
            in_specs=[anywhere] * (len(values) + len(others)),
            out_specs=[anywhere] * len(values),
            input_output_aliases={k: k for k in range(len(values))},
            compiler_params=pltpu.CompilerParams(vmem_limit_bytes=VMEM),
            cost_estimate=pl.CostEstimate(flops=0, bytes_accessed=0, transcendentals=0),
        )(*values, *others)
    )


def solution(mesh):
    rows = mesh.shape["rows"]
    cols = mesh.shape["cols"]
    chips = rows // 2

    def swap(value, mask):
        return lax.ppermute(value, "rows", [(i, i ^ mask) for i in range(rows)])

    def side(value):
        pairs = [[2 * i, 2 * i + 1] for i in range(chips)]
        return lax.all_gather(
            value, "rows", axis=0, tiled=True, axis_index_groups=pairs
        )

    def trade(value, start):
        pairs = []
        for i in range(start, cols - 1, 2):
            pairs += [(i, i + 1), (i + 1, i)]
        return lax.ppermute(value, "cols", pairs)

    def on_device(iterate):
        m, n = iterate.shape
        mp = m // PIECES
        w = min(WIDTH, mp)
        q = 2 * mp // w
        z = lax.axis_index("cols")
        core = lax.axis_index("rows") % 2
        even = jnp.where(z % 2 == 0, z, cols - 1 - z)
        where = jnp.stack([even, core]).astype(jnp.int32)
        evens = range(0, cols - 1, 2)
        x0 = [
            iterate[p * mp : (p + 1) * mp].astype(jnp.bfloat16) for p in range(PIECES)
        ]

        groups = [(d, p) for d in range(chips) for p in range(PIECES)]
        order = [(g, i) for g in groups for i in range(q)]
        count = len(order)
        lag = SKEW * (cols - 2)
        steps = count + lag
        ready = {
            g: order.index((g, q - 1)) + lag + SKEW for g in groups
        }

        held = {}
        passing = {s: [] for s in range(steps + 1)}
        follow = {s: [] for s in range(steps + 1)}

        def hold(key, value, s):
            held[key] = value
            if 0 <= s < steps:
                passing[s].append(key)

        def then(s, action):
            if 0 <= s < steps:
                follow[s].append(action)
            else:
                late.append(action)

        late = []
        blocks = {}

        crossed = []

        def behind(value):
            return gate([value], crossed[-1:])[0] if crossed else value

        def cross(key):
            d, p = key
            need = order.index((key, 0))
            crossed.append(swap(behind(held.pop(("x0", key))), 2 * d))
            hold(("b", key), side(crossed[-1]), need - 2)
            then(need - 2, functools.partial(settle, key))

        def settle(key):
            blocks[key] = held.pop(("b", key))

        for g in groups:
            d, p = g
            piece = x0[p]
            if d == 0:
                blocks[g] = side(piece)
                continue
            i = (d - 1) * PIECES + p
            begin = i * q - 1
            hold(("x0", g), piece, begin)
            if begin < 0:
                cross(g)
            else:
                then(begin, functools.partial(cross, g))

        own, sent, got_e, got_o = [], {}, {}, {}
        strip, chip, far = {}, {}, {}

        def at(values, j):
            if isinstance(values, dict):
                return (values[j], None) if j in values else None
            return values[j] if 0 <= j < len(values) else None

        def at_row(chunk):
            return jnp.full((1,), chunk, jnp.int32)

        def final(j):
            return {
                k: [at(sent, j + SKEW * k), at(got_e, j + SKEW * (cols - 2 - k))]
                for k in evens
            }

        def launch(g, s):
            d0, p = g
            strip[g] = held.pop(("s", g))
            if d0 == 0 and chips == 2:
                strip[g] = behind(strip[g])
            chip[g] = side(strip[g])
            for d in range(1, chips):
                e = d ^ d0
                if e == 0:
                    continue
                crossed.append(swap(strip[g], 2 * d))
                value = side(crossed[-1])
                if s + q + 3 < steps:
                    hold(("f", d, e, p), value, s + q + 3)
                    then(s + q + 3, functools.partial(land, d, e, p))
                else:
                    far[d, e, p] = value

        def land(d, e, p):
            far[d, e, p] = held.pop(("f", d, e, p))

        def target(j):
            (d, p), i = order[j]
            near = q // 2
            if d:
                column = lambda where: i
            elif i < near:
                column = lambda where: where[1] * near + i
            else:
                column = lambda where: (1 - where[1]) * near + i - near
            return held.get(("s", (d, p))), 2 * mp, column

        poly, others = {}, {}

        def turned(p):
            return lambda j: j * PIECES + p

        def poly_first(p):
            poly[p] = dots(
                [
                    (strip[0, r], 0, 2 * mp, chip[0, r], turned(p))
                    for r in range(PIECES)
                ],
                2 * mp,
                mp,
                HIGH,
                coef_c,
                [(coef_b, strip[0, p])],
                jnp.float32,
            )

        def poly_next(r, p):
            poly[p] = dots(
                [
                    (strip[d, r], 0, 2 * mp, chip[d, r], turned(p))
                    for d in range(1, chips)
                ],
                2 * mp,
                mp,
                HIGH,
                coef_c,
                [(1.0, poly[p])],
                jnp.bfloat16 if r == PIECES - 1 else jnp.float32,
            )

        def others_next(r, e, p):
            pairs = [
                (strip[d, r], c, mp, far[d, e, p], c * PIECES + r)
                for d in range(1, chips)
                for c in range(2)
            ]
            adds = [] if r == 0 else [(1.0, others[e, p])]
            if r == p:
                pairs += [
                    (strip[0, t], c, mp, chip[e, p], c * PIECES + t)
                    for t in range(PIECES)
                    for c in range(2)
                ]
                adds += [(coef_b, strip[e, p])]
            others[e, p] = dots(
                pairs,
                2 * mp,
                mp,
                HIGH,
                coef_c,
                adds,
                jnp.bfloat16 if r == PIECES - 1 else jnp.float32,
            )

        def early(p, s):
            poly_first(p)
            if s + 1 < steps:
                held["poly", p] = poly[p]
                passing[s + 1].append(("poly", p))
                follow[s + 1].insert(0, functools.partial(regain, p))

        def regain(p):
            poly[p] = held.pop(("poly", p))

        first_at = ready[0, PIECES - 1] + 2
        for p in range(PIECES):
            then(first_at + p, functools.partial(early, p, first_at + p))

        token = jnp.zeros((8, 128), jnp.float32)
        for s in range(steps):
            if s < count:
                g, i = order[s]
                d, p = g
                near = q // 2
                made = None
                if d == 0 and i == 0:
                    made = gram(x0, x0[p], at_row(0), near, w)
                elif d == 0 and i == near:
                    made = gram(x0, blocks[g], at_row((1 - core) * near), near, w)
                elif d > 0 and i == 0:
                    made = gram(x0, blocks[g], at_row(0), q, w)
                if made is not None:
                    own += [(made, c) for c in range(made.shape[0])]
            last_e, last_o = at(got_e, s - SKEW), at(got_o, s - SKEW)
            sums = [
                {
                    k: [at(own, s - SKEW * k)] + ([last_o] if k else [])
                    for k in evens
                }
            ]
            if SKEW <= s < count + SKEW * (cols - 3):
                sums.append(
                    {
                        k: [at(own, s - SKEW * (cols - 1 - k)), last_e] if k else []
                        for k in evens
                    }
                )
            sends = len(sums)
            j = s - lag - SKEW
            if j >= 0:
                sums.append(final(j))
            keys = passing[s]
            out = mix(
                where,
                sums,
                [held[k] for k in keys] + [token],
                PARTS,
                target(j) if j >= 0 else None,
            )
            if j >= 0:
                held["s", order[j][0]] = out[sends]
            token = out[-1]
            sent[s] = out[0]
            got_e[s] = trade(out[0], 0)
            if sends > 1:
                got_o[s] = trade(out[1], 1)
            for k, v in zip(keys, out[len(sums) : -1]):
                held[k] = v
            for g in groups:
                if ready[g] == s:
                    launch(g, s)
            for action in follow[s]:
                action()
        for action in late:
            action()

        def finish():
            for g in groups:
                if g in strip:
                    continue
                for i in range(q):
                    j = order.index((g, i))
                    if j + lag + SKEW >= steps:
                        out = mix(where, [final(j)], [], PARTS, target(j))
                        held["s", g] = out[0]
                launch(g, steps)

        far_chips = range(1, chips)
        if all((d, 0) in strip for d in far_chips):
            for p in range(PIECES):
                poly_next(0, p)
            for e in far_chips:
                others_next(0, e, 0)
            values = [poly[p] for p in range(PIECES)] + [others[e, 0] for e in far_chips]
            out = gate(values + [got_e[steps - 1], token])
            got_e[steps - 1], token = out[-2:]
            for p in range(PIECES):
                poly[p] = out[p]
            for e in far_chips:
                others[e, 0] = out[PIECES - 1 + e]
            finish()
            skip = 1
        else:
            finish()
            skip = 0
        for r in range(PIECES):
            for e in far_chips:
                for p in range(PIECES):
                    if p != r:
                        others_next(r, e, p)
            if r == 0 and skip:
                continue
            for p in range(PIECES):
                poly_next(r, p)
            for e in far_chips:
                others_next(r, e, r)

        factor = 0.2 * math.sqrt(max(HEIGHT, BREADTH))
        return dots(
            [
                (poly[p] if e == 0 else others[e, p], 0, 2 * mp, blocks[e, p], 0)
                for e in range(chips)
                for p in range(PIECES)
            ],
            n,
            TILE,
            m,
            1.0,
            [(coef_a, iterate)],
            jnp.float32,
            factor,
        )

    return jax.shard_map(
        on_device,
        mesh=mesh,
        in_specs=(P(("groups", "rows"), "cols"),),
        out_specs=P(("groups", "rows"), "cols"),
        check_vma=False,
    )
```

time: 423 us -> 472 us (1.12)
  waiting for transfers between devices: 50.9 us -> 101 us
  other arithmetic: 12.1 us -> 4.67 us
  Pallas kernels: 239 us -> 246 us
    ppermute x4, waiting for transfers between devices: 4.68 us -> 80.1 us  [swap(): return lax.ppermute(value, 'rows', [(i, i ^ mask) for i in range(rows)])]
    pallas_call x11, Pallas kernels: 111 us -> 133 us  [dots(): pl.pallas_call(functools.partial(dots_body, tuple(flips), (dot_scale,) +...]
    ppermute x36, waiting for transfers between devices: 38.1 us -> 19 us  [trade(): return lax.ppermute(value, 'cols', pairs)]
    pallas_call x22, Pallas kernels: 85.1 us -> 70.8 us  [mix(): pl.pallas_call(functools.partial(mix_body, tuple(plan), count, idle), out...]
    all_gather x10, waiting for transfers between devices: 5.95 us -> 0.11 us  [side(): lax.all_gather(value, 'rows', axis=0, tiled=True, axis_index_groups=pairs)]
    unnamed x97 -> x81, local copies, waits for them, and re-layouts: 22.6 us -> 21 us
  transfers between devices with their start and end apart: 50 -> 50, of which waited for: 12 -> 10; matrix products, arithmetic and copies ran while one was open for 3% -> 1% of each run, Pallas kernels for 41% -> 39%
where the time goes in v4:
time: 472 us; the launch traced here: 470 us
  Pallas kernels  246 us (52%)
  waiting for transfers between devices  101 us (21%)
  starting transfers between devices  80.1 us (17%)
  local copies, waits for them, and re-layouts  23.9 us (5%)
  between operations  14 us (3%)
    pallas_call x11, Pallas kernels, dots(): pl.pallas_call(functools.partial(dots_body, tuple(flips), (dot_scale,) +...  133 us
    ppermute x4, waiting for transfers between devices, swap(): return lax.ppermute(value, 'rows', [(i, i ^ mask) for i in range(rows)])  80.1 us
    ppermute x36, starting transfers between devices, trade(): return lax.ppermute(value, 'cols', pairs)  73 us
    pallas_call x22, Pallas kernels, mix(): pl.pallas_call(functools.partial(mix_body, tuple(plan), count, idle), out...  70.8 us
    pallas_call x6, Pallas kernels, gram(): pl.pallas_call(gram_body, out_shape=jax.ShapeDtypeStruct((count, m, width...  42 us
    unnamed x81, local copies, waits for them, and re-layouts  21 us
    ppermute x36, waiting for transfers between devices, trade(): return lax.ppermute(value, 'cols', pairs)  19 us
  transfers between devices with their start and end apart: 50, of which 10 were waited for; matrix products, arithmetic and copies ran while one was open for 1% of the time, Pallas kernels for 39%

profile of v4, /device:TPU:0, one launch (start us, length us, event | category | flops | bytes accessed | tf_op | source)
XLA Modules:
  0.0 469.5 jit_solution(17882020019703497539)
XLA Ops:
  18.1 6.1 %shard_map.18.refs_0_.refs_1_ = bf16[2,1024,256]{2,1,0:T(8,128)(2,1)} custom-call(s32[1]{0:T(128)} %constant.30.clone.1.where, bf16[512,2048]{1,0:T(8,128)(2,1)} %get-tuple-element.166.refs_0_.refs_2_, bf16[512,2048]{1,0:T(8,128)(2,1)} %get-tuple-element.165.refs_1_.refs_2_, bf16[512,2048]{1,0:T(8,128)(2,1)} %get-tuple-element.166.refs_0_.refs_2_), custom_call_target="tpu_custom_call" | custom-call | flops 2147483648 | tf_op jit(solution)/shard_map/pallas_call | solution.py:118
  28.8 34.4 %collective-permute-done.6.refs_1_ = bf16[512,2048]{1,0:T(8,128)(2,1)} collective-permute-done((bf16[512,2048]{1,0:T(8,128)(2,1)S(1)}, bf16[512,2048]{1,0:T(8,128)(2,1)}, u32[]{:S(2)}, u32[]{:S(2)}) %collective-permute-start.6) | collective-permute-done | bytes 2097184 | tf_op jit(solution)/shard_map/ppermute | solution.py:250
  69.0 6.3 %shard_map.21.refs_0_.refs_3_ = bf16[2,1024,256]{2,1,0:T(8,128)(2,1)} custom-call(s32[1]{0:T(128)} %bitcast.2.where, bf16[512,2048]{1,0:T(8,128)(2,1)} %get-tuple-element.166.refs_0_.refs_2_, bf16[512,2048]{1,0:T(8,128)(2,1)} %get-tuple-element.165.refs_1_.refs_2_, bf16[1024,2048]{1,0:T(8,128)(2,1)} %all-gather.13.cloned.1.call-done.refs_2_.refs_1_), custom_call_target="tpu_custom_call" | custom-call | flops 2147483648 | tf_op jit(solution)/shard_map/pallas_call | solution.py:118
  89.3 6.2 %shard_map.20.refs_0_.refs_5_.refs_3_ = bf16[2,1024,256]{2,1,0:T(8,128)(2,1)} custom-call(s32[1]{0:T(128)} %constant.30.clone.1.where, bf16[512,2048]{1,0:T(8,128)(2,1)} %get-tuple-element.166.refs_0_.refs_2_, bf16[512,2048]{1,0:T(8,128)(2,1)} %get-tuple-element.165.refs_1_.refs_2_, bf16[512,2048]{1,0:T(8,128)(2,1)} %get-tuple-element.165.refs_1_.refs_2_), custom_call_target="tpu_custom_call" | custom-call | flops 2147483648 | tf_op jit(solution)/shard_map/pallas_call | solution.py:118
  98.6 5.9 %shard_map.17.refs_0_.refs_5_.refs_3_ = bf16[2,1024,256]{2,1,0:T(8,128)(2,1)} custom-call(s32[1]{0:T(128)} %bitcast.2.where, bf16[512,2048]{1,0:T(8,128)(2,1)} %get-tuple-element.166.refs_0_.refs_2_, bf16[512,2048]{1,0:T(8,128)(2,1)} %get-tuple-element.165.refs_1_.refs_2_, bf16[1024,2048]{1,0:T(8,128)(2,1)} %all-gather.11.cloned.1.call-done.refs_2_.refs_3_), custom_call_target="tpu_custom_call" | custom-call | flops 2147483648 | tf_op jit(solution)/shard_map/pallas_call | solution.py:118
  109.6 19.3 %collective-permute-done.15.refs_1_ = bf16[512,2048]{1,0:T(8,128)(2,1)S(1)} collective-permute-done((bf16[512,2048]{1,0:T(8,128)(2,1)}, bf16[512,2048]{1,0:T(8,128)(2,1)S(1)}, u32[]{:S(2)}, u32[]{:S(2)}) %collective-permute-start.15) | collective-permute-done | bytes 2097184 | tf_op jit(solution)/shard_map/ppermute | solution.py:250
  139.9 4.6 collective-permute-start.9
  151.9 4.8 %collective-permute-start.16 = (bf16[1024,256]{1,0:T(8,128)(2,1)}, bf16[1024,256]{1,0:T(8,128)(2,1)S(1)}, u32[]{:S(2)}, u32[]{:S(2)}) collective-permute-start(bf16[1024,256]{1,0:T(8,128)(2,1)} %get-tuple-element.111.refs_6_.refs_1_), channel_id=1, source_target_pairs={{0,1},{1,0},{2,3},{3,2},{4,5},{5,4},{6,7},{7,6},{8,9},{9,8},{10,11... | collective-permute-start | bytes 1572872 | tf_op jit(solution)/shard_map/ppermute | solution.py:262
  157.4 8.7 %shard_map.28.refs_0_.refs_5_.refs_3_ = bf16[4,1024,256]{2,1,0:T(8,128)(2,1)} custom-call(s32[1]{0:T(128)} %constant.30.clone.1.where, bf16[512,2048]{1,0:T(8,128)(2,1)} %get-tuple-element.166.refs_0_.refs_2_, bf16[512,2048]{1,0:T(8,128)(2,1)} %get-tuple-element.165.refs_1_.refs_2_, bf16[1024,2048]{1,0:T(8,128)(2,1)} %get-tuple-element.99.refs_2_.refs_5_), custom_call_target="tpu_custom_call" | custom-call | flops 4294967296 | tf_op jit(solution)/shard_map/pallas_call | solution.py:118
  207.7 8.7 %shard_map.34.refs_0_.refs_5_.refs_2_.refs_4_ = bf16[4,1024,256]{2,1,0:T(8,128)(2,1)} custom-call(s32[1]{0:T(128)} %constant.30.clone.1.where, bf16[512,2048]{1,0:T(8,128)(2,1)} %get-tuple-element.166.refs_0_.refs_2_, bf16[512,2048]{1,0:T(8,128)(2,1)} %get-tuple-element.165.refs_1_.refs_2_, bf16[1024,2048]{1,0:T(8,128)(2,1)} %get-tuple-element.116.refs_2_.refs_7_), custom_call_target="tpu_custom_call" | custom-call | flops 4294967296 | tf_op jit(solution)/shard_map/pallas_call | solution.py:118
  232.2 6.5 %collective-permute-done.26.refs_2_.refs_5_ = bf16[1024,256]{1,0:T(8,128)(2,1)S(1)} collective-permute-done((bf16[1024,256]{1,0:T(8,128)(2,1)S(1)}, bf16[1024,256]{1,0:T(8,128)(2,1)S(1)}, u32[]{:S(2)}, u32[]{:S(2)}) %collective-permute-start.26) | collective-permute-done | bytes 524320 | tf_op jit(solution)/shard_map/ppermute | solution.py:262
  259.1 11.9 %shard_map.43.refs_8_ = f32[1024,1024]{1,0:T(8,128)} custom-call(bf16[1024,1024]{1,0:T(8,128)(2,1)} %shard_map.40.refs_0_.refs_4_.refs_6_, bf16[2048,1024]{1,0:T(8,128)(2,1)} %all-gather.19.cloned.1.call-done.refs_1_, bf16[1024,1024]{1,0:T(8,128)(2,1)} %shard_map.41.refs_2_.refs_4_.refs_8_.refs_10_, ...), custom_call_target="tpu_custom_call" | custom-call | flops 4294967296 | tf_op jit(solution)/shard_map/pallas_call | solution.py:87
  275.5 11.8 %shard_map.42.refs_7_ = f32[1024,1024]{1,0:T(8,128)} custom-call(bf16[1024,1024]{1,0:T(8,128)(2,1)} %shard_map.40.refs_0_.refs_4_.refs_6_, bf16[2048,1024]{1,0:T(8,128)(2,1)} %all-gather.19.cloned.1.call-done.refs_1_, bf16[1024,1024]{1,0:T(8,128)(2,1)} %shard_map.41.refs_2_.refs_4_.refs_8_.refs_10_, ...), custom_call_target="tpu_custom_call" | custom-call | flops 4294967296 | tf_op jit(solution)/shard_map/pallas_call | solution.py:87
  298.7 26.5 %collective-permute-done.39 = bf16[1024,1024]{1,0:T(8,128)(2,1)} collective-permute-done((bf16[1024,1024]{1,0:T(8,128)(2,1)S(1)}, bf16[1024,1024]{1,0:T(8,128)(2,1)}, u32[]{:S(2)}, u32[]{:S(2)}) %collective-permute-start.39) | collective-permute-done | bytes 2097184 | tf_op jit(solution)/shard_map/ppermute | solution.py:250
  335.4 4.5 collective-permute-done.33.refs_1_
  349.5 9.7 %shard_map.46.refs_0_ = f32[1024,1024]{1,0:T(8,128)} custom-call(bf16[1024,1024]{1,0:T(8,128)(2,1)} %get-tuple-element.146.refs_0_.refs_2_.refs_12_, bf16[2048,1024]{1,0:T(8,128)(2,1)} %all-gather.25.cloned.1.call-done.refs_1_.refs_5_.refs_7_.refs_9_.refs_11_, f32[1024,1024]{1,0:T(8,128)} %get-tuple-element.147.refs_2_), custom_call_target="tpu_custom_call" | custom-call | flops 2147483648 | tf_op jit(solution)/shard_map/pallas_call | solution.py:87
  359.2 9.7 %shard_map.47.refs_1_ = f32[1024,1024]{1,0:T(8,128)} custom-call(bf16[1024,1024]{1,0:T(8,128)(2,1)} %get-tuple-element.146.refs_0_.refs_2_.refs_12_, bf16[2048,1024]{1,0:T(8,128)(2,1)} %all-gather.25.cloned.1.call-done.refs_1_.refs_5_.refs_7_.refs_9_.refs_11_, f32[1024,1024]{1,0:T(8,128)} %get-tuple-element.148.refs_2_), custom_call_target="tpu_custom_call" | custom-call | flops 2147483648 | tf_op jit(solution)/shard_map/pallas_call | solution.py:87
  368.9 14.4 %shard_map.48.refs_2_ = f32[1024,1024]{1,0:T(8,128)} custom-call(bf16[1024,1024]{1,0:T(8,128)(2,1)} %get-tuple-element.146.refs_0_.refs_2_.refs_12_, bf16[2048,1024]{1,0:T(8,128)(2,1)} %get-tuple-element.149.refs_1_.refs_3_, bf16[1024,1024]{1,0:T(8,128)(2,1)} %get-tuple-element.146.refs_0_.refs_2_.refs_12_, ...), custom_call_target="tpu_custom_call" | custom-call | flops 6442450944 | tf_op jit(solution)/shard_map/pallas_call | solution.py:87
  386.9 8.8 %shard_map.57.refs_12_ = f32[1024,1024]{1,0:T(8,128)} custom-call(bf16[1024,1024]{1,0:T(8,128)(2,1)} %get-tuple-element.146.refs_0_.refs_2_.refs_12_, bf16[2048,1024]{1,0:T(8,128)(2,1)} %all-gather.29.cloned.1.call-done.refs_1_.refs_3_, bf16[1024,1024]{1,0:T(8,128)(2,1)} %get-tuple-element.146.refs_0_.refs_2_.refs_12_, ...), custom_call_target="tpu_custom_call" | custom-call | flops 2147483648 | tf_op jit(solution)/shard_map/pallas_call | solution.py:87
  395.6 9.3 %shard_map.56.refs_4_ = bf16[1024,1024]{1,0:T(8,128)(2,1)} custom-call(bf16[1024,1024]{1,0:T(8,128)(2,1)} %shard_map.53.refs_0_.refs_2_.refs_13_, bf16[2048,1024]{1,0:T(8,128)(2,1)} %get-tuple-element.149.refs_1_.refs_3_, bf16[1024,1024]{1,0:T(8,128)(2,1)} %shard_map.53.refs_0_.refs_2_.refs_13_, bf16[2048,1024]{1,0:T(8,128)(2,1)} %get-tuple-element.149.refs_1_.refs_3_, ...), custom_call_target="tpu_custom_call" | custom-call | flops 2147483648 | tf_op jit(solution)/shard_map/pallas_call | solution.py:87
  404.9 9.2 %shard_map.54.refs_0_ = bf16[1024,1024]{1,0:T(8,128)(2,1)} custom-call(bf16[1024,1024]{1,0:T(8,128)(2,1)} %shard_map.53.refs_0_.refs_2_.refs_13_, bf16[2048,1024]{1,0:T(8,128)(2,1)} %all-gather.27.cloned.1.call-done.refs_1_.refs_5_.refs_7_.refs_9_.refs_11_, f32[1024,1024]{1,0:T(8,128)} %get-tuple-element.162.refs_2_), custom_call_target="tpu_custom_call" | custom-call | flops 2147483648 | tf_op jit(solution)/shard_map/pallas_call | solution.py:87
  414.1 9.2 %shard_map.55.refs_2_ = bf16[1024,1024]{1,0:T(8,128)(2,1)} custom-call(bf16[1024,1024]{1,0:T(8,128)(2,1)} %shard_map.53.refs_0_.refs_2_.refs_13_, bf16[2048,1024]{1,0:T(8,128)(2,1)} %all-gather.27.cloned.1.call-done.refs_1_.refs_5_.refs_7_.refs_9_.refs_11_, f32[1024,1024]{1,0:T(8,128)} %get-tuple-element.163.refs_2_), custom_call_target="tpu_custom_call" | custom-call | flops 2147483648 | tf_op jit(solution)/shard_map/pallas_call | solution.py:87
  423.3 14.6 %shard_map.58.refs_6_ = bf16[1024,1024]{1,0:T(8,128)(2,1)} custom-call(bf16[1024,1024]{1,0:T(8,128)(2,1)} %shard_map.53.refs_0_.refs_2_.refs_13_, bf16[2048,1024]{1,0:T(8,128)(2,1)} %all-gather.29.cloned.1.call-done.refs_1_.refs_3_, bf16[1024,1024]{1,0:T(8,128)(2,1)} %shard_map.53.refs_0_.refs_2_.refs_13_, ...), custom_call_target="tpu_custom_call" | custom-call | flops 6442450944 | tf_op jit(solution)/shard_map/pallas_call | solution.py:87
  437.9 24.8 %shard_map.59 = f32[1024,2048]{1,0:T(8,128)} custom-call(bf16[1024,1024]{1,0:T(8,128)(2,1)} %shard_map.54.refs_0_, bf16[1024,2048]{1,0:T(8,128)(2,1)} %all-gather.13.cloned.1.call-done.refs_2_.refs_1_, bf16[1024,1024]{1,0:T(8,128)(2,1)} %shard_map.55.refs_2_, bf16[1024,2048]{1,0:T(8,128)(2,1)} %all-gather.11.cloned.1.call-done.refs_2_.refs_3_, ...), custom_call_target="tpu_custom_call" | custom-call | flops 17179869184 | tf_op jit(solution)/shard_map/pallas_call | solution.py:87
  (214 shorter events, 179.7 us)
Async XLA Ops:
  6.5 62.4 %all-gather.13.cloned.1.call-start = ((), (), s32[]{:S(2)}) async-start(), calls=%async_computation.1 | async-start | bytes 6291456 | tf_op jit(solution)/shard_map/all_gather | solution.py:254
  12.9 85.7 %all-gather.11.cloned.1.call-start = ((), (), s32[]{:S(2)}) async-start(), calls=%async_computation | async-start | bytes 6291456 | tf_op jit(solution)/shard_map/all_gather | solution.py:254
  13.7 121.7 %all-gather.15.cloned.1.call-start = ((), (), s32[]{:S(2)}) async-start(), calls=%async_computation.2 | async-start | bytes 6291456 | tf_op jit(solution)/shard_map/all_gather | solution.py:254
  14.5 48.7 %collective-permute-start.6 = (bf16[512,2048]{1,0:T(8,128)(2,1)S(1)}, bf16[512,2048]{1,0:T(8,128)(2,1)}, u32[]{:S(2)}, u32[]{:S(2)}) collective-permute-start(bf16[512,2048]{1,0:T(8,128)(2,1)S(1)} %copy-done.3), channel_id=1, source_target_pairs={{0,8},{4,12},{8,0},{12,4},{1,9},{5,13},{9,1},{13,5},{2,10},{6,14},... | collective-permute-start | bytes 6291464 | tf_op jit(solution)/shard_map/ppermute | solution.py:250
  27.2 48.1 %collective-permute-start = (bf16[1024,256]{1,0:T(8,128)(2,1)}, bf16[1024,256]{1,0:T(8,128)(2,1)S(1)}, u32[]{:S(2)}, u32[]{:S(2)}) collective-permute-start(bf16[1024,256]{1,0:T(8,128)(2,1)} %get-tuple-element.85.refs_1_), channel_id=1, source_target_pairs={{0,1},{1,0},{2,3},{3,2},{4,5},{5,4},{6,7},{7,6},{8,9},{9,8},{10,11... | collective-permute-start | bytes 1572872 | tf_op jit(solution)/shard_map/ppermute | solution.py:262
  63.2 123.8 %all-gather.17.cloned.1.call-start = ((), (), s32[]{:S(2)}) async-start(), calls=%async_computation.3 | async-start | bytes 6291456 | tf_op jit(solution)/shard_map/all_gather | solution.py:254
  82.7 46.1 %collective-permute-start.15 = (bf16[512,2048]{1,0:T(8,128)(2,1)}, bf16[512,2048]{1,0:T(8,128)(2,1)S(1)}, u32[]{:S(2)}, u32[]{:S(2)}) collective-permute-start(bf16[512,2048]{1,0:T(8,128)(2,1)} %shard_map.31), channel_id=1, source_target_pairs={{0,8},{4,12},{8,0},{12,4},{1,9},{5,13},{9,1},{13,5},{2,10},{6,14},... | collective-permute-start | bytes 6291464 | tf_op jit(solution)/shard_map/ppermute | solution.py:250
  95.5 34.7 %collective-permute-start.7 = (bf16[1024,256]{1,0:T(8,128)(2,1)}, bf16[1024,256]{1,0:T(8,128)(2,1)}, u32[]{:S(2)}, u32[]{:S(2)}) collective-permute-start(bf16[1024,256]{1,0:T(8,128)(2,1)} %get-tuple-element.95), channel_id=1, source_target_pairs={{1,2},{2,1},{5,6},{6,5},{9,10},{10,9},{13,14},{14,13},{17,18},{18,... | collective-permute-start | bytes 1572872 | tf_op jit(solution)/shard_map/ppermute | solution.py:262
  97.0 33.3 %collective-permute-start.8 = (bf16[1024,256]{1,0:T(8,128)(2,1)S(1)}, bf16[1024,256]{1,0:T(8,128)(2,1)}, u32[]{:S(2)}, u32[]{:S(2)}) collective-permute-start(bf16[1024,256]{1,0:T(8,128)(2,1)S(1)} %copy-done.12), channel_id=1, source_target_pairs={{0,1},{1,0},{2,3},{3,2},{4,5},{5,4},{6,7},{7,6},{8,9},{9,8},{10,11... | collective-permute-start | bytes 1572872 | tf_op jit(solution)/shard_map/ppermute | solution.py:262
  107.5 27.8 %collective-permute-start.4 = (bf16[1024,256]{1,0:T(8,128)(2,1)}, bf16[1024,256]{1,0:T(8,128)(2,1)S(1)}, u32[]{:S(2)}, u32[]{:S(2)}) collective-permute-start(bf16[1024,256]{1,0:T(8,128)(2,1)} %get-tuple-element.93.refs_6_.refs_1_), channel_id=1, source_target_pairs={{0,1},{1,0},{2,3},{3,2},{4,5},{5,4},{6,7},{7,6},{8,9},{9,8},{10,11... | collective-permute-start | bytes 1572872 | tf_op jit(solution)/shard_map/ppermute | solution.py:262
  130.2 128.8 %all-gather.19.cloned.1.call-start = ((), (), s32[]{:S(2)}) async-start(), calls=%async_computation.4 | async-start | bytes 6291456 | tf_op jit(solution)/shard_map/all_gather | solution.py:254
  180.3 78.8 %all-gather.21.cloned.1.call-start = ((), (), s32[]{:S(2)}) async-start(), calls=%async_computation.5 | async-start | bytes 6291456 | tf_op jit(solution)/shard_map/all_gather | solution.py:254
  181.9 43.3 %collective-permute-start.30 = (bf16[1024,1024]{1,0:T(8,128)(2,1)S(1)}, bf16[1024,1024]{1,0:T(8,128)(2,1)}, u32[]{:S(2)}, u32[]{:S(2)}) collective-permute-start(bf16[1024,1024]{1,0:T(8,128)(2,1)S(1)} %copy-done), channel_id=1, source_target_pairs={{0,8},{4,12},{8,0},{12,4},{1,9},{5,13},{9,1},{13,5},{2,10},{6,14},... | collective-permute-start | bytes 6291464 | tf_op jit(solution)/shard_map/ppermute | solution.py:250
  225.2 45.9 %all-gather.23.cloned.1.call-start = ((), (), s32[]{:S(2)}) async-start(), calls=%async_computation.6 | async-start | bytes 6291456 | tf_op jit(solution)/shard_map/all_gather | solution.py:254
  226.0 123.5 %all-gather.25.cloned.1.call-start = ((), (), s32[]{:S(2)}) async-start(), calls=%async_computation.7 | async-start | bytes 6291456 | tf_op jit(solution)/shard_map/all_gather | solution.py:254
  243.1 27.9 %collective-permute-start.31 = (bf16[1024,256]{1,0:T(8,128)(2,1)}, bf16[1024,256]{1,0:T(8,128)(2,1)S(1)}, u32[]{:S(2)}, u32[]{:S(2)}) collective-permute-start(bf16[1024,256]{1,0:T(8,128)(2,1)} %get-tuple-element.140.refs_5_.refs_0_), channel_id=1, source_target_pairs={{0,1},{1,0},{2,3},{3,2},{4,5},{5,4},{6,7},{7,6},{8,9},{9,8},{10,11... | collective-permute-start | bytes 1572872 | tf_op jit(solution)/shard_map/ppermute | solution.py:262
  254.7 32.5 %collective-permute-start.28 = (bf16[1024,256]{1,0:T(8,128)(2,1)}, bf16[1024,256]{1,0:T(8,128)(2,1)S(1)}, u32[]{:S(2)}, u32[]{:S(2)}) collective-permute-start(bf16[1024,256]{1,0:T(8,128)(2,1)} %get-tuple-element.136.refs_5_.refs_0_), channel_id=1, source_target_pairs={{0,1},{1,0},{2,3},{3,2},{4,5},{5,4},{6,7},{7,6},{8,9},{9,8},{10,11... | collective-permute-start | bytes 1572872 | tf_op jit(solution)/shard_map/ppermute | solution.py:262
  258.3 29.0 %collective-permute-start.29 = (bf16[1024,256]{1,0:T(8,128)(2,1)}, bf16[1024,256]{1,0:T(8,128)(2,1)S(1)}, u32[]{:S(2)}, u32[]{:S(2)}) collective-permute-start(bf16[1024,256]{1,0:T(8,128)(2,1)} %get-tuple-element.137), channel_id=1, source_target_pairs={{1,2},{2,1},{5,6},{6,5},{9,10},{10,9},{13,14},{14,13},{17,18},{18,... | collective-permute-start | bytes 1572872 | tf_op jit(solution)/shard_map/ppermute | solution.py:262
  291.8 95.1 %all-gather.29.cloned.1.call-start = ((), (), s32[]{:S(2)}) async-start(), calls=%async_computation.9 | async-start | bytes 6291456 | tf_op jit(solution)/shard_map/all_gather | solution.py:254
  293.4 31.8 %collective-permute-start.39 = (bf16[1024,1024]{1,0:T(8,128)(2,1)S(1)}, bf16[1024,1024]{1,0:T(8,128)(2,1)}, u32[]{:S(2)}, u32[]{:S(2)}) collective-permute-start(bf16[1024,1024]{1,0:T(8,128)(2,1)S(1)} %copy-done.1), channel_id=1, source_target_pairs={{0,8},{4,12},{8,0},{12,4},{1,9},{5,13},{9,1},{13,5},{2,10},{6,14},... | collective-permute-start | bytes 6291464 | tf_op jit(solution)/shard_map/ppermute | solution.py:250
  294.2 34.1 %collective-permute-start.35 = (bf16[1024,256]{1,0:T(8,128)(2,1)S(1)}, bf16[1024,256]{1,0:T(8,128)(2,1)}, u32[]{:S(2)}, u32[]{:S(2)}) collective-permute-start(bf16[1024,256]{1,0:T(8,128)(2,1)S(1)} %copy-done.24), channel_id=1, source_target_pairs={{0,1},{1,0},{2,3},{3,2},{4,5},{5,4},{6,7},{7,6},{8,9},{9,8},{10,11... | collective-permute-start | bytes 1572872 | tf_op jit(solution)/shard_map/ppermute | solution.py:262
  297.3 30.9 %collective-permute-start.36 = (bf16[1024,256]{1,0:T(8,128)(2,1)}, bf16[1024,256]{1,0:T(8,128)(2,1)}, u32[]{:S(2)}, u32[]{:S(2)}) collective-permute-start(bf16[1024,256]{1,0:T(8,128)(2,1)} %get-tuple-element.153), channel_id=1, source_target_pairs={{1,2},{2,1},{5,6},{6,5},{9,10},{10,9},{13,14},{14,13},{17,18},{18,... | collective-permute-start | bytes 1572872 | tf_op jit(solution)/shard_map/ppermute | solution.py:262
  325.2 79.7 %all-gather.27.cloned.1.call-start = ((), (), s32[]{:S(2)}) async-start(), calls=%async_computation.8 | async-start | bytes 6291456 | tf_op jit(solution)/shard_map/all_gather | solution.py:254
  344.0 39.3 %collective-permute-start.37 = (bf16[1024,256]{1,0:T(8,128)(2,1)}, bf16[1024,256]{1,0:T(8,128)(2,1)S(1)}, u32[]{:S(2)}, u32[]{:S(2)}) collective-permute-start(bf16[1024,256]{1,0:T(8,128)(2,1)} %get-tuple-element.157.refs_2_), channel_id=1, source_target_pairs={{0,1},{1,0},{2,3},{3,2},{4,5},{5,4},{6,7},{7,6},{8,9},{9,8},{10,11... | collective-permute-start | bytes 1572872 | tf_op jit(solution)/shard_map/ppermute | solution.py:262
  (66 other events, 568.2 us)
Sparse Core Ops, SparseCore 0:
  13.1 16.3 all-gather.12
  31.0 14.8 all-gather.10
  63.3 15.1 all-gather.14
  130.3 14.5 all-gather.16
  180.4 13.5 all-gather.18
  225.3 14.1 all-gather.20
  241.0 14.8 all-gather.22
  291.9 13.6 all-gather.24
  325.3 14.8 all-gather.28
  387.0 13.8 all-gather.26

commit v5 on v4

--- a/solution.py
+++ b/solution.py
@@ -19,7 +19,7 @@
 WIDTH = 256
 SKEW = 2
 TILE = 256
-HIGH = 256
+GAP = 4
 VMEM = 60 * 1024 * 1024
 SMALL = VMEM
 PARTS = 2
@@ -28,8 +28,9 @@
 NT = (((1,), (1,)), ((), ()))
 
 
-def dots_body(flips, scales, out_scale, height, *refs):
+def dots_body(flips, scales, spans, out_scale, height, *refs):
     count = len(flips)
+    tile_at = pl.program_id(0)
     pairs, adds, out = refs[: 2 * count], refs[2 * count : -1], refs[-1]
     for start in range(0, out.shape[0], height):
         here = pl.ds(start, height)
@@ -44,8 +45,12 @@
             total = term if total is None else total + term
         if scales[0] != 1.0:
             total = scales[0] * total
-        for scale, add in zip(scales[1:], adds):
-            value = add[here, :].astype(jnp.float32)
+        left = list(adds)
+        for scale, (number, span) in zip(scales[1:], spans):
+            value = left.pop(0)[here, :]
+            for k in range(1, number):
+                value = jnp.where(tile_at < k * span, value, left.pop(0)[here, :])
+            value = value.astype(jnp.float32)
             total = total + (value if scale == 1.0 else scale * value)
         if out_scale != 1.0:
             total = out_scale * total
@@ -81,14 +86,26 @@
             )
         flips.append(flip)
         flops += 2 * m * depth * width
-    for _, add in adds:
-        operands.append(add)
-        specs.append(pl.BlockSpec((high, tile), lambda j, i: (i, j)))
+    spans = []
+    for _, joined in adds:
+        span = joined[0].shape[1] // tile
+        spans.append((len(joined), span))
+        for k, add in enumerate(joined):
+            operands.append(add)
+            specs.append(
+                pl.BlockSpec(
+                    (high, tile),
+                    functools.partial(
+                        lambda f, t, j, i: (i, jnp.clip(j - f, 0, t - 1)), k * span, span
+                    ),
+                )
+            )
     return pl.pallas_call(
         functools.partial(
             dots_body,
             tuple(flips),
             (dot_scale,) + tuple(s for s, _ in adds),
+            tuple(spans),
             out_scale,
             min(stripe, high),
         ),
@@ -216,28 +233,9 @@
             input_output_aliases={1 + count + k: a for k, a in enumerate(alias)},
             compiler_params=pltpu.CompilerParams(vmem_limit_bytes=SMALL),
             cost_estimate=pl.CostEstimate(
-                flops=10**10, bytes_accessed=0, transcendentals=0
+                flops=4 * 10**10, bytes_accessed=0, transcendentals=0
             ),
         )(where, *[a for a, _ in sources], *passed)
-    )
-
-
-def gate_body(*refs):
-    pass
-
-
-def gate(values, others=()):
-    anywhere = pl.BlockSpec(memory_space=pl.ANY)
-    return list(
-        pl.pallas_call(
-            gate_body,
-            out_shape=[jax.ShapeDtypeStruct(v.shape, v.dtype) for v in values],
-            in_specs=[anywhere] * (len(values) + len(others)),
-            out_specs=[anywhere] * len(values),
-            input_output_aliases={k: k for k in range(len(values))},
-            compiler_params=pltpu.CompilerParams(vmem_limit_bytes=VMEM),
-            cost_estimate=pl.CostEstimate(flops=0, bytes_accessed=0, transcendentals=0),
-        )(*values, *others)
     )
 
 
@@ -302,20 +300,14 @@
         late = []
         blocks = {}
 
-        crossed = []
-
-        def behind(value):
-            return gate([value], crossed[-1:])[0] if crossed else value
-
         def cross(key):
             d, p = key
-            need = order.index((key, 0))
-            crossed.append(swap(behind(held.pop(("x0", key))), 2 * d))
-            hold(("b", key), side(crossed[-1]), need - 2)
-            then(need - 2, functools.partial(settle, key))
+            end = ((d - 1) * PIECES + p + 1) * q
+            hold(("x", key), swap(held.pop(("x0", key)), 2 * d), end)
+            then(end, functools.partial(settle, key))
 
         def settle(key):
-            blocks[key] = held.pop(("b", key))
+            blocks[key] = side(held.pop(("x", key)))
 
         for g in groups:
             d, p = g
@@ -351,23 +343,28 @@
         def launch(g, s):
             d0, p = g
             strip[g] = held.pop(("s", g))
-            if d0 == 0 and chips == 2:
-                strip[g] = behind(strip[g])
-            chip[g] = side(strip[g])
+            later(("c", g), side(strip[g]), s + GAP, chip, g)
             for d in range(1, chips):
                 e = d ^ d0
                 if e == 0:
                     continue
-                crossed.append(swap(strip[g], 2 * d))
-                value = side(crossed[-1])
-                if s + q + 3 < steps:
-                    hold(("f", d, e, p), value, s + q + 3)
-                    then(s + q + 3, functools.partial(land, d, e, p))
+                over = swap(strip[g], 2 * d)
+                if s + q < steps:
+                    hold(("f", d, e, p), over, s + q)
+                    then(s + q, functools.partial(land, d, e, p, s + q))
                 else:
-                    far[d, e, p] = value
-
-        def land(d, e, p):
-            far[d, e, p] = held.pop(("f", d, e, p))
+                    far[d, e, p] = side(over)
+
+        def land(d, e, p, s):
+            value = side(held.pop(("f", d, e, p)))
+            later(("g", d, e, p), value, s + GAP, far, (d, e, p))
+
+        def later(key, value, s, table, place):
+            if s >= steps:
+                table[place] = value
+                return
+            hold(key, value, s)
+            then(s, lambda: table.__setitem__(place, held.pop(key)))
 
         def target(j):
             (d, p), i = order[j]
@@ -380,76 +377,31 @@
                 column = lambda where: (1 - where[1]) * near + i - near
             return held.get(("s", (d, p))), 2 * mp, column
 
-        poly, others = {}, {}
-
-        def turned(p):
-            return lambda j: j * PIECES + p
-
-        def poly_first(p):
-            poly[p] = dots(
-                [
-                    (strip[0, r], 0, 2 * mp, chip[0, r], turned(p))
-                    for r in range(PIECES)
-                ],
-                2 * mp,
-                mp,
-                HIGH,
-                coef_c,
-                [(coef_b, strip[0, p])],
-                jnp.float32,
-            )
-
-        def poly_next(r, p):
-            poly[p] = dots(
-                [
-                    (strip[d, r], 0, 2 * mp, chip[d, r], turned(p))
-                    for d in range(1, chips)
-                ],
-                2 * mp,
-                mp,
-                HIGH,
-                coef_c,
-                [(1.0, poly[p])],
-                jnp.bfloat16 if r == PIECES - 1 else jnp.float32,
-            )
-
-        def others_next(r, e, p):
+        def turned(j):
+            per = mp // TILE if mp > TILE else 1
+            return ((j // per) % 2 * PIECES + j // (2 * per)) * per + j % per
+
+        def others(e, p):
             pairs = [
                 (strip[d, r], c, mp, far[d, e, p], c * PIECES + r)
                 for d in range(1, chips)
+                for r in range(PIECES)
                 for c in range(2)
             ]
-            adds = [] if r == 0 else [(1.0, others[e, p])]
-            if r == p:
-                pairs += [
-                    (strip[0, t], c, mp, chip[e, p], c * PIECES + t)
-                    for t in range(PIECES)
-                    for c in range(2)
-                ]
-                adds += [(coef_b, strip[e, p])]
-            others[e, p] = dots(
+            pairs += [
+                (strip[0, r], c, mp, chip[e, p], c * PIECES + r)
+                for r in range(PIECES)
+                for c in range(2)
+            ]
+            return dots(
                 pairs,
                 2 * mp,
-                mp,
-                HIGH,
+                min(TILE, mp),
+                m,
                 coef_c,
-                adds,
-                jnp.bfloat16 if r == PIECES - 1 else jnp.float32,
-            )
-
-        def early(p, s):
-            poly_first(p)
-            if s + 1 < steps:
-                held["poly", p] = poly[p]
-                passing[s + 1].append(("poly", p))
-                follow[s + 1].insert(0, functools.partial(regain, p))
-
-        def regain(p):
-            poly[p] = held.pop(("poly", p))
-
-        first_at = ready[0, PIECES - 1] + 2
-        for p in range(PIECES):
-            then(first_at + p, functools.partial(early, p, first_at + p))
+                [(coef_b, [strip[e, p]])],
+                jnp.bfloat16,
+            )
 
         token = jnp.zeros((8, 128), jnp.float32)
         for s in range(steps):
@@ -503,65 +455,46 @@
                 held[k] = v
             for g in groups:
                 if ready[g] == s:
-                    launch(g, s)
+                    wait = 1 if g[0] == 0 and g[1] and s + 1 < steps else 0
+                    if wait:
+                        passing[s + 1].append(("s", g))
+                        follow[s + 1].append(functools.partial(launch, g, s + 1))
+                    else:
+                        launch(g, s)
             for action in follow[s]:
                 action()
         for action in late:
             action()
 
-        def finish():
-            for g in groups:
-                if g in strip:
-                    continue
-                for i in range(q):
-                    j = order.index((g, i))
-                    if j + lag + SKEW >= steps:
-                        out = mix(where, [final(j)], [], PARTS, target(j))
-                        held["s", g] = out[0]
-                launch(g, steps)
-
-        far_chips = range(1, chips)
-        if all((d, 0) in strip for d in far_chips):
-            for p in range(PIECES):
-                poly_next(0, p)
-            for e in far_chips:
-                others_next(0, e, 0)
-            values = [poly[p] for p in range(PIECES)] + [others[e, 0] for e in far_chips]
-            out = gate(values + [got_e[steps - 1], token])
-            got_e[steps - 1], token = out[-2:]
-            for p in range(PIECES):
-                poly[p] = out[p]
-            for e in far_chips:
-                others[e, 0] = out[PIECES - 1 + e]
-            finish()
-            skip = 1
-        else:
-            finish()
-            skip = 0
-        for r in range(PIECES):
-            for e in far_chips:
-                for p in range(PIECES):
-                    if p != r:
-                        others_next(r, e, p)
-            if r == 0 and skip:
+        for g in groups:
+            if g in strip:
                 continue
-            for p in range(PIECES):
-                poly_next(r, p)
-            for e in far_chips:
-                others_next(r, e, r)
-
+            for i in range(q):
+                j = order.index((g, i))
+                if j + lag + SKEW >= steps:
+                    out = mix(where, [final(j)], [], PARTS, target(j))
+                    held["s", g] = out[0]
+            launch(g, steps)
+
+        poly = {(e, p): others(e, p) for p in range(PIECES) for e in range(1, chips)}
+        first = dots(
+            [(strip[g], 0, 2 * mp, chip[g], turned) for g in groups],
+            2 * m,
+            min(TILE, mp),
+            m,
+            coef_c,
+            [(coef_b, [strip[0, p] for p in range(PIECES)])],
+            jnp.bfloat16,
+        )
         factor = 0.2 * math.sqrt(max(HEIGHT, BREADTH))
         return dots(
-            [
-                (poly[p] if e == 0 else others[e, p], 0, 2 * mp, blocks[e, p], 0)
-                for e in range(chips)
-                for p in range(PIECES)
-            ],
+            [(first, p, 2 * mp, blocks[0, p], 0) for p in range(PIECES)]
+            + [(poly[g], 0, 2 * mp, blocks[g], 0) for g in groups if g[0]],
             n,
             TILE,
             m,
             1.0,
-            [(coef_a, iterate)],
+            [(coef_a, [iterate])],
             jnp.float32,
             factor,
         )

time: 472 us -> 352 us (0.75)
  waiting for transfers between devices: 101 us -> 40.9 us
  Pallas kernels: 246 us -> 194 us
  starting transfers between devices: 80.1 us -> 73 us
    ppermute x4, waiting for transfers between devices: 80.1 us -> 6.88 us  [swap(): return lax.ppermute(value, 'rows', [(i, i ^ mask) for i in range(rows)])]
    pallas_call x11 -> x4, Pallas kernels: 133 us -> 80.1 us  [dots(): pl.pallas_call(functools.partial(dots_body, tuple(flips), (dot_scale,) +...]
    ppermute x36, waiting for transfers between devices: 19 us -> 33.7 us  [trade(): return lax.ppermute(value, 'cols', pairs)]
    ppermute x36, starting transfers between devices: 73 us -> 68.2 us  [trade(): return lax.ppermute(value, 'cols', pairs)]
    unnamed x81 -> x63, local copies, waits for them, and re-layouts: 21 us -> 21.4 us
  transfers between devices with their start and end apart: 50 -> 50, of which waited for: 10 -> 14; matrix products, arithmetic and copies ran while one was open for 1% -> 1% of each run, Pallas kernels for 39% -> 37%
where the time goes in v5:
time: 352 us; the launch traced here: 350 us
  Pallas kernels  194 us (55%)
  starting transfers between devices  73 us (21%)
  waiting for transfers between devices  40.9 us (12%)
  local copies, waits for them, and re-layouts  24.3 us (7%)
  between operations  13.8 us (4%)
  other arithmetic  4.64 us (1%)
    pallas_call x4, Pallas kernels, dots(): pl.pallas_call(functools.partial(dots_body, tuple(flips), (dot_scale,) +...  80.1 us
    pallas_call x22, Pallas kernels, mix(): pl.pallas_call(functools.partial(mix_body, tuple(plan), count, idle), out...  71.2 us
    ppermute x36, starting transfers between devices, trade(): return lax.ppermute(value, 'cols', pairs)  68.2 us
    pallas_call x6, Pallas kernels, gram(): pl.pallas_call(gram_body, out_shape=jax.ShapeDtypeStruct((count, m, width...  42.3 us
    ppermute x36, waiting for transfers between devices, trade(): return lax.ppermute(value, 'cols', pairs)  33.7 us
    unnamed x63, local copies, waits for them, and re-layouts  21.4 us
  transfers between devices with their start and end apart: 50, of which 14 were waited for; matrix products, arithmetic and copies ran while one was open for 1% of the time, Pallas kernels for 37%

profile of v5, /device:TPU:0, one launch (start us, length us, event | category | flops | bytes accessed | tf_op | source)
XLA Modules:
  0.0 350.2 jit_solution(6969027498294363356)
XLA Ops:
  6.5 4.0 %convert.4 = bf16[1024,2048]{1,0:T(8,128)(2,1)S(1)} convert(f32[1024,2048]{1,0:T(8,128)} %refs_8_.1) | non-fusion elementwise | flops 2097152 | bytes 12582912 | tf_op jit(solution)/shard_map/convert.1
  16.6 6.1 %shard_map.18.refs_0_.refs_1_ = bf16[2,1024,256]{2,1,0:T(8,128)(2,1)} custom-call(s32[1]{0:T(128)} %constant.30.clone.1.where, bf16[512,2048]{1,0:T(8,128)(2,1)} %get-tuple-element.162.refs_0_.refs_2_, bf16[512,2048]{1,0:T(8,128)(2,1)} %get-tuple-element.161.refs_1_.refs_2_, bf16[512,2048]{1,0:T(8,128)(2,1)} %get-tuple-element.162.refs_0_.refs_2_), custom_call_target="tpu_custom_call" | custom-call | flops 2147483648 | tf_op jit(solution)/shard_map/pallas_call | solution.py:135
  32.7 6.0 %shard_map.17.refs_0_.refs_5_.refs_3_ = bf16[2,1024,256]{2,1,0:T(8,128)(2,1)} custom-call(s32[1]{0:T(128)} %constant.30.clone.1.where, bf16[512,2048]{1,0:T(8,128)(2,1)} %get-tuple-element.162.refs_0_.refs_2_, bf16[512,2048]{1,0:T(8,128)(2,1)} %get-tuple-element.161.refs_1_.refs_2_, bf16[512,2048]{1,0:T(8,128)(2,1)} %get-tuple-element.161.refs_1_.refs_2_), custom_call_target="tpu_custom_call" | custom-call | flops 2147483648 | tf_op jit(solution)/shard_map/pallas_call | solution.py:135
  38.8 6.7 %shard_map.19.refs_0_.refs_3_ = bf16[2,1024,256]{2,1,0:T(8,128)(2,1)} custom-call(s32[1]{0:T(128)} %bitcast.2.where, bf16[512,2048]{1,0:T(8,128)(2,1)} %get-tuple-element.162.refs_0_.refs_2_, bf16[512,2048]{1,0:T(8,128)(2,1)} %get-tuple-element.161.refs_1_.refs_2_, bf16[1024,2048]{1,0:T(8,128)(2,1)} %all-gather.11.cloned.1.call-done.refs_2_.refs_1_), custom_call_target="tpu_custom_call" | custom-call | flops 2147483648 | tf_op jit(solution)/shard_map/pallas_call | solution.py:135
  49.8 4.5 %collective-permute-start.2 = (bf16[1024,256]{1,0:T(8,128)(2,1)}, bf16[1024,256]{1,0:T(8,128)(2,1)S(1)}, u32[]{:S(2)}, u32[]{:S(2)}) collective-permute-start(bf16[1024,256]{1,0:T(8,128)(2,1)} %get-tuple-element.87.refs_1_), channel_id=1, source_target_pairs={{0,1},{1,0},{2,3},{3,2},{4,5},{5,4},{6,7},{7,6},{8,9},{9,8},{10,11... | collective-permute-start | bytes 1572872 | tf_op jit(solution)/shard_map/ppermute | solution.py:260
  59.8 6.0 %shard_map.26.refs_0_.refs_5_.refs_3_ = bf16[2,1024,256]{2,1,0:T(8,128)(2,1)} custom-call(s32[1]{0:T(128)} %bitcast.2.where, bf16[512,2048]{1,0:T(8,128)(2,1)} %get-tuple-element.162.refs_0_.refs_2_, bf16[512,2048]{1,0:T(8,128)(2,1)} %get-tuple-element.161.refs_1_.refs_2_, bf16[1024,2048]{1,0:T(8,128)(2,1)} %all-gather.15.cloned.1.call-done.refs_2_.refs_3_), custom_call_target="tpu_custom_call" | custom-call | flops 2147483648 | tf_op jit(solution)/shard_map/pallas_call | solution.py:135
  75.0 3.5 %collective-permute-done.6.refs_4_.refs_7_ = bf16[1024,256]{1,0:T(8,128)(2,1)S(1)} collective-permute-done((bf16[1024,256]{1,0:T(8,128)(2,1)}, bf16[1024,256]{1,0:T(8,128)(2,1)S(1)}, u32[]{:S(2)}, u32[]{:S(2)}) %collective-permute-start.6) | collective-permute-done | bytes 524320 | tf_op jit(solution)/shard_map/ppermute | solution.py:260
  85.3 4.4 %collective-permute-done.9.refs_2_.refs_7_ = bf16[1024,256]{1,0:T(8,128)(2,1)S(1)} collective-permute-done((bf16[1024,256]{1,0:T(8,128)(2,1)S(1)}, bf16[1024,256]{1,0:T(8,128)(2,1)S(1)}, u32[]{:S(2)}, u32[]{:S(2)}) %collective-permute-start.9) | collective-permute-done | bytes 524320 | tf_op jit(solution)/shard_map/ppermute | solution.py:260
  97.1 3.8 %collective-permute-done.7.refs_2_.refs_7_ = bf16[1024,256]{1,0:T(8,128)(2,1)S(1)} collective-permute-done((bf16[1024,256]{1,0:T(8,128)(2,1)}, bf16[1024,256]{1,0:T(8,128)(2,1)S(1)}, u32[]{:S(2)}, u32[]{:S(2)}) %collective-permute-start.7) | collective-permute-done | bytes 524320 | tf_op jit(solution)/shard_map/ppermute | solution.py:260
  108.5 8.7 %shard_map.25.refs_0_.refs_5_.refs_3_ = bf16[4,1024,256]{2,1,0:T(8,128)(2,1)} custom-call(s32[1]{0:T(128)} %constant.30.clone.1.where, bf16[512,2048]{1,0:T(8,128)(2,1)} %get-tuple-element.162.refs_0_.refs_2_, bf16[512,2048]{1,0:T(8,128)(2,1)} %get-tuple-element.161.refs_1_.refs_2_, bf16[1024,2048]{1,0:T(8,128)(2,1)} %all-gather.13.cloned.1.call-done.refs_2_.refs_5_), custom_call_target="tpu_custom_call" | custom-call | flops 4294967296 | tf_op jit(solution)/shard_map/pallas_call | solution.py:135
  126.7 3.8 %shard_map.31 = (bf16[1024,256]{1,0:T(8,128)(2,1)}, bf16[1024,256]{1,0:T(8,128)(2,1)}, bf16[1024,1024]{1,0:T(8,128)(2,1)}, f32[8,128]{1,0:T(8,128)}) custom-call(s32[2]{0:T(128)} %pad_add_fusion.where, bf16[4,1024,256]{2,1,0:T(8,128)(2,1)} %shard_map.25.refs_0_.refs_5_.refs_3_, ...), custom_call_target="tpu_custom_call", output_to_operand_aliasing={{3}: (9, {}), {2}: (10, {})} | custom-call | flops 40000000000 | tf_op jit(solution)/shard_map/pallas_call | solution.py:223
  140.0 3.5 %collective-permute-start.23 = (bf16[1024,256]{1,0:T(8,128)(2,1)}, bf16[1024,256]{1,0:T(8,128)(2,1)S(1)}, u32[]{:S(2)}, u32[]{:S(2)}) collective-permute-start(bf16[1024,256]{1,0:T(8,128)(2,1)} %get-tuple-element.122.refs_6_.refs_0_), channel_id=1, source_target_pairs={{0,1},{1,0},{2,3},{3,2},{4,5},{5,4},{6,7},{7,6},{8,9},{9,8},{10,11... | collective-permute-start | bytes 1572872 | tf_op jit(solution)/shard_map/ppermute | solution.py:260
  156.2 8.7 %shard_map.32.refs_0_.refs_5_.refs_2_.refs_4_ = bf16[4,1024,256]{2,1,0:T(8,128)(2,1)} custom-call(s32[1]{0:T(128)} %constant.30.clone.1.where, bf16[512,2048]{1,0:T(8,128)(2,1)} %get-tuple-element.162.refs_0_.refs_2_, bf16[512,2048]{1,0:T(8,128)(2,1)} %get-tuple-element.161.refs_1_.refs_2_, bf16[1024,2048]{1,0:T(8,128)(2,1)} %all-gather.17.cloned.1.call-done.refs_2_.refs_7_), custom_call_target="tpu_custom_call" | custom-call | flops 4294967296 | tf_op jit(solution)/shard_map/pallas_call | solution.py:135
  165.7 3.5 shard_map.35
  173.4 3.7 %collective-permute-done.22.refs_9_ = bf16[1024,1024]{1,0:T(8,128)(2,1)S(1)} collective-permute-done((bf16[1024,1024]{1,0:T(8,128)(2,1)}, bf16[1024,1024]{1,0:T(8,128)(2,1)S(1)}, u32[]{:S(2)}, u32[]{:S(2)}) %collective-permute-start.22) | collective-permute-done | bytes 2097184 | tf_op jit(solution)/shard_map/ppermute | solution.py:248
  187.0 3.8 %shard_map.37 = (bf16[1024,256]{1,0:T(8,128)(2,1)}, bf16[1024,256]{1,0:T(8,128)(2,1)}, bf16[1024,1024]{1,0:T(8,128)(2,1)}, bf16[1024,1024]{1,0:T(8,128)(2,1)}, f32[8,128]{1,0:T(8,128)}) custom-call(s32[2]{0:T(128)} %pad_add_fusion.where, ...), custom_call_target="tpu_custom_call", output_to_operand_aliasing={{3}: (9, {}), {4}: (10, {})} | custom-call | flops 40000000000 | tf_op jit(solution)/shard_map/pallas_call | solution.py:223
  201.2 4.5 %collective-permute-start.34 = (bf16[1024,256]{1,0:T(8,128)(2,1)}, bf16[1024,256]{1,0:T(8,128)(2,1)S(1)}, u32[]{:S(2)}, u32[]{:S(2)}) collective-permute-start(bf16[1024,256]{1,0:T(8,128)(2,1)} %get-tuple-element.144.refs_5_.refs_0_), channel_id=1, source_target_pairs={{0,1},{1,0},{2,3},{3,2},{4,5},{5,4},{6,7},{7,6},{8,9},{9,8},{10,11... | collective-permute-start | bytes 1572872 | tf_op jit(solution)/shard_map/ppermute | solution.py:260
  213.0 3.8 %collective-permute-start.31 = (bf16[1024,256]{1,0:T(8,128)(2,1)}, bf16[1024,256]{1,0:T(8,128)(2,1)S(1)}, u32[]{:S(2)}, u32[]{:S(2)}) collective-permute-start(bf16[1024,256]{1,0:T(8,128)(2,1)} %get-tuple-element.142.refs_4_), channel_id=1, source_target_pairs={{0,1},{1,0},{2,3},{3,2},{4,5},{5,4},{6,7},{7,6},{8,9},{9,8},{10,11... | collective-permute-start | bytes 1572872 | tf_op jit(solution)/shard_map/ppermute | solution.py:260
  224.3 3.8 %collective-permute-start.36 = (bf16[1024,256]{1,0:T(8,128)(2,1)}, bf16[1024,256]{1,0:T(8,128)(2,1)S(1)}, u32[]{:S(2)}, u32[]{:S(2)}) collective-permute-start(bf16[1024,256]{1,0:T(8,128)(2,1)} %get-tuple-element.152.refs_4_), channel_id=1, source_target_pairs={{0,1},{1,0},{2,3},{3,2},{4,5},{5,4},{6,7},{7,6},{8,9},{9,8},{10,11... | collective-permute-start | bytes 1572872 | tf_op jit(solution)/shard_map/ppermute | solution.py:260
  246.8 7.1 %collective-permute-done.39.refs_1_ = bf16[1024,256]{1,0:T(8,128)(2,1)S(1)} collective-permute-done((bf16[1024,256]{1,0:T(8,128)(2,1)}, bf16[1024,256]{1,0:T(8,128)(2,1)S(1)}, u32[]{:S(2)}, u32[]{:S(2)}) %collective-permute-start.39) | collective-permute-done | bytes 524320 | tf_op jit(solution)/shard_map/ppermute | solution.py:260
  263.2 15.0 %shard_map.46.refs_4_ = bf16[1024,1024]{1,0:T(8,128)(2,1)} custom-call(bf16[1024,1024]{1,0:T(8,128)(2,1)} %get-tuple-element.151.refs_4_.refs_0_.refs_2_.refs_16_, bf16[2048,1024]{1,0:T(8,128)(2,1)} %get-tuple-element.159.refs_1_.refs_3_.refs_5_.refs_7_, bf16[1024,1024]{1,0:T(8,128)(2,1)} %get-tuple-element.151.refs_4_.refs_0_.refs_2_.refs_16_, ...), custom_call_target="tpu_custom_call" | custom-call | flops 8589934592 | tf_op jit(solution)/shard_map/pallas_call | solution.py:103
  278.3 15.0 %shard_map.47.refs_6_ = bf16[1024,1024]{1,0:T(8,128)(2,1)} custom-call(bf16[1024,1024]{1,0:T(8,128)(2,1)} %get-tuple-element.151.refs_4_.refs_0_.refs_2_.refs_16_, bf16[2048,1024]{1,0:T(8,128)(2,1)} %all-gather.29.cloned.1.call-done.refs_1_.refs_3_.refs_5_.refs_7_, bf16[1024,1024]{1,0:T(8,128)(2,1)} %get-tuple-element.151.refs_4_.refs_0_.refs_2_.refs_16_, ...), custom_call_target="tpu_custom_call" | custom-call | flops 8589934592 | tf_op jit(solution)/shard_map/pallas_call | solution.py:103
  293.3 25.3 %shard_map.45.refs_0_.refs_2_ = bf16[1024,2048]{1,0:T(8,128)(2,1)} custom-call(bf16[1024,1024]{1,0:T(8,128)(2,1)} %get-tuple-element.111.refs_0_.refs_8_.refs_10_, bf16[2048,1024]{1,0:T(8,128)(2,1)} %get-tuple-element.128.refs_1_, bf16[1024,1024]{1,0:T(8,128)(2,1)} %get-tuple-element.133.refs_2_.refs_9_.refs_12_.refs_14_, ...), custom_call_target="tpu_custom_call" | custom-call | flops 17179869184 | tf_op jit(solution)/shard_map/pallas_call | solution.py:103
  318.6 24.8 %shard_map.48 = f32[1024,2048]{1,0:T(8,128)} custom-call(bf16[1024,2048]{1,0:T(8,128)(2,1)} %shard_map.45.refs_0_.refs_2_, bf16[1024,2048]{1,0:T(8,128)(2,1)} %all-gather.11.cloned.1.call-done.refs_2_.refs_1_, bf16[1024,2048]{1,0:T(8,128)(2,1)} %shard_map.45.refs_0_.refs_2_, bf16[1024,2048]{1,0:T(8,128)(2,1)} %all-gather.15.cloned.1.call-done.refs_2_.refs_3_, ...), custom_call_target="tpu_custom_call" | custom-call | flops 17179869184 | tf_op jit(solution)/shard_map/pallas_call | solution.py:103
  (185 shorter events, 156.1 us)
Async XLA Ops:
  6.5 32.2 %all-gather.11.cloned.1.call-start = ((), (), s32[]{:S(2)}) async-start(), calls=%async_computation | async-start | bytes 6291456 | tf_op jit(solution)/shard_map/all_gather | solution.py:252
  12.9 47.0 %all-gather.15.cloned.1.call-start = ((), (), s32[]{:S(2)}) async-start(), calls=%async_computation.2 | async-start | bytes 6291456 | tf_op jit(solution)/shard_map/all_gather | solution.py:252
  12.9 52.9 %collective-permute-start.3 = (bf16[512,2048]{1,0:T(8,128)(2,1)}, bf16[512,2048]{1,0:T(8,128)(2,1)}, u32[]{:S(2)}, u32[]{:S(2)}) collective-permute-start(bf16[512,2048]{1,0:T(8,128)(2,1)} %get-tuple-element.162.refs_0_.refs_2_), channel_id=1, source_target_pairs={{0,8},{4,12},{8,0},{12,4},{1,9},{5,13},{9,1},{13,5},{2,10},{6,14},... | collective-permute-start | bytes 6291464 | tf_op jit(solution)/shard_map/ppermute | solution.py:248
  25.8 19.6 %collective-permute-start = (bf16[1024,256]{1,0:T(8,128)(2,1)}, bf16[1024,256]{1,0:T(8,128)(2,1)S(1)}, u32[]{:S(2)}, u32[]{:S(2)}) collective-permute-start(bf16[1024,256]{1,0:T(8,128)(2,1)} %get-tuple-element.83.refs_1_), channel_id=1, source_target_pairs={{0,1},{1,0},{2,3},{3,2},{4,5},{5,4},{6,7},{7,6},{8,9},{9,8},{10,11... | collective-permute-start | bytes 1572872 | tf_op jit(solution)/shard_map/ppermute | solution.py:260
  29.8 24.4 %collective-permute-start.4 = (bf16[1024,256]{1,0:T(8,128)(2,1)}, bf16[1024,256]{1,0:T(8,128)(2,1)S(1)}, u32[]{:S(2)}, u32[]{:S(2)}) collective-permute-start(bf16[1024,256]{1,0:T(8,128)(2,1)} %get-tuple-element.88.refs_1_), channel_id=1, source_target_pairs={{0,1},{1,0},{2,3},{3,2},{4,5},{5,4},{6,7},{7,6},{8,9},{9,8},{10,11... | collective-permute-start | bytes 1572872 | tf_op jit(solution)/shard_map/ppermute | solution.py:260
  30.3 78.2 %all-gather.13.cloned.1.call-start = ((), (), s32[]{:S(2)}) async-start(), calls=%async_computation.1 | async-start | bytes 6291456 | tf_op jit(solution)/shard_map/all_gather | solution.py:252
  58.5 20.0 %collective-permute-start.6 = (bf16[1024,256]{1,0:T(8,128)(2,1)}, bf16[1024,256]{1,0:T(8,128)(2,1)S(1)}, u32[]{:S(2)}, u32[]{:S(2)}) collective-permute-start(bf16[1024,256]{1,0:T(8,128)(2,1)} %get-tuple-element.92.refs_1_), channel_id=1, source_target_pairs={{0,1},{1,0},{2,3},{3,2},{4,5},{5,4},{6,7},{7,6},{8,9},{9,8},{10,11... | collective-permute-start | bytes 1572872 | tf_op jit(solution)/shard_map/ppermute | solution.py:260
  65.9 51.3 %collective-permute-start.15 = (bf16[512,2048]{1,0:T(8,128)(2,1)}, bf16[512,2048]{1,0:T(8,128)(2,1)}, u32[]{:S(2)}, u32[]{:S(2)}) collective-permute-start(bf16[512,2048]{1,0:T(8,128)(2,1)} %get-tuple-element.106), channel_id=1, source_target_pairs={{0,8},{4,12},{8,0},{12,4},{1,9},{5,13},{9,1},{13,5},{2,10},{6,14},... | collective-permute-start | bytes 6291464 | tf_op jit(solution)/shard_map/ppermute | solution.py:248
  71.1 85.1 %all-gather.17.cloned.1.call-start = ((), (), s32[]{:S(2)}) async-start(), calls=%async_computation.3 | async-start | bytes 6291456 | tf_op jit(solution)/shard_map/all_gather | solution.py:252
  94.2 23.0 %collective-permute-start.13 = (bf16[1024,256]{1,0:T(8,128)(2,1)}, bf16[1024,256]{1,0:T(8,128)(2,1)S(1)}, u32[]{:S(2)}, u32[]{:S(2)}) collective-permute-start(bf16[1024,256]{1,0:T(8,128)(2,1)} %get-tuple-element.104.refs_6_.refs_1_), channel_id=1, source_target_pairs={{0,1},{1,0},{2,3},{3,2},{4,5},{5,4},{6,7},{7,6},{8,9},{9,8},{10,11... | collective-permute-start | bytes 1572872 | tf_op jit(solution)/shard_map/ppermute | solution.py:260
  96.5 20.7 %collective-permute-start.14 = (bf16[1024,256]{1,0:T(8,128)(2,1)}, bf16[1024,256]{1,0:T(8,128)(2,1)S(1)}, u32[]{:S(2)}, u32[]{:S(2)}) collective-permute-start(bf16[1024,256]{1,0:T(8,128)(2,1)} %get-tuple-element.105), channel_id=1, source_target_pairs={{1,2},{2,1},{5,6},{6,5},{9,10},{10,9},{13,14},{14,13},{17,18},{18,... | collective-permute-start | bytes 1572872 | tf_op jit(solution)/shard_map/ppermute | solution.py:260
  105.5 20.2 %collective-permute-start.11 = (bf16[1024,256]{1,0:T(8,128)(2,1)}, bf16[1024,256]{1,0:T(8,128)(2,1)S(1)}, u32[]{:S(2)}, u32[]{:S(2)}) collective-permute-start(bf16[1024,256]{1,0:T(8,128)(2,1)} %get-tuple-element.102.refs_6_.refs_1_), channel_id=1, source_target_pairs={{0,1},{1,0},{2,3},{3,2},{4,5},{5,4},{6,7},{7,6},{8,9},{9,8},{10,11... | collective-permute-start | bytes 1572872 | tf_op jit(solution)/shard_map/ppermute | solution.py:260
  121.6 55.5 %all-gather.19.cloned.1.call-start = ((), (), s32[]{:S(2)}) async-start(), calls=%async_computation.4 | async-start | bytes 6291456 | tf_op jit(solution)/shard_map/all_gather | solution.py:252
  134.7 42.4 %collective-permute-start.22 = (bf16[1024,1024]{1,0:T(8,128)(2,1)}, bf16[1024,1024]{1,0:T(8,128)(2,1)S(1)}, u32[]{:S(2)}, u32[]{:S(2)}) collective-permute-start(bf16[1024,1024]{1,0:T(8,128)(2,1)} %get-tuple-element.111.refs_0_.refs_8_.refs_10_), channel_id=1, source_target_pairs={{0,8},{4,12},{8,0},{12,4},{1,9},{5,13},{9,1},{13,5},{2,10},{6,14},... | collective-permute-start | bytes 6291464 | tf_op jit(solution)/shard_map/ppermute | solution.py:248
  135.2 84.9 %all-gather.23.cloned.1.call-start = ((), (), s32[]{:S(2)}) async-start(), calls=%async_computation.6 | async-start | bytes 6291456 | tf_op jit(solution)/shard_map/all_gather | solution.py:252
  140.0 24.9 %collective-permute-start.23 = (bf16[1024,256]{1,0:T(8,128)(2,1)}, bf16[1024,256]{1,0:T(8,128)(2,1)S(1)}, u32[]{:S(2)}, u32[]{:S(2)}) collective-permute-start(bf16[1024,256]{1,0:T(8,128)(2,1)} %get-tuple-element.122.refs_6_.refs_0_), channel_id=1, source_target_pairs={{0,1},{1,0},{2,3},{3,2},{4,5},{5,4},{6,7},{7,6},{8,9},{9,8},{10,11... | collective-permute-start | bytes 1572872 | tf_op jit(solution)/shard_map/ppermute | solution.py:260
  143.5 21.4 %collective-permute-start.24 = (bf16[1024,256]{1,0:T(8,128)(2,1)}, bf16[1024,256]{1,0:T(8,128)(2,1)}, u32[]{:S(2)}, u32[]{:S(2)}) collective-permute-start(bf16[1024,256]{1,0:T(8,128)(2,1)} %get-tuple-element.123), channel_id=1, source_target_pairs={{1,2},{2,1},{5,6},{6,5},{9,10},{10,9},{13,14},{14,13},{17,18},{18,... | collective-permute-start | bytes 1572872 | tf_op jit(solution)/shard_map/ppermute | solution.py:260
  151.9 21.5 %collective-permute-start.20 = (bf16[1024,256]{1,0:T(8,128)(2,1)}, bf16[1024,256]{1,0:T(8,128)(2,1)S(1)}, u32[]{:S(2)}, u32[]{:S(2)}) collective-permute-start(bf16[1024,256]{1,0:T(8,128)(2,1)} %get-tuple-element.120.refs_6_.refs_0_), channel_id=1, source_target_pairs={{0,1},{1,0},{2,3},{3,2},{4,5},{5,4},{6,7},{7,6},{8,9},{9,8},{10,11... | collective-permute-start | bytes 1572872 | tf_op jit(solution)/shard_map/ppermute | solution.py:260
  181.9 52.6 %all-gather.21.cloned.1.call-start = ((), (), s32[]{:S(2)}) async-start(), calls=%async_computation.5 | async-start | bytes 6291456 | tf_op jit(solution)/shard_map/all_gather | solution.py:252
  194.1 40.4 %collective-permute-start.33 = (bf16[1024,1024]{1,0:T(8,128)(2,1)}, bf16[1024,1024]{1,0:T(8,128)(2,1)S(1)}, u32[]{:S(2)}, u32[]{:S(2)}) collective-permute-start(bf16[1024,1024]{1,0:T(8,128)(2,1)} %get-tuple-element.133.refs_2_.refs_9_.refs_12_.refs_14_), channel_id=1, source_target_pairs={{0,8},{4,12},{8,0},{12,4},{1,9},{5,13},{9,1},{13,5},{2,10},{6,14},... | collective-permute-start | bytes 6291464 | tf_op jit(solution)/shard_map/ppermute | solution.py:248
  194.7 68.5 %all-gather.25.cloned.1.call-start = ((), (), s32[]{:S(2)}) async-start(), calls=%async_computation.7 | async-start | bytes 6291456 | tf_op jit(solution)/shard_map/all_gather | solution.py:252
  201.2 18.9 %collective-permute-start.34 = (bf16[1024,256]{1,0:T(8,128)(2,1)}, bf16[1024,256]{1,0:T(8,128)(2,1)S(1)}, u32[]{:S(2)}, u32[]{:S(2)}) collective-permute-start(bf16[1024,256]{1,0:T(8,128)(2,1)} %get-tuple-element.144.refs_5_.refs_0_), channel_id=1, source_target_pairs={{0,1},{1,0},{2,3},{3,2},{4,5},{5,4},{6,7},{7,6},{8,9},{9,8},{10,11... | collective-permute-start | bytes 1572872 | tf_op jit(solution)/shard_map/ppermute | solution.py:260
  229.5 48.7 %all-gather.29.cloned.1.call-start = ((), (), s32[]{:S(2)}) async-start(), calls=%async_computation.9 | async-start | bytes 6291456 | tf_op jit(solution)/shard_map/all_gather | solution.py:252
  246.7 31.5 %all-gather.27.cloned.1.call-start = ((), (), s32[]{:S(2)}) async-start(), calls=%async_computation.8 | async-start | bytes 6291456 | tf_op jit(solution)/shard_map/all_gather | solution.py:252
  (57 other events, 452.5 us)
Sparse Core Ops, SparseCore 0:
  13.0 16.3 all-gather.10
  31.0 14.8 all-gather.14
  71.2 13.5 all-gather.12
  121.7 13.3 all-gather.16
  136.5 14.8 all-gather.18
  182.1 12.6 all-gather.22
  196.3 14.8 all-gather.20
  229.7 12.3 all-gather.24
  246.9 12.2 all-gather.28
  263.3 12.6 all-gather.26

commit v6 on v5

--- a/solution.py
+++ b/solution.py
@@ -118,6 +118,27 @@
             flops=flops, bytes_accessed=0, transcendentals=0
         ),
     )(*operands)
+
+
+def cast_body(source, out):
+    out[...] = source[...].astype(out.dtype)
+
+
+def cast(value, piece, pieces):
+    m, n = value.shape
+    high = m // pieces
+    parts = 4
+    return pl.pallas_call(
+        cast_body,
+        out_shape=jax.ShapeDtypeStruct((high, n), jnp.bfloat16),
+        grid=(parts,),
+        in_specs=[
+            pl.BlockSpec((high // parts, n), lambda j: (piece * parts + j, 0))
+        ],
+        out_specs=pl.BlockSpec((high // parts, n), lambda j: (j, 0)),
+        compiler_params=pltpu.CompilerParams(vmem_limit_bytes=VMEM),
+        cost_estimate=pl.CostEstimate(flops=high * n, bytes_accessed=0, transcendentals=0),
+    )(value)
 
 
 def gram_body(where, *refs):
@@ -270,7 +291,7 @@
         where = jnp.stack([even, core]).astype(jnp.int32)
         evens = range(0, cols - 1, 2)
         x0 = [
-            iterate[p * mp : (p + 1) * mp].astype(jnp.bfloat16) for p in range(PIECES)
+            cast(iterate, p, PIECES) for p in range(PIECES)
         ]
 
         groups = [(d, p) for d in range(chips) for p in range(PIECES)]
@@ -377,11 +398,12 @@
                 column = lambda where: (1 - where[1]) * near + i - near
             return held.get(("s", (d, p))), 2 * mp, column
 
-        def turned(j):
-            per = mp // TILE if mp > TILE else 1
-            return ((j // per) % 2 * PIECES + j // (2 * per)) * per + j % per
+        def turned(tile):
+            per = mp // tile
+            return lambda j: ((j // per) % 2 * PIECES + j // (2 * per)) * per + j % per
 
         def others(e, p):
+            tile, stripe = ((TILE, 1024), (2 * TILE, 512))[p % 2]
             pairs = [
                 (strip[d, r], c, mp, far[d, e, p], c * PIECES + r)
                 for d in range(1, chips)
@@ -396,12 +418,18 @@
             return dots(
                 pairs,
                 2 * mp,
-                min(TILE, mp),
+                min(tile, mp),
                 m,
                 coef_c,
                 [(coef_b, [strip[e, p]])],
                 jnp.bfloat16,
-            )
+                stripe=stripe,
+            )
+
+        for p in range(1, PIECES):
+            begin = order.index(((0, p), 0))
+            hold(("r", p, 0), at_row(0), begin - 2)
+            hold(("r", p, 1), at_row((1 - core) * (q // 2)), begin + q // 2 - 2)
 
         token = jnp.zeros((8, 128), jnp.float32)
         for s in range(steps):
@@ -411,9 +439,11 @@
                 near = q // 2
                 made = None
                 if d == 0 and i == 0:
-                    made = gram(x0, x0[p], at_row(0), near, w)
+                    row = held.pop(("r", p, 0)) if p else at_row(0)
+                    made = gram(x0, x0[p], row, near, w)
                 elif d == 0 and i == near:
-                    made = gram(x0, blocks[g], at_row((1 - core) * near), near, w)
+                    row = held.pop(("r", p, 1)) if p else at_row((1 - core) * near)
+                    made = gram(x0, blocks[g], row, near, w)
                 elif d > 0 and i == 0:
                     made = gram(x0, blocks[g], at_row(0), q, w)
                 if made is not None:
@@ -477,14 +507,16 @@
             launch(g, steps)
 
         poly = {(e, p): others(e, p) for p in range(PIECES) for e in range(1, chips)}
+        tile = min(2 * TILE, mp)
         first = dots(
-            [(strip[g], 0, 2 * mp, chip[g], turned) for g in groups],
+            [(strip[g], 0, 2 * mp, chip[g], turned(tile)) for g in groups],
             2 * m,
-            min(TILE, mp),
+            tile,
             m,
             coef_c,
             [(coef_b, [strip[0, p] for p in range(PIECES)])],
             jnp.bfloat16,
+            stripe=1024,
         )
         factor = 0.2 * math.sqrt(max(HEIGHT, BREADTH))
         return dots(
@@ -497,6 +529,7 @@
             [(coef_a, [iterate])],
             jnp.float32,
             factor,
+            stripe=1024,
         )
 
     return jax.shard_map(

time: 352 us -> 353 us (level)
  Pallas kernels: 194 us -> 204 us
  waiting for transfers between devices: 40.9 us -> 35.8 us
  other arithmetic: 4.64 us -> 0.64 us
    pallas_call x0 -> x2, Pallas kernels: none -> 8.45 us  [cast(): pl.pallas_call(cast_body, out_shape=jax.ShapeDtypeStruct((high, n), jnp.b...]
    ppermute x36, waiting for transfers between devices: 33.7 us -> 25.8 us  [trade(): return lax.ppermute(value, 'cols', pairs)]
    another operation x1 -> x0, other arithmetic: 4.02 us -> none
    unnamed x63 -> x59, local copies, waits for them, and re-layouts: 21.4 us -> 20.6 us
  transfers between devices with their start and end apart: 50 -> 50, of which waited for: 14 -> 13; matrix products, arithmetic and copies ran while one was open for 1% -> 1% of each run, Pallas kernels for 37% -> 38%
where the time goes in v6:
time: 353 us; the launch traced here: 351 us
  Pallas kernels  204 us (58%)
  starting transfers between devices  76 us (22%)
  waiting for transfers between devices  35.8 us (10%)
  local copies, waits for them, and re-layouts  21.2 us (6%)
  between operations  13.8 us (4%)
    pallas_call x4, Pallas kernels, dots(): pl.pallas_call(functools.partial(dots_body, tuple(flips), (dot_scale,) +...  80.9 us
    ppermute x36, starting transfers between devices, trade(): return lax.ppermute(value, 'cols', pairs)  71.5 us
    pallas_call x22, Pallas kernels, mix(): pl.pallas_call(functools.partial(mix_body, tuple(plan), count, idle), out...  71.1 us
    pallas_call x6, Pallas kernels, gram(): pl.pallas_call(gram_body, out_shape=jax.ShapeDtypeStruct((count, m, width...  43.5 us
    ppermute x36, waiting for transfers between devices, trade(): return lax.ppermute(value, 'cols', pairs)  25.8 us
    unnamed x59, local copies, waits for them, and re-layouts  20.6 us
    ppermute x4, waiting for transfers between devices, swap(): return lax.ppermute(value, 'rows', [(i, i ^ mask) for i in range(rows)])  9.71 us
    pallas_call x2, Pallas kernels, cast(): pl.pallas_call(cast_body, out_shape=jax.ShapeDtypeStruct((high, n), jnp.b...  8.45 us
  transfers between devices with their start and end apart: 50, of which 13 were waited for; matrix products, arithmetic and copies ran while one was open for 1% of the time, Pallas kernels for 38%

profile of v6, /device:TPU:0, one launch (start us, length us, event | category | flops | bytes accessed | tf_op | source)
XLA Modules:
  0.0 351.4 jit_solution(15937130916828207334)
XLA Ops:
  6.5 4.2 %shard_map.17.refs_0_.refs_2_ = bf16[512,2048]{1,0:T(8,128)(2,1)} custom-call(f32[1024,2048]{1,0:T(8,128)} %refs_8_.1), custom_call_target="tpu_custom_call" | custom-call | flops 1048576 | tf_op jit(solution)/shard_map/pallas_call | solution.py:131
  13.8 4.2 %shard_map.18.refs_1_.refs_2_ = bf16[512,2048]{1,0:T(8,128)(2,1)} custom-call(f32[1024,2048]{1,0:T(8,128)} %refs_8_.1), custom_call_target="tpu_custom_call" | custom-call | flops 1048576 | tf_op jit(solution)/shard_map/pallas_call | solution.py:131
  18.7 6.6 %shard_map.20.refs_0_.refs_1_ = bf16[2,1024,256]{2,1,0:T(8,128)(2,1)} custom-call(s32[1]{0:T(128)} %constant.30.clone.1.where, bf16[512,2048]{1,0:T(8,128)(2,1)} %shard_map.17.refs_0_.refs_2_, bf16[512,2048]{1,0:T(8,128)(2,1)} %shard_map.18.refs_1_.refs_2_, bf16[512,2048]{1,0:T(8,128)(2,1)} %shard_map.17.refs_0_.refs_2_), custom_call_target="tpu_custom_call" | custom-call | flops 2147483648 | tf_op jit(solution)/shard_map/pallas_call | solution.py:156
  35.2 6.0 %shard_map.19.refs_0_.refs_3_ = bf16[2,1024,256]{2,1,0:T(8,128)(2,1)} custom-call(s32[1]{0:T(128)} %bitcast.2.where.refs_6_, bf16[512,2048]{1,0:T(8,128)(2,1)} %shard_map.17.refs_0_.refs_2_, bf16[512,2048]{1,0:T(8,128)(2,1)} %shard_map.18.refs_1_.refs_2_, bf16[1024,2048]{1,0:T(8,128)(2,1)} %all-gather.11.cloned.1.call-done.refs_2_.refs_1_), custom_call_target="tpu_custom_call" | custom-call | flops 2147483648 | tf_op jit(solution)/shard_map/pallas_call | solution.py:156
  47.7 4.4 %collective-permute-start.2 = (bf16[1024,256]{1,0:T(8,128)(2,1)}, bf16[1024,256]{1,0:T(8,128)(2,1)S(1)}, u32[]{:S(2)}, u32[]{:S(2)}) collective-permute-start(bf16[1024,256]{1,0:T(8,128)(2,1)} %get-tuple-element.90.refs_1_), channel_id=1, source_target_pairs={{0,1},{1,0},{2,3},{3,2},{4,5},{5,4},{6,7},{7,6},{8,9},{9,8},{10,11... | collective-permute-start | bytes 1572872 | tf_op jit(solution)/shard_map/ppermute | solution.py:281
  59.0 4.4 %collective-permute-start.6 = (bf16[1024,256]{1,0:T(8,128)(2,1)}, bf16[1024,256]{1,0:T(8,128)(2,1)S(1)}, u32[]{:S(2)}, u32[]{:S(2)}) collective-permute-start(bf16[1024,256]{1,0:T(8,128)(2,1)} %get-tuple-element.95.refs_1_), channel_id=1, source_target_pairs={{0,1},{1,0},{2,3},{3,2},{4,5},{5,4},{6,7},{7,6},{8,9},{9,8},{10,11... | collective-permute-start | bytes 1572872 | tf_op jit(solution)/shard_map/ppermute | solution.py:281
  63.4 6.9 %shard_map.24.refs_0_.refs_5_.refs_3_ = bf16[2,1024,256]{2,1,0:T(8,128)(2,1)} custom-call(s32[1]{0:T(128)} %get-tuple-element.88.where, bf16[512,2048]{1,0:T(8,128)(2,1)} %shard_map.17.refs_0_.refs_2_, bf16[512,2048]{1,0:T(8,128)(2,1)} %shard_map.18.refs_1_.refs_2_, bf16[512,2048]{1,0:T(8,128)(2,1)} %shard_map.18.refs_1_.refs_2_), custom_call_target="tpu_custom_call" | custom-call | flops 2147483648 | tf_op jit(solution)/shard_map/pallas_call | solution.py:156
  83.7 6.6 %shard_map.28.refs_0_.refs_5_.refs_3_ = bf16[2,1024,256]{2,1,0:T(8,128)(2,1)} custom-call(s32[1]{0:T(128)} %get-tuple-element.96.where, bf16[512,2048]{1,0:T(8,128)(2,1)} %shard_map.17.refs_0_.refs_2_, bf16[512,2048]{1,0:T(8,128)(2,1)} %shard_map.18.refs_1_.refs_2_, bf16[1024,2048]{1,0:T(8,128)(2,1)} %all-gather.15.cloned.1.call-done.refs_2_.refs_3_), custom_call_target="tpu_custom_call" | custom-call | flops 2147483648 | tf_op jit(solution)/shard_map/pallas_call | solution.py:156
  91.3 3.9 %shard_map.30 = (bf16[1024,256]{1,0:T(8,128)(2,1)}, bf16[1024,256]{1,0:T(8,128)(2,1)}, bf16[1024,1024]{1,0:T(8,128)(2,1)}, f32[8,128]{1,0:T(8,128)}) custom-call(s32[2]{0:T(128)} %pad_add_fusion.where, bf16[2,1024,256]{2,1,0:T(8,128)(2,1)} %shard_map.28.refs_0_.refs_5_.refs_3_, ...), custom_call_target="tpu_custom_call", output_to_operand_aliasing={{3}: (9, {})} | custom-call | flops 40000000000 | tf_op jit(solution)/shard_map/pallas_call | solution.py:244
  95.2 4.4 %collective-permute-start.13 = (bf16[1024,256]{1,0:T(8,128)(2,1)}, bf16[1024,256]{1,0:T(8,128)(2,1)S(1)}, u32[]{:S(2)}, u32[]{:S(2)}) collective-permute-start(bf16[1024,256]{1,0:T(8,128)(2,1)} %get-tuple-element.108.refs_6_.refs_1_), channel_id=1, source_target_pairs={{0,1},{1,0},{2,3},{3,2},{4,5},{5,4},{6,7},{7,6},{8,9},{9,8},{10,11... | collective-permute-start | bytes 1572872 | tf_op jit(solution)/shard_map/ppermute | solution.py:281
  106.9 8.7 %shard_map.27.refs_0_.refs_5_.refs_3_ = bf16[4,1024,256]{2,1,0:T(8,128)(2,1)} custom-call(s32[1]{0:T(128)} %constant.30.clone.1.where, bf16[512,2048]{1,0:T(8,128)(2,1)} %shard_map.17.refs_0_.refs_2_, bf16[512,2048]{1,0:T(8,128)(2,1)} %shard_map.18.refs_1_.refs_2_, bf16[1024,2048]{1,0:T(8,128)(2,1)} %all-gather.13.cloned.1.call-done.refs_2_.refs_5_), custom_call_target="tpu_custom_call" | custom-call | flops 4294967296 | tf_op jit(solution)/shard_map/pallas_call | solution.py:156
  121.1 4.0 %collective-permute-start.18 = (bf16[1024,256]{1,0:T(8,128)(2,1)S(1)}, bf16[1024,256]{1,0:T(8,128)(2,1)}, u32[]{:S(2)}, u32[]{:S(2)}) collective-permute-start(bf16[1024,256]{1,0:T(8,128)(2,1)S(1)} %copy-done.3), channel_id=1, source_target_pairs={{0,1},{1,0},{2,3},{3,2},{4,5},{5,4},{6,7},{7,6},{8,9},{9,8},{10,11... | collective-permute-start | bytes 1572872 | tf_op jit(solution)/shard_map/ppermute | solution.py:281
  140.6 4.3 %collective-permute-start.23 = (bf16[1024,256]{1,0:T(8,128)(2,1)}, bf16[1024,256]{1,0:T(8,128)(2,1)S(1)}, u32[]{:S(2)}, u32[]{:S(2)}) collective-permute-start(bf16[1024,256]{1,0:T(8,128)(2,1)} %get-tuple-element.126.refs_6_.refs_0_), channel_id=1, source_target_pairs={{0,1},{1,0},{2,3},{3,2},{4,5},{5,4},{6,7},{7,6},{8,9},{9,8},{10,11... | collective-permute-start | bytes 1572872 | tf_op jit(solution)/shard_map/ppermute | solution.py:281
  157.6 8.7 %shard_map.34.refs_0_.refs_5_.refs_2_.refs_4_ = bf16[4,1024,256]{2,1,0:T(8,128)(2,1)} custom-call(s32[1]{0:T(128)} %constant.30.clone.1.where, bf16[512,2048]{1,0:T(8,128)(2,1)} %shard_map.17.refs_0_.refs_2_, bf16[512,2048]{1,0:T(8,128)(2,1)} %shard_map.18.refs_1_.refs_2_, bf16[1024,2048]{1,0:T(8,128)(2,1)} %all-gather.17.cloned.1.call-done.refs_2_.refs_7_), custom_call_target="tpu_custom_call" | custom-call | flops 4294967296 | tf_op jit(solution)/shard_map/pallas_call | solution.py:156
  172.8 4.2 %collective-permute-done.22.refs_9_ = bf16[1024,1024]{1,0:T(8,128)(2,1)S(1)} collective-permute-done((bf16[1024,1024]{1,0:T(8,128)(2,1)}, bf16[1024,1024]{1,0:T(8,128)(2,1)S(1)}, u32[]{:S(2)}, u32[]{:S(2)}) %collective-permute-start.22) | collective-permute-done | bytes 2097184 | tf_op jit(solution)/shard_map/ppermute | solution.py:269
  200.4 4.9 %collective-permute-start.34 = (bf16[1024,256]{1,0:T(8,128)(2,1)}, bf16[1024,256]{1,0:T(8,128)(2,1)S(1)}, u32[]{:S(2)}, u32[]{:S(2)}) collective-permute-start(bf16[1024,256]{1,0:T(8,128)(2,1)} %get-tuple-element.148.refs_5_.refs_0_), channel_id=1, source_target_pairs={{0,1},{1,0},{2,3},{3,2},{4,5},{5,4},{6,7},{7,6},{8,9},{9,8},{10,11... | collective-permute-start | bytes 1572872 | tf_op jit(solution)/shard_map/ppermute | solution.py:281
  212.2 4.2 %collective-permute-start.31 = (bf16[1024,256]{1,0:T(8,128)(2,1)}, bf16[1024,256]{1,0:T(8,128)(2,1)S(1)}, u32[]{:S(2)}, u32[]{:S(2)}) collective-permute-start(bf16[1024,256]{1,0:T(8,128)(2,1)} %get-tuple-element.146.refs_4_), channel_id=1, source_target_pairs={{0,1},{1,0},{2,3},{3,2},{4,5},{5,4},{6,7},{7,6},{8,9},{9,8},{10,11... | collective-permute-start | bytes 1572872 | tf_op jit(solution)/shard_map/ppermute | solution.py:281
  223.4 4.2 %collective-permute-start.36 = (bf16[1024,256]{1,0:T(8,128)(2,1)}, bf16[1024,256]{1,0:T(8,128)(2,1)S(1)}, u32[]{:S(2)}, u32[]{:S(2)}) collective-permute-start(bf16[1024,256]{1,0:T(8,128)(2,1)} %get-tuple-element.156.refs_4_), channel_id=1, source_target_pairs={{0,1},{1,0},{2,3},{3,2},{4,5},{5,4},{6,7},{7,6},{8,9},{9,8},{10,11... | collective-permute-start | bytes 1572872 | tf_op jit(solution)/shard_map/ppermute | solution.py:281
  230.5 5.5 %collective-permute-done.33.refs_7_ = bf16[1024,1024]{1,0:T(8,128)(2,1)S(1)} collective-permute-done((bf16[1024,1024]{1,0:T(8,128)(2,1)}, bf16[1024,1024]{1,0:T(8,128)(2,1)S(1)}, u32[]{:S(2)}, u32[]{:S(2)}) %collective-permute-start.33) | collective-permute-done | bytes 2097184 | tf_op jit(solution)/shard_map/ppermute | solution.py:269
  246.7 7.6 %collective-permute-done.39.refs_1_ = bf16[1024,256]{1,0:T(8,128)(2,1)S(1)} collective-permute-done((bf16[1024,256]{1,0:T(8,128)(2,1)}, bf16[1024,256]{1,0:T(8,128)(2,1)S(1)}, u32[]{:S(2)}, u32[]{:S(2)}) %collective-permute-start.39) | collective-permute-done | bytes 524320 | tf_op jit(solution)/shard_map/ppermute | solution.py:281
  263.6 15.0 %shard_map.48.refs_4_ = bf16[1024,1024]{1,0:T(8,128)(2,1)} custom-call(bf16[1024,1024]{1,0:T(8,128)(2,1)} %get-tuple-element.155.refs_4_.refs_0_.refs_2_.refs_16_, bf16[2048,1024]{1,0:T(8,128)(2,1)} %get-tuple-element.163.refs_1_.refs_3_.refs_5_.refs_7_, bf16[1024,1024]{1,0:T(8,128)(2,1)} %get-tuple-element.155.refs_4_.refs_0_.refs_2_.refs_16_, ...), custom_call_target="tpu_custom_call" | custom-call | flops 8589934592 | tf_op jit(solution)/shard_map/pallas_call | solution.py:103
  278.6 15.6 %shard_map.49.refs_6_ = bf16[1024,1024]{1,0:T(8,128)(2,1)} custom-call(bf16[1024,1024]{1,0:T(8,128)(2,1)} %get-tuple-element.155.refs_4_.refs_0_.refs_2_.refs_16_, bf16[2048,1024]{1,0:T(8,128)(2,1)} %all-gather.29.cloned.1.call-done.refs_1_.refs_3_.refs_5_.refs_7_, bf16[1024,1024]{1,0:T(8,128)(2,1)} %get-tuple-element.155.refs_4_.refs_0_.refs_2_.refs_16_, ...), custom_call_target="tpu_custom_call" | custom-call | flops 8589934592 | tf_op jit(solution)/shard_map/pallas_call | solution.py:103
  294.3 25.5 %shard_map.47.refs_0_.refs_2_ = bf16[1024,2048]{1,0:T(8,128)(2,1)} custom-call(bf16[1024,1024]{1,0:T(8,128)(2,1)} %get-tuple-element.115.refs_0_.refs_8_.refs_10_, bf16[2048,1024]{1,0:T(8,128)(2,1)} %get-tuple-element.132.refs_1_, bf16[1024,1024]{1,0:T(8,128)(2,1)} %get-tuple-element.137.refs_2_.refs_9_.refs_12_.refs_14_, ...), custom_call_target="tpu_custom_call" | custom-call | flops 17179869184 | tf_op jit(solution)/shard_map/pallas_call | solution.py:103
  319.8 24.8 %shard_map.50 = f32[1024,2048]{1,0:T(8,128)} custom-call(bf16[1024,2048]{1,0:T(8,128)(2,1)} %shard_map.47.refs_0_.refs_2_, bf16[1024,2048]{1,0:T(8,128)(2,1)} %all-gather.11.cloned.1.call-done.refs_2_.refs_1_, bf16[1024,2048]{1,0:T(8,128)(2,1)} %shard_map.47.refs_0_.refs_2_, bf16[1024,2048]{1,0:T(8,128)(2,1)} %all-gather.15.cloned.1.call-done.refs_2_.refs_3_, ...), custom_call_target="tpu_custom_call" | custom-call | flops 17179869184 | tf_op jit(solution)/shard_map/pallas_call | solution.py:103
  (181 shorter events, 148.7 us)
Async XLA Ops:
  6.5 28.7 %all-gather.11.cloned.1.call-start = ((), (), s32[]{:S(2)}) async-start(), calls=%async_computation | async-start | bytes 6291456 | tf_op jit(solution)/shard_map/all_gather | solution.py:273
  10.8 72.9 %all-gather.15.cloned.1.call-start = ((), (), s32[]{:S(2)}) async-start(), calls=%async_computation.2 | async-start | bytes 6291456 | tf_op jit(solution)/shard_map/all_gather | solution.py:273
  10.8 59.5 %collective-permute-start.3 = (bf16[512,2048]{1,0:T(8,128)(2,1)}, bf16[512,2048]{1,0:T(8,128)(2,1)}, u32[]{:S(2)}, u32[]{:S(2)}) collective-permute-start(bf16[512,2048]{1,0:T(8,128)(2,1)} %shard_map.17.refs_0_.refs_2_), channel_id=1, source_target_pairs={{0,8},{4,12},{8,0},{12,4},{1,9},{5,13},{9,1},{13,5},{2,10},{6,14},... | collective-permute-start | bytes 6291464 | tf_op jit(solution)/shard_map/ppermute | solution.py:269
  32.3 22.3 %collective-permute-start.4 = (bf16[1024,256]{1,0:T(8,128)(2,1)}, bf16[1024,256]{1,0:T(8,128)(2,1)S(1)}, u32[]{:S(2)}, u32[]{:S(2)}) collective-permute-start(bf16[1024,256]{1,0:T(8,128)(2,1)} %get-tuple-element.91.refs_1_), channel_id=1, source_target_pairs={{0,1},{1,0},{2,3},{3,2},{4,5},{5,4},{6,7},{7,6},{8,9},{9,8},{10,11... | collective-permute-start | bytes 1572872 | tf_op jit(solution)/shard_map/ppermute | solution.py:281
  32.8 74.1 %all-gather.13.cloned.1.call-start = ((), (), s32[]{:S(2)}) async-start(), calls=%async_computation.1 | async-start | bytes 6291456 | tf_op jit(solution)/shard_map/all_gather | solution.py:273
  47.0 23.4 %collective-permute-start.1 = (bf16[1024,256]{1,0:T(8,128)(2,1)}, bf16[1024,256]{1,0:T(8,128)(2,1)S(1)}, u32[]{:S(2)}, u32[]{:S(2)}) collective-permute-start(bf16[1024,256]{1,0:T(8,128)(2,1)} %get-tuple-element.89), channel_id=1, source_target_pairs={{1,2},{2,1},{5,6},{6,5},{9,10},{10,9},{13,14},{14,13},{17,18},{18,... | collective-permute-start | bytes 1572872 | tf_op jit(solution)/shard_map/ppermute | solution.py:281
  47.7 22.7 %collective-permute-start.2 = (bf16[1024,256]{1,0:T(8,128)(2,1)}, bf16[1024,256]{1,0:T(8,128)(2,1)S(1)}, u32[]{:S(2)}, u32[]{:S(2)}) collective-permute-start(bf16[1024,256]{1,0:T(8,128)(2,1)} %get-tuple-element.90.refs_1_), channel_id=1, source_target_pairs={{0,1},{1,0},{2,3},{3,2},{4,5},{5,4},{6,7},{7,6},{8,9},{9,8},{10,11... | collective-permute-start | bytes 1572872 | tf_op jit(solution)/shard_map/ppermute | solution.py:281
  70.3 45.3 %collective-permute-start.15 = (bf16[512,2048]{1,0:T(8,128)(2,1)}, bf16[512,2048]{1,0:T(8,128)(2,1)}, u32[]{:S(2)}, u32[]{:S(2)}) collective-permute-start(bf16[512,2048]{1,0:T(8,128)(2,1)} %get-tuple-element.110), channel_id=1, source_target_pairs={{0,8},{4,12},{8,0},{12,4},{1,9},{5,13},{9,1},{13,5},{2,10},{6,14},... | collective-permute-start | bytes 6291464 | tf_op jit(solution)/shard_map/ppermute | solution.py:269
  80.8 19.4 %collective-permute-start.7 = (bf16[1024,256]{1,0:T(8,128)(2,1)}, bf16[1024,256]{1,0:T(8,128)(2,1)S(1)}, u32[]{:S(2)}, u32[]{:S(2)}) collective-permute-start(bf16[1024,256]{1,0:T(8,128)(2,1)} %get-tuple-element.99.refs_6_.refs_1_), channel_id=1, source_target_pairs={{0,1},{1,0},{2,3},{3,2},{4,5},{5,4},{6,7},{7,6},{8,9},{9,8},{10,11... | collective-permute-start | bytes 1572872 | tf_op jit(solution)/shard_map/ppermute | solution.py:281
  83.6 74.0 %all-gather.17.cloned.1.call-start = ((), (), s32[]{:S(2)}) async-start(), calls=%async_computation.3 | async-start | bytes 6291456 | tf_op jit(solution)/shard_map/all_gather | solution.py:273
  95.2 20.4 %collective-permute-start.13 = (bf16[1024,256]{1,0:T(8,128)(2,1)}, bf16[1024,256]{1,0:T(8,128)(2,1)S(1)}, u32[]{:S(2)}, u32[]{:S(2)}) collective-permute-start(bf16[1024,256]{1,0:T(8,128)(2,1)} %get-tuple-element.108.refs_6_.refs_1_), channel_id=1, source_target_pairs={{0,1},{1,0},{2,3},{3,2},{4,5},{5,4},{6,7},{7,6},{8,9},{9,8},{10,11... | collective-permute-start | bytes 1572872 | tf_op jit(solution)/shard_map/ppermute | solution.py:281
  104.6 21.9 %collective-permute-start.11 = (bf16[1024,256]{1,0:T(8,128)(2,1)}, bf16[1024,256]{1,0:T(8,128)(2,1)S(1)}, u32[]{:S(2)}, u32[]{:S(2)}) collective-permute-start(bf16[1024,256]{1,0:T(8,128)(2,1)} %get-tuple-element.106.refs_6_.refs_1_), channel_id=1, source_target_pairs={{0,1},{1,0},{2,3},{3,2},{4,5},{5,4},{6,7},{7,6},{8,9},{9,8},{10,11... | collective-permute-start | bytes 1572872 | tf_op jit(solution)/shard_map/ppermute | solution.py:281
  106.2 20.4 %collective-permute-start.12 = (bf16[1024,256]{1,0:T(8,128)(2,1)}, bf16[1024,256]{1,0:T(8,128)(2,1)S(1)}, u32[]{:S(2)}, u32[]{:S(2)}) collective-permute-start(bf16[1024,256]{1,0:T(8,128)(2,1)} %get-tuple-element.107), channel_id=1, source_target_pairs={{1,2},{2,1},{5,6},{6,5},{9,10},{10,9},{13,14},{14,13},{17,18},{18,... | collective-permute-start | bytes 1572872 | tf_op jit(solution)/shard_map/ppermute | solution.py:281
  120.1 57.0 %all-gather.19.cloned.1.call-start = ((), (), s32[]{:S(2)}) async-start(), calls=%async_computation.4 | async-start | bytes 6291456 | tf_op jit(solution)/shard_map/all_gather | solution.py:273
  133.7 43.3 %collective-permute-start.22 = (bf16[1024,1024]{1,0:T(8,128)(2,1)}, bf16[1024,1024]{1,0:T(8,128)(2,1)S(1)}, u32[]{:S(2)}, u32[]{:S(2)}) collective-permute-start(bf16[1024,1024]{1,0:T(8,128)(2,1)} %get-tuple-element.115.refs_0_.refs_8_.refs_10_), channel_id=1, source_target_pairs={{0,8},{4,12},{8,0},{12,4},{1,9},{5,13},{9,1},{13,5},{2,10},{6,14},... | collective-permute-start | bytes 6291464 | tf_op jit(solution)/shard_map/ppermute | solution.py:269
  134.5 84.8 %all-gather.23.cloned.1.call-start = ((), (), s32[]{:S(2)}) async-start(), calls=%async_computation.6 | async-start | bytes 6291456 | tf_op jit(solution)/shard_map/all_gather | solution.py:273
  140.6 25.7 %collective-permute-start.23 = (bf16[1024,256]{1,0:T(8,128)(2,1)}, bf16[1024,256]{1,0:T(8,128)(2,1)S(1)}, u32[]{:S(2)}, u32[]{:S(2)}) collective-permute-start(bf16[1024,256]{1,0:T(8,128)(2,1)} %get-tuple-element.126.refs_6_.refs_0_), channel_id=1, source_target_pairs={{0,1},{1,0},{2,3},{3,2},{4,5},{5,4},{6,7},{7,6},{8,9},{9,8},{10,11... | collective-permute-start | bytes 1572872 | tf_op jit(solution)/shard_map/ppermute | solution.py:281
  144.9 21.4 %collective-permute-start.24 = (bf16[1024,256]{1,0:T(8,128)(2,1)}, bf16[1024,256]{1,0:T(8,128)(2,1)}, u32[]{:S(2)}, u32[]{:S(2)}) collective-permute-start(bf16[1024,256]{1,0:T(8,128)(2,1)} %get-tuple-element.127), channel_id=1, source_target_pairs={{1,2},{2,1},{5,6},{6,5},{9,10},{10,9},{13,14},{14,13},{17,18},{18,... | collective-permute-start | bytes 1572872 | tf_op jit(solution)/shard_map/ppermute | solution.py:281
  152.6 20.2 %collective-permute-start.20 = (bf16[1024,256]{1,0:T(8,128)(2,1)}, bf16[1024,256]{1,0:T(8,128)(2,1)S(1)}, u32[]{:S(2)}, u32[]{:S(2)}) collective-permute-start(bf16[1024,256]{1,0:T(8,128)(2,1)} %get-tuple-element.124.refs_6_.refs_0_), channel_id=1, source_target_pairs={{0,1},{1,0},{2,3},{3,2},{4,5},{5,4},{6,7},{7,6},{8,9},{9,8},{10,11... | collective-permute-start | bytes 1572872 | tf_op jit(solution)/shard_map/ppermute | solution.py:281
  181.9 54.1 %all-gather.21.cloned.1.call-start = ((), (), s32[]{:S(2)}) async-start(), calls=%async_computation.5 | async-start | bytes 6291456 | tf_op jit(solution)/shard_map/all_gather | solution.py:273
  195.3 40.7 %collective-permute-start.33 = (bf16[1024,1024]{1,0:T(8,128)(2,1)}, bf16[1024,1024]{1,0:T(8,128)(2,1)S(1)}, u32[]{:S(2)}, u32[]{:S(2)}) collective-permute-start(bf16[1024,1024]{1,0:T(8,128)(2,1)} %get-tuple-element.137.refs_2_.refs_9_.refs_12_.refs_14_), channel_id=1, source_target_pairs={{0,8},{4,12},{8,0},{12,4},{1,9},{5,13},{9,1},{13,5},{2,10},{6,14},... | collective-permute-start | bytes 6291464 | tf_op jit(solution)/shard_map/ppermute | solution.py:269
  195.5 68.1 %all-gather.25.cloned.1.call-start = ((), (), s32[]{:S(2)}) async-start(), calls=%async_computation.7 | async-start | bytes 6291456 | tf_op jit(solution)/shard_map/all_gather | solution.py:273
  229.2 49.4 %all-gather.29.cloned.1.call-start = ((), (), s32[]{:S(2)}) async-start(), calls=%async_computation.9 | async-start | bytes 6291456 | tf_op jit(solution)/shard_map/all_gather | solution.py:273
  246.7 31.9 %all-gather.27.cloned.1.call-start = ((), (), s32[]{:S(2)}) async-start(), calls=%async_computation.8 | async-start | bytes 6291456 | tf_op jit(solution)/shard_map/all_gather | solution.py:273
  (55 other events, 443.4 us)
Sparse Core Ops, SparseCore 0:
  10.9 16.3 all-gather.10
  32.9 13.9 all-gather.14
  83.8 14.5 all-gather.12
  120.2 14.6 all-gather.16
  136.2 14.8 all-gather.18
  182.0 13.3 all-gather.22
  196.9 14.8 all-gather.20
  229.3 13.0 all-gather.24
  246.8 12.6 all-gather.28
  263.7 12.8 all-gather.26

commit v7 on v6

--- a/solution.py
+++ b/solution.py
@@ -118,27 +118,6 @@
             flops=flops, bytes_accessed=0, transcendentals=0
         ),
     )(*operands)
-
-
-def cast_body(source, out):
-    out[...] = source[...].astype(out.dtype)
-
-
-def cast(value, piece, pieces):
-    m, n = value.shape
-    high = m // pieces
-    parts = 4
-    return pl.pallas_call(
-        cast_body,
-        out_shape=jax.ShapeDtypeStruct((high, n), jnp.bfloat16),
-        grid=(parts,),
-        in_specs=[
-            pl.BlockSpec((high // parts, n), lambda j: (piece * parts + j, 0))
-        ],
-        out_specs=pl.BlockSpec((high // parts, n), lambda j: (j, 0)),
-        compiler_params=pltpu.CompilerParams(vmem_limit_bytes=VMEM),
-        cost_estimate=pl.CostEstimate(flops=high * n, bytes_accessed=0, transcendentals=0),
-    )(value)
 
 
 def gram_body(where, *refs):
@@ -291,7 +270,7 @@
         where = jnp.stack([even, core]).astype(jnp.int32)
         evens = range(0, cols - 1, 2)
         x0 = [
-            cast(iterate, p, PIECES) for p in range(PIECES)
+            iterate[p * mp : (p + 1) * mp].astype(jnp.bfloat16) for p in range(PIECES)
         ]
 
         groups = [(d, p) for d in range(chips) for p in range(PIECES)]
@@ -364,7 +343,8 @@
         def launch(g, s):
             d0, p = g
             strip[g] = held.pop(("s", g))
-            later(("c", g), side(strip[g]), s + GAP, chip, g)
+            hidden = g == (0, PIECES - 1) and s + GAP < steps
+            later(("c", g), side(strip[g]), steps - 1 if hidden else s + GAP, chip, g)
             for d in range(1, chips):
                 e = d ^ d0
                 if e == 0:
@@ -496,31 +476,48 @@
         for action in late:
             action()
 
+        tile = min(2 * TILE, mp)
+
+        def first(part, adds, dtype):
+            return dots(
+                [(strip[g], 0, 2 * mp, chip[g], turned(tile)) for g in part],
+                2 * m,
+                tile,
+                m,
+                coef_c,
+                adds,
+                dtype,
+                stripe=1024,
+            )
+
+        near = groups[:PIECES]
+        early = None
+        if all(g in strip for g in near):
+            early = first(
+                near, [(coef_b, [strip[0, p] for p in range(PIECES)])], jnp.float32
+            )
         for g in groups:
             if g in strip:
                 continue
             for i in range(q):
                 j = order.index((g, i))
                 if j + lag + SKEW >= steps:
-                    out = mix(where, [final(j)], [], PARTS, target(j))
+                    pass_on = [] if early is None else [early]
+                    out = mix(where, [final(j)], pass_on, PARTS, target(j))
                     held["s", g] = out[0]
+                    early = out[1] if pass_on else None
             launch(g, steps)
 
         poly = {(e, p): others(e, p) for p in range(PIECES) for e in range(1, chips)}
-        tile = min(2 * TILE, mp)
-        first = dots(
-            [(strip[g], 0, 2 * mp, chip[g], turned(tile)) for g in groups],
-            2 * m,
-            tile,
-            m,
-            coef_c,
-            [(coef_b, [strip[0, p] for p in range(PIECES)])],
-            jnp.bfloat16,
-            stripe=1024,
-        )
+        if early is None:
+            own_poly = first(
+                groups, [(coef_b, [strip[0, p] for p in range(PIECES)])], jnp.bfloat16
+            )
+        else:
+            own_poly = first(groups[PIECES:], [(1.0, [early])], jnp.bfloat16)
         factor = 0.2 * math.sqrt(max(HEIGHT, BREADTH))
         return dots(
-            [(first, p, 2 * mp, blocks[0, p], 0) for p in range(PIECES)]
+            [(own_poly, p, 2 * mp, blocks[0, p], 0) for p in range(PIECES)]
             + [(poly[g], 0, 2 * mp, blocks[g], 0) for g in groups if g[0]],
             n,
             TILE,

time: 353 us -> 354 us (level)
  other arithmetic: 0.64 us -> 4.63 us
    ppermute x36, waiting for transfers between devices: 25.8 us -> 15.6 us  [trade(): return lax.ppermute(value, 'cols', pairs)]
    ppermute x4, waiting for transfers between devices: 9.71 us -> 18.5 us  [swap(): return lax.ppermute(value, 'rows', [(i, i ^ mask) for i in range(rows)])]
    pallas_call x2 -> x0, Pallas kernels: 8.45 us -> none  [cast(): pl.pallas_call(cast_body, out_shape=jax.ShapeDtypeStruct((high, n), jnp.b...]
    pallas_call x4 -> x5, Pallas kernels: 80.9 us -> 86.5 us  [dots(): pl.pallas_call(functools.partial(dots_body, tuple(flips), (dot_scale,) +...]
    another operation x0 -> x1, other arithmetic: none -> 4.02 us
    unnamed x59 -> x61, local copies, waits for them, and re-layouts: 20.6 us -> 19.5 us
  transfers between devices with their start and end apart: 50 -> 50, of which waited for: 13 -> 10; matrix products, arithmetic and copies ran while one was open for 1% -> 1% of each run, Pallas kernels for 38% -> 41%
where the time goes in v7:
time: 354 us; the launch traced here: 352 us
  Pallas kernels  201 us (57%)
  starting transfers between devices  76.2 us (22%)
  waiting for transfers between devices  34.4 us (10%)
  local copies, waits for them, and re-layouts  22.4 us (6%)
  between operations  13.9 us (4%)
  other arithmetic  4.63 us (1%)
    pallas_call x5, Pallas kernels, dots(): pl.pallas_call(functools.partial(dots_body, tuple(flips), (dot_scale,) +...  86.5 us
    pallas_call x22, Pallas kernels, mix(): pl.pallas_call(functools.partial(mix_body, tuple(plan), count, idle), out...  71.2 us
    ppermute x36, starting transfers between devices, trade(): return lax.ppermute(value, 'cols', pairs)  68.6 us
    pallas_call x6, Pallas kernels, gram(): pl.pallas_call(gram_body, out_shape=jax.ShapeDtypeStruct((count, m, width...  42.8 us
    unnamed x61, local copies, waits for them, and re-layouts  19.5 us
    ppermute x4, waiting for transfers between devices, swap(): return lax.ppermute(value, 'rows', [(i, i ^ mask) for i in range(rows)])  18.5 us
    ppermute x36, waiting for transfers between devices, trade(): return lax.ppermute(value, 'cols', pairs)  15.6 us
    ppermute x4, starting transfers between devices, swap(): return lax.ppermute(value, 'rows', [(i, i ^ mask) for i in range(rows)])  7.3 us
  transfers between devices with their start and end apart: 50, of which 10 were waited for; matrix products, arithmetic and copies ran while one was open for 1% of the time, Pallas kernels for 41%

profile of v7, /device:TPU:0, one launch (start us, length us, event | category | flops | bytes accessed | tf_op | source)
XLA Modules:
  0.0 352.0 jit_solution(4045828304932136497)
XLA Ops:
  6.5 4.0 %convert.4 = bf16[1024,2048]{1,0:T(8,128)(2,1)S(1)} convert(f32[1024,2048]{1,0:T(8,128)} %refs_8_.1) | non-fusion elementwise | flops 2097152 | bytes 12582912 | tf_op jit(solution)/shard_map/convert.1
  16.5 6.1 %shard_map.18.refs_0_.refs_1_ = bf16[2,1024,256]{2,1,0:T(8,128)(2,1)} custom-call(s32[1]{0:T(128)} %constant.30.clone.1.where, bf16[512,2048]{1,0:T(8,128)(2,1)} %get-tuple-element.174.refs_0_.refs_2_, bf16[512,2048]{1,0:T(8,128)(2,1)} %get-tuple-element.173.refs_1_.refs_2_, bf16[512,2048]{1,0:T(8,128)(2,1)} %get-tuple-element.174.refs_0_.refs_2_), custom_call_target="tpu_custom_call" | custom-call | flops 2147483648 | tf_op jit(solution)/shard_map/pallas_call | solution.py:135
  32.6 5.9 %shard_map.17.refs_0_.refs_3_ = bf16[2,1024,256]{2,1,0:T(8,128)(2,1)} custom-call(s32[1]{0:T(128)} %bitcast.2.where.refs_6_, bf16[512,2048]{1,0:T(8,128)(2,1)} %get-tuple-element.174.refs_0_.refs_2_, bf16[512,2048]{1,0:T(8,128)(2,1)} %get-tuple-element.173.refs_1_.refs_2_, bf16[1024,2048]{1,0:T(8,128)(2,1)} %all-gather.11.cloned.1.call-done.refs_2_.refs_1_), custom_call_target="tpu_custom_call" | custom-call | flops 2147483648 | tf_op jit(solution)/shard_map/pallas_call | solution.py:135
  45.4 4.5 %collective-permute-start.2 = (bf16[1024,256]{1,0:T(8,128)(2,1)}, bf16[1024,256]{1,0:T(8,128)(2,1)S(1)}, u32[]{:S(2)}, u32[]{:S(2)}) collective-permute-start(bf16[1024,256]{1,0:T(8,128)(2,1)} %get-tuple-element.94.refs_1_), channel_id=1, source_target_pairs={{0,1},{1,0},{2,3},{3,2},{4,5},{5,4},{6,7},{7,6},{8,9},{9,8},{10,11... | collective-permute-start | bytes 1572872 | tf_op jit(solution)/shard_map/ppermute | solution.py:260
  56.4 4.4 %collective-permute-start.6 = (bf16[1024,256]{1,0:T(8,128)(2,1)}, bf16[1024,256]{1,0:T(8,128)(2,1)S(1)}, u32[]{:S(2)}, u32[]{:S(2)}) collective-permute-start(bf16[1024,256]{1,0:T(8,128)(2,1)} %get-tuple-element.100.refs_1_), channel_id=1, source_target_pairs={{0,1},{1,0},{2,3},{3,2},{4,5},{5,4},{6,7},{7,6},{8,9},{9,8},{10,11... | collective-permute-start | bytes 1572872 | tf_op jit(solution)/shard_map/ppermute | solution.py:260
  60.7 6.7 %shard_map.22.refs_0_.refs_5_.refs_3_ = bf16[2,1024,256]{2,1,0:T(8,128)(2,1)} custom-call(s32[1]{0:T(128)} %get-tuple-element.92.where, bf16[512,2048]{1,0:T(8,128)(2,1)} %get-tuple-element.174.refs_0_.refs_2_, bf16[512,2048]{1,0:T(8,128)(2,1)} %get-tuple-element.173.refs_1_.refs_2_, bf16[512,2048]{1,0:T(8,128)(2,1)} %get-tuple-element.173.refs_1_.refs_2_), custom_call_target="tpu_custom_call" | custom-call | flops 2147483648 | tf_op jit(solution)/shard_map/pallas_call | solution.py:135
  79.7 6.7 %shard_map.27.refs_0_.refs_5_.refs_3_ = bf16[2,1024,256]{2,1,0:T(8,128)(2,1)} custom-call(s32[1]{0:T(128)} %get-tuple-element.103.where, bf16[512,2048]{1,0:T(8,128)(2,1)} %get-tuple-element.174.refs_0_.refs_2_, bf16[512,2048]{1,0:T(8,128)(2,1)} %get-tuple-element.173.refs_1_.refs_2_, bf16[1024,2048]{1,0:T(8,128)(2,1)} %all-gather.15.cloned.1.call-done.refs_2_.refs_3_), custom_call_target="tpu_custom_call" | custom-call | flops 2147483648 | tf_op jit(solution)/shard_map/pallas_call | solution.py:135
  88.5 3.9 %shard_map.28 = (bf16[1024,256]{1,0:T(8,128)(2,1)}, bf16[1024,256]{1,0:T(8,128)(2,1)}, bf16[1024,1024]{1,0:T(8,128)(2,1)}, f32[8,128]{1,0:T(8,128)}) custom-call(s32[2]{0:T(128)} %pad_add_fusion.where, bf16[2,1024,256]{2,1,0:T(8,128)(2,1)} %shard_map.27.refs_0_.refs_5_.refs_3_, ...), custom_call_target="tpu_custom_call", output_to_operand_aliasing={{3}: (9, {})} | custom-call | flops 40000000000 | tf_op jit(solution)/shard_map/pallas_call | solution.py:223
  92.4 4.6 %collective-permute-start.13 = (bf16[1024,256]{1,0:T(8,128)(2,1)}, bf16[1024,256]{1,0:T(8,128)(2,1)S(1)}, u32[]{:S(2)}, u32[]{:S(2)}) collective-permute-start(bf16[1024,256]{1,0:T(8,128)(2,1)} %get-tuple-element.112.refs_6_.refs_1_), channel_id=1, source_target_pairs={{0,1},{1,0},{2,3},{3,2},{4,5},{5,4},{6,7},{7,6},{8,9},{9,8},{10,11... | collective-permute-start | bytes 1572872 | tf_op jit(solution)/shard_map/ppermute | solution.py:260
  104.4 8.7 %shard_map.25.refs_0_.refs_5_.refs_3_ = bf16[4,1024,256]{2,1,0:T(8,128)(2,1)} custom-call(s32[1]{0:T(128)} %constant.30.clone.1.where, bf16[512,2048]{1,0:T(8,128)(2,1)} %get-tuple-element.174.refs_0_.refs_2_, bf16[512,2048]{1,0:T(8,128)(2,1)} %get-tuple-element.173.refs_1_.refs_2_, bf16[1024,2048]{1,0:T(8,128)(2,1)} %all-gather.13.cloned.1.call-done.refs_2_.refs_5_), custom_call_target="tpu_custom_call" | custom-call | flops 4294967296 | tf_op jit(solution)/shard_map/pallas_call | solution.py:135
  118.6 4.6 %collective-permute-start.18 = (bf16[1024,256]{1,0:T(8,128)(2,1)S(1)}, bf16[1024,256]{1,0:T(8,128)(2,1)S(1)}, u32[]{:S(2)}, u32[]{:S(2)}) collective-permute-start(bf16[1024,256]{1,0:T(8,128)(2,1)S(1)} %copy-done.3), channel_id=1, source_target_pairs={{0,1},{1,0},{2,3},{3,2},{4,5},{5,4},{6,7},{7,6},{8,9},{9,8},{10,11... | collective-permute-start | bytes 1572872 | tf_op jit(solution)/shard_map/ppermute | solution.py:260
  125.7 3.8 %shard_map.31 = (bf16[1024,256]{1,0:T(8,128)(2,1)}, bf16[1024,256]{1,0:T(8,128)(2,1)}, bf16[1024,1024]{1,0:T(8,128)(2,1)}, f32[8,128]{1,0:T(8,128)}) custom-call(s32[2]{0:T(128)} %pad_add_fusion.where, bf16[4,1024,256]{2,1,0:T(8,128)(2,1)} %shard_map.25.refs_0_.refs_5_.refs_3_, ...), custom_call_target="tpu_custom_call", output_to_operand_aliasing={{3}: (9, {}), {2}: (10, {})} | custom-call | flops 40000000000 | tf_op jit(solution)/shard_map/pallas_call | solution.py:223
  145.7 4.0 %shard_map.33 = (bf16[1024,256]{1,0:T(8,128)(2,1)}, bf16[1024,256]{1,0:T(8,128)(2,1)}, bf16[1024,1024]{1,0:T(8,128)(2,1)}, f32[8,128]{1,0:T(8,128)}) custom-call(s32[2]{0:T(128)} %pad_add_fusion.where, bf16[4,1024,256]{2,1,0:T(8,128)(2,1)} %shard_map.25.refs_0_.refs_5_.refs_3_, ...), custom_call_target="tpu_custom_call", output_to_operand_aliasing={{3}: (9, {}), {2}: (10, {})} | custom-call | flops 40000000000 | tf_op jit(solution)/shard_map/pallas_call | solution.py:223
  149.7 3.8 %collective-permute-start.20 = (bf16[1024,256]{1,0:T(8,128)(2,1)}, bf16[1024,256]{1,0:T(8,128)(2,1)S(1)}, u32[]{:S(2)}, u32[]{:S(2)}) collective-permute-start(bf16[1024,256]{1,0:T(8,128)(2,1)} %get-tuple-element.126.refs_6_.refs_0_), channel_id=1, source_target_pairs={{0,1},{1,0},{2,3},{3,2},{4,5},{5,4},{6,7},{7,6},{8,9},{9,8},{10,11... | collective-permute-start | bytes 1572872 | tf_op jit(solution)/shard_map/ppermute | solution.py:260
  155.0 8.7 %shard_map.34.refs_0_.refs_5_.refs_2_.refs_4_ = bf16[4,1024,256]{2,1,0:T(8,128)(2,1)} custom-call(s32[1]{0:T(128)} %constant.30.clone.1.where, bf16[512,2048]{1,0:T(8,128)(2,1)} %get-tuple-element.174.refs_0_.refs_2_, bf16[512,2048]{1,0:T(8,128)(2,1)} %get-tuple-element.173.refs_1_.refs_2_, bf16[1024,2048]{1,0:T(8,128)(2,1)} %all-gather.17.cloned.1.call-done.refs_2_.refs_7_), custom_call_target="tpu_custom_call" | custom-call | flops 4294967296 | tf_op jit(solution)/shard_map/pallas_call | solution.py:135
  170.3 3.9 %collective-permute-done.22.refs_9_ = bf16[1024,1024]{1,0:T(8,128)(2,1)S(1)} collective-permute-done((bf16[1024,1024]{1,0:T(8,128)(2,1)}, bf16[1024,1024]{1,0:T(8,128)(2,1)S(1)}, u32[]{:S(2)}, u32[]{:S(2)}) %collective-permute-start.22) | collective-permute-done | bytes 2097184 | tf_op jit(solution)/shard_map/ppermute | solution.py:248
  190.7 3.7 %collective-permute-done.25.refs_2_.refs_5_ = bf16[1024,256]{1,0:T(8,128)(2,1)S(1)} collective-permute-done((bf16[1024,256]{1,0:T(8,128)(2,1)}, bf16[1024,256]{1,0:T(8,128)(2,1)S(1)}, u32[]{:S(2)}, u32[]{:S(2)}) %collective-permute-start.25) | collective-permute-done | bytes 524320 | tf_op jit(solution)/shard_map/ppermute | solution.py:260
  199.1 4.0 %collective-permute-start.29 = (bf16[1024,256]{1,0:T(8,128)(2,1)}, bf16[1024,256]{1,0:T(8,128)(2,1)S(1)}, u32[]{:S(2)}, u32[]{:S(2)}) collective-permute-start(bf16[1024,256]{1,0:T(8,128)(2,1)} %get-tuple-element.144.refs_5_.refs_0_), channel_id=1, source_target_pairs={{0,1},{1,0},{2,3},{3,2},{4,5},{5,4},{6,7},{7,6},{8,9},{9,8},{10,11... | collective-permute-start | bytes 1572872 | tf_op jit(solution)/shard_map/ppermute | solution.py:260
  228.2 14.6 %collective-permute-done.37.refs_6_ = bf16[1024,1024]{1,0:T(8,128)(2,1)} collective-permute-done((bf16[1024,1024]{1,0:T(8,128)(2,1)S(1)}, bf16[1024,1024]{1,0:T(8,128)(2,1)}, u32[]{:S(2)}, u32[]{:S(2)}) %collective-permute-start.37) | collective-permute-done | bytes 2097184 | tf_op jit(solution)/shard_map/ppermute | solution.py:248
  251.3 16.2 %shard_map.43.refs_4_ = f32[1024,2048]{1,0:T(8,128)} custom-call(bf16[1024,1024]{1,0:T(8,128)(2,1)} %get-tuple-element.129.refs_0_.refs_4_.refs_8_.refs_10_, bf16[2048,1024]{1,0:T(8,128)(2,1)} %get-tuple-element.164.refs_1_, bf16[1024,1024]{1,0:T(8,128)(2,1)} %get-tuple-element.156.refs_2_.refs_5_.refs_12_.refs_14_, ...), custom_call_target="tpu_custom_call" | custom-call | flops 8589934592 | tf_op jit(solution)/shard_map/pallas_call | solution.py:103
  274.8 15.1 %shard_map.47.refs_4_ = bf16[1024,1024]{1,0:T(8,128)(2,1)} custom-call(bf16[1024,1024]{1,0:T(8,128)(2,1)} %get-tuple-element.153.refs_0_.refs_2_.refs_16_, bf16[2048,1024]{1,0:T(8,128)(2,1)} %get-tuple-element.171.refs_1_.refs_3_.refs_5_.refs_7_, bf16[1024,1024]{1,0:T(8,128)(2,1)} %get-tuple-element.153.refs_0_.refs_2_.refs_16_, ...), custom_call_target="tpu_custom_call" | custom-call | flops 8589934592 | tf_op jit(solution)/shard_map/pallas_call | solution.py:103
  290.0 15.7 %shard_map.48.refs_6_ = bf16[1024,1024]{1,0:T(8,128)(2,1)} custom-call(bf16[1024,1024]{1,0:T(8,128)(2,1)} %get-tuple-element.153.refs_0_.refs_2_.refs_16_, bf16[2048,1024]{1,0:T(8,128)(2,1)} %all-gather.29.cloned.1.call-done.refs_1_.refs_3_.refs_5_.refs_7_, bf16[1024,1024]{1,0:T(8,128)(2,1)} %get-tuple-element.153.refs_0_.refs_2_.refs_16_, ...), custom_call_target="tpu_custom_call" | custom-call | flops 8589934592 | tf_op jit(solution)/shard_map/pallas_call | solution.py:103
  305.7 14.7 %shard_map.46.refs_0_.refs_2_ = bf16[1024,2048]{1,0:T(8,128)(2,1)} custom-call(bf16[1024,1024]{1,0:T(8,128)(2,1)} %get-tuple-element.153.refs_0_.refs_2_.refs_16_, bf16[2048,1024]{1,0:T(8,128)(2,1)} %all-gather.23.cloned.1.call-done.refs_1_.refs_9_.refs_11_.refs_13_.refs_15_, bf16[1024,1024]{1,0:T(8,128)(2,1)} %get-tuple-element.169.refs_2_.refs_4_.refs_6_.refs_16_, ...), custom_call_target="tpu_custom_call" | custom-call | flops 8589934592 | tf_op jit(solution)/shard_map/pallas_call | solution.py:103
  320.4 24.8 %shard_map.49 = f32[1024,2048]{1,0:T(8,128)} custom-call(bf16[1024,2048]{1,0:T(8,128)(2,1)} %shard_map.46.refs_0_.refs_2_, bf16[1024,2048]{1,0:T(8,128)(2,1)} %all-gather.11.cloned.1.call-done.refs_2_.refs_1_, bf16[1024,2048]{1,0:T(8,128)(2,1)} %shard_map.46.refs_0_.refs_2_, bf16[1024,2048]{1,0:T(8,128)(2,1)} %all-gather.15.cloned.1.call-done.refs_2_.refs_3_, ...), custom_call_target="tpu_custom_call" | custom-call | flops 17179869184 | tf_op jit(solution)/shard_map/pallas_call | solution.py:103
  (184 shorter events, 145.1 us)
Async XLA Ops:
  6.5 26.1 %all-gather.11.cloned.1.call-start = ((), (), s32[]{:S(2)}) async-start(), calls=%async_computation | async-start | bytes 6291456 | tf_op jit(solution)/shard_map/all_gather | solution.py:252
  12.9 66.9 %all-gather.15.cloned.1.call-start = ((), (), s32[]{:S(2)}) async-start(), calls=%async_computation.2 | async-start | bytes 6291456 | tf_op jit(solution)/shard_map/all_gather | solution.py:252
  12.9 54.5 %collective-permute-start.3 = (bf16[512,2048]{1,0:T(8,128)(2,1)}, bf16[512,2048]{1,0:T(8,128)(2,1)}, u32[]{:S(2)}, u32[]{:S(2)}) collective-permute-start(bf16[512,2048]{1,0:T(8,128)(2,1)} %get-tuple-element.174.refs_0_.refs_2_), channel_id=1, source_target_pairs={{0,8},{4,12},{8,0},{12,4},{1,9},{5,13},{9,1},{13,5},{2,10},{6,14},... | collective-permute-start | bytes 6291464 | tf_op jit(solution)/shard_map/ppermute | solution.py:248
  29.7 22.3 %collective-permute-start.4 = (bf16[1024,256]{1,0:T(8,128)(2,1)}, bf16[1024,256]{1,0:T(8,128)(2,1)S(1)}, u32[]{:S(2)}, u32[]{:S(2)}) collective-permute-start(bf16[1024,256]{1,0:T(8,128)(2,1)} %get-tuple-element.95.refs_1_), channel_id=1, source_target_pairs={{0,1},{1,0},{2,3},{3,2},{4,5},{5,4},{6,7},{7,6},{8,9},{9,8},{10,11... | collective-permute-start | bytes 1572872 | tf_op jit(solution)/shard_map/ppermute | solution.py:260
  30.2 74.2 %all-gather.13.cloned.1.call-start = ((), (), s32[]{:S(2)}) async-start(), calls=%async_computation.1 | async-start | bytes 6291456 | tf_op jit(solution)/shard_map/all_gather | solution.py:252
  44.7 23.3 %collective-permute-start.1 = (bf16[1024,256]{1,0:T(8,128)(2,1)}, bf16[1024,256]{1,0:T(8,128)(2,1)S(1)}, u32[]{:S(2)}, u32[]{:S(2)}) collective-permute-start(bf16[1024,256]{1,0:T(8,128)(2,1)} %get-tuple-element.93), channel_id=1, source_target_pairs={{1,2},{2,1},{5,6},{6,5},{9,10},{10,9},{13,14},{14,13},{17,18},{18,... | collective-permute-start | bytes 1572872 | tf_op jit(solution)/shard_map/ppermute | solution.py:260
  45.4 22.6 %collective-permute-start.2 = (bf16[1024,256]{1,0:T(8,128)(2,1)}, bf16[1024,256]{1,0:T(8,128)(2,1)S(1)}, u32[]{:S(2)}, u32[]{:S(2)}) collective-permute-start(bf16[1024,256]{1,0:T(8,128)(2,1)} %get-tuple-element.94.refs_1_), channel_id=1, source_target_pairs={{0,1},{1,0},{2,3},{3,2},{4,5},{5,4},{6,7},{7,6},{8,9},{9,8},{10,11... | collective-permute-start | bytes 1572872 | tf_op jit(solution)/shard_map/ppermute | solution.py:260
  67.4 45.7 %collective-permute-start.15 = (bf16[512,2048]{1,0:T(8,128)(2,1)}, bf16[512,2048]{1,0:T(8,128)(2,1)}, u32[]{:S(2)}, u32[]{:S(2)}) collective-permute-start(bf16[512,2048]{1,0:T(8,128)(2,1)} %get-tuple-element.114), channel_id=1, source_target_pairs={{0,8},{4,12},{8,0},{12,4},{1,9},{5,13},{9,1},{13,5},{2,10},{6,14},... | collective-permute-start | bytes 6291464 | tf_op jit(solution)/shard_map/ppermute | solution.py:248
  79.7 75.3 %all-gather.17.cloned.1.call-start = ((), (), s32[]{:S(2)}) async-start(), calls=%async_computation.3 | async-start | bytes 6291456 | tf_op jit(solution)/shard_map/all_gather | solution.py:252
  102.2 22.5 %collective-permute-start.11 = (bf16[1024,256]{1,0:T(8,128)(2,1)}, bf16[1024,256]{1,0:T(8,128)(2,1)S(1)}, u32[]{:S(2)}, u32[]{:S(2)}) collective-permute-start(bf16[1024,256]{1,0:T(8,128)(2,1)} %get-tuple-element.110.refs_6_.refs_1_), channel_id=1, source_target_pairs={{0,1},{1,0},{2,3},{3,2},{4,5},{5,4},{6,7},{7,6},{8,9},{9,8},{10,11... | collective-permute-start | bytes 1572872 | tf_op jit(solution)/shard_map/ppermute | solution.py:260
  103.7 21.0 %collective-permute-start.12 = (bf16[1024,256]{1,0:T(8,128)(2,1)}, bf16[1024,256]{1,0:T(8,128)(2,1)S(1)}, u32[]{:S(2)}, u32[]{:S(2)}) collective-permute-start(bf16[1024,256]{1,0:T(8,128)(2,1)} %get-tuple-element.111), channel_id=1, source_target_pairs={{1,2},{2,1},{5,6},{6,5},{9,10},{10,9},{13,14},{14,13},{17,18},{18,... | collective-permute-start | bytes 1572872 | tf_op jit(solution)/shard_map/ppermute | solution.py:260
  117.6 56.6 %all-gather.19.cloned.1.call-start = ((), (), s32[]{:S(2)}) async-start(), calls=%async_computation.4 | async-start | bytes 6291456 | tf_op jit(solution)/shard_map/all_gather | solution.py:252
  131.8 42.3 %collective-permute-start.22 = (bf16[1024,1024]{1,0:T(8,128)(2,1)}, bf16[1024,1024]{1,0:T(8,128)(2,1)S(1)}, u32[]{:S(2)}, u32[]{:S(2)}) collective-permute-start(bf16[1024,1024]{1,0:T(8,128)(2,1)} %get-tuple-element.129.refs_0_.refs_4_.refs_8_.refs_10_), channel_id=1, source_target_pairs={{0,8},{4,12},{8,0},{12,4},{1,9},{5,13},{9,1},{13,5},{2,10},{6,14},... | collective-permute-start | bytes 6291464 | tf_op jit(solution)/shard_map/ppermute | solution.py:248
  133.4 83.5 %all-gather.21.cloned.1.call-start = ((), (), s32[]{:S(2)}) async-start(), calls=%async_computation.5 | async-start | bytes 6291456 | tf_op jit(solution)/shard_map/all_gather | solution.py:252
  138.6 25.1 %collective-permute-start.23 = (bf16[1024,256]{1,0:T(8,128)(2,1)}, bf16[1024,256]{1,0:T(8,128)(2,1)S(1)}, u32[]{:S(2)}, u32[]{:S(2)}) collective-permute-start(bf16[1024,256]{1,0:T(8,128)(2,1)} %get-tuple-element.130.refs_6_.refs_0_), channel_id=1, source_target_pairs={{0,1},{1,0},{2,3},{3,2},{4,5},{5,4},{6,7},{7,6},{8,9},{9,8},{10,11... | collective-permute-start | bytes 1572872 | tf_op jit(solution)/shard_map/ppermute | solution.py:260
  142.2 21.5 %collective-permute-start.24 = (bf16[1024,256]{1,0:T(8,128)(2,1)}, bf16[1024,256]{1,0:T(8,128)(2,1)}, u32[]{:S(2)}, u32[]{:S(2)}) collective-permute-start(bf16[1024,256]{1,0:T(8,128)(2,1)} %get-tuple-element.131), channel_id=1, source_target_pairs={{1,2},{2,1},{5,6},{6,5},{9,10},{10,9},{13,14},{14,13},{17,18},{18,... | collective-permute-start | bytes 1572872 | tf_op jit(solution)/shard_map/ppermute | solution.py:260
  182.2 65.5 %all-gather.25.cloned.1.call-start = ((), (), s32[]{:S(2)}) async-start(), calls=%async_computation.7 | async-start | bytes 6291456 | tf_op jit(solution)/shard_map/all_gather | solution.py:252
  204.5 38.2 %collective-permute-start.37 = (bf16[1024,1024]{1,0:T(8,128)(2,1)S(1)}, bf16[1024,1024]{1,0:T(8,128)(2,1)}, u32[]{:S(2)}, u32[]{:S(2)}) collective-permute-start(bf16[1024,1024]{1,0:T(8,128)(2,1)S(1)} %copy-done.1), channel_id=1, source_target_pairs={{0,8},{4,12},{8,0},{12,4},{1,9},{5,13},{9,1},{13,5},{2,10},{6,14},... | collective-permute-start | bytes 6291464 | tf_op jit(solution)/shard_map/ppermute | solution.py:248
  206.8 68.0 %all-gather.23.cloned.1.call-start = ((), (), s32[]{:S(2)}) async-start(), calls=%async_computation.6 | async-start | bytes 6291456 | tf_op jit(solution)/shard_map/all_gather | solution.py:252
  221.0 68.9 %all-gather.29.cloned.1.call-start = ((), (), s32[]{:S(2)}) async-start(), calls=%async_computation.9 | async-start | bytes 6291456 | tf_op jit(solution)/shard_map/all_gather | solution.py:252
  222.0 25.6 %collective-permute-start.33 = (bf16[1024,256]{1,0:T(8,128)(2,1)S(1)}, bf16[1024,256]{1,0:T(8,128)(2,1)}, u32[]{:S(2)}, u32[]{:S(2)}) collective-permute-start(bf16[1024,256]{1,0:T(8,128)(2,1)S(1)} %copy-done.19), channel_id=1, source_target_pairs={{0,1},{1,0},{2,3},{3,2},{4,5},{5,4},{6,7},{7,6},{8,9},{9,8},{10,11... | collective-permute-start | bytes 1572872 | tf_op jit(solution)/shard_map/ppermute | solution.py:260
  225.6 22.0 %collective-permute-start.34 = (bf16[1024,256]{1,0:T(8,128)(2,1)S(1)}, bf16[1024,256]{1,0:T(8,128)(2,1)}, u32[]{:S(2)}, u32[]{:S(2)}) collective-permute-start(bf16[1024,256]{1,0:T(8,128)(2,1)S(1)} %copy-done.20), channel_id=1, source_target_pairs={{1,2},{2,1},{5,6},{6,5},{9,10},{10,9},{13,14},{14,13},{17,18},{18,... | collective-permute-start | bytes 1572872 | tf_op jit(solution)/shard_map/ppermute | solution.py:260
  245.9 21.6 %collective-permute-start.39 = (bf16[1024,256]{1,0:T(8,128)(2,1)}, bf16[1024,256]{1,0:T(8,128)(2,1)S(1)}, u32[]{:S(2)}, u32[]{:S(2)}) collective-permute-start(bf16[1024,256]{1,0:T(8,128)(2,1)} %get-tuple-element.163.refs_2_), channel_id=1, source_target_pairs={{0,1},{1,0},{2,3},{3,2},{4,5},{5,4},{6,7},{7,6},{8,9},{9,8},{10,11... | collective-permute-start | bytes 1572872 | tf_op jit(solution)/shard_map/ppermute | solution.py:260
  247.6 42.4 %all-gather.27.cloned.1.call-start = ((), (), s32[]{:S(2)}) async-start(), calls=%async_computation.8 | async-start | bytes 6291456 | tf_op jit(solution)/shard_map/all_gather | solution.py:252
  (56 other events, 473.5 us)
Sparse Core Ops, SparseCore 0:
  13.0 16.3 all-gather.10
  30.9 14.8 all-gather.14
  79.8 15.6 all-gather.12
  117.7 15.9 all-gather.16
  135.1 14.8 all-gather.18
  182.3 13.1 all-gather.20
  207.0 12.3 all-gather.24
  221.1 15.6 all-gather.22
  247.7 13.5 all-gather.28
  274.9 13.4 all-gather.26

commit v8 on v7

--- a/solution.py
+++ b/solution.py
@@ -343,16 +343,15 @@
         def launch(g, s):
             d0, p = g
             strip[g] = held.pop(("s", g))
-            hidden = g == (0, PIECES - 1) and s + GAP < steps
-            later(("c", g), side(strip[g]), steps - 1 if hidden else s + GAP, chip, g)
+            later(("c", g), side(strip[g]), s + GAP, chip, g)
             for d in range(1, chips):
                 e = d ^ d0
                 if e == 0:
                     continue
                 over = swap(strip[g], 2 * d)
-                if s + q < steps:
-                    hold(("f", d, e, p), over, s + q)
-                    then(s + q, functools.partial(land, d, e, p, s + q))
+                if s + q + p < steps:
+                    hold(("f", d, e, p), over, s + q + p)
+                    then(s + q + p, functools.partial(land, d, e, p, s + q + p))
                 else:
                     far[d, e, p] = side(over)
 
@@ -383,7 +382,7 @@
             return lambda j: ((j // per) % 2 * PIECES + j // (2 * per)) * per + j % per
 
         def others(e, p):
-            tile, stripe = ((TILE, 1024), (2 * TILE, 512))[p % 2]
+            tile, stripe = TILE, 512
             pairs = [
                 (strip[d, r], c, mp, far[d, e, p], c * PIECES + r)
                 for d in range(1, chips)
@@ -446,7 +445,7 @@
             j = s - lag - SKEW
             if j >= 0:
                 sums.append(final(j))
-            keys = passing[s]
+            keys = list(passing[s])
             out = mix(
                 where,
                 sums,

time: 354 us -> 349 us (0.986)
  waiting for transfers between devices: 34.4 us -> 27.9 us
    ppermute x4, waiting for transfers between devices: 18.5 us -> 10.5 us  [swap(): return lax.ppermute(value, 'rows', [(i, i ^ mask) for i in range(rows)])]
  transfers between devices with their start and end apart: 50 -> 50, of which waited for: 10 -> 10; matrix products, arithmetic and copies ran while one was open for 1% -> 1% of each run, Pallas kernels for 41% -> 42%
where the time goes in v8:
time: 349 us; the launch traced here: 348 us
  Pallas kernels  199 us (57%)
  starting transfers between devices  79.2 us (23%)
  waiting for transfers between devices  27.9 us (8%)
  local copies, waits for them, and re-layouts  22.9 us (7%)
  between operations  13.9 us (4%)
  other arithmetic  4.67 us (1%)
    pallas_call x5, Pallas kernels, dots(): pl.pallas_call(functools.partial(dots_body, tuple(flips), (dot_scale,) +...  85.5 us
    ppermute x36, starting transfers between devices, trade(): return lax.ppermute(value, 'cols', pairs)  71 us
    pallas_call x22, Pallas kernels, mix(): pl.pallas_call(functools.partial(mix_body, tuple(plan), count, idle), out...  70.9 us
    pallas_call x6, Pallas kernels, gram(): pl.pallas_call(gram_body, out_shape=jax.ShapeDtypeStruct((count, m, width...  42.9 us
    unnamed x61, local copies, waits for them, and re-layouts  20.1 us
    ppermute x36, waiting for transfers between devices, trade(): return lax.ppermute(value, 'cols', pairs)  17.2 us
    ppermute x4, waiting for transfers between devices, swap(): return lax.ppermute(value, 'rows', [(i, i ^ mask) for i in range(rows)])  10.5 us
    ppermute x4, starting transfers between devices, swap(): return lax.ppermute(value, 'rows', [(i, i ^ mask) for i in range(rows)])  7.78 us
  transfers between devices with their start and end apart: 50, of which 10 were waited for; matrix products, arithmetic and copies ran while one was open for 1% of the time, Pallas kernels for 42%

profile of v8, /device:TPU:0, one launch (start us, length us, event | category | flops | bytes accessed | tf_op | source)
XLA Modules:
  0.0 347.8 jit_solution(7581457942134262627)
XLA Ops:
  6.5 4.0 %convert.4 = bf16[1024,2048]{1,0:T(8,128)(2,1)S(1)} convert(f32[1024,2048]{1,0:T(8,128)} %refs_8_.1) | non-fusion elementwise | flops 2097152 | bytes 12582912 | tf_op jit(solution)/shard_map/convert.1
  16.6 6.1 %shard_map.18.refs_0_.refs_1_ = bf16[2,1024,256]{2,1,0:T(8,128)(2,1)} custom-call(s32[1]{0:T(128)} %constant.30.clone.1.where, bf16[512,2048]{1,0:T(8,128)(2,1)} %get-tuple-element.174.refs_0_.refs_2_, bf16[512,2048]{1,0:T(8,128)(2,1)} %get-tuple-element.173.refs_1_.refs_2_, bf16[512,2048]{1,0:T(8,128)(2,1)} %get-tuple-element.174.refs_0_.refs_2_), custom_call_target="tpu_custom_call" | custom-call | flops 2147483648 | tf_op jit(solution)/shard_map/pallas_call | solution.py:135
  32.7 5.9 %shard_map.17.refs_0_.refs_3_ = bf16[2,1024,256]{2,1,0:T(8,128)(2,1)} custom-call(s32[1]{0:T(128)} %bitcast.2.where.refs_6_, bf16[512,2048]{1,0:T(8,128)(2,1)} %get-tuple-element.174.refs_0_.refs_2_, bf16[512,2048]{1,0:T(8,128)(2,1)} %get-tuple-element.173.refs_1_.refs_2_, bf16[1024,2048]{1,0:T(8,128)(2,1)} %all-gather.11.cloned.1.call-done.refs_2_.refs_1_), custom_call_target="tpu_custom_call" | custom-call | flops 2147483648 | tf_op jit(solution)/shard_map/pallas_call | solution.py:135
  45.3 4.5 %collective-permute-start.2 = (bf16[1024,256]{1,0:T(8,128)(2,1)}, bf16[1024,256]{1,0:T(8,128)(2,1)S(1)}, u32[]{:S(2)}, u32[]{:S(2)}) collective-permute-start(bf16[1024,256]{1,0:T(8,128)(2,1)} %get-tuple-element.94.refs_1_), channel_id=1, source_target_pairs={{0,1},{1,0},{2,3},{3,2},{4,5},{5,4},{6,7},{7,6},{8,9},{9,8},{10,11... | collective-permute-start | bytes 1572872 | tf_op jit(solution)/shard_map/ppermute | solution.py:260
  56.4 4.4 %collective-permute-start.6 = (bf16[1024,256]{1,0:T(8,128)(2,1)}, bf16[1024,256]{1,0:T(8,128)(2,1)S(1)}, u32[]{:S(2)}, u32[]{:S(2)}) collective-permute-start(bf16[1024,256]{1,0:T(8,128)(2,1)} %get-tuple-element.100.refs_1_), channel_id=1, source_target_pairs={{0,1},{1,0},{2,3},{3,2},{4,5},{5,4},{6,7},{7,6},{8,9},{9,8},{10,11... | collective-permute-start | bytes 1572872 | tf_op jit(solution)/shard_map/ppermute | solution.py:260
  60.8 6.8 %shard_map.22.refs_0_.refs_5_.refs_3_ = bf16[2,1024,256]{2,1,0:T(8,128)(2,1)} custom-call(s32[1]{0:T(128)} %get-tuple-element.92.where, bf16[512,2048]{1,0:T(8,128)(2,1)} %get-tuple-element.174.refs_0_.refs_2_, bf16[512,2048]{1,0:T(8,128)(2,1)} %get-tuple-element.173.refs_1_.refs_2_, bf16[512,2048]{1,0:T(8,128)(2,1)} %get-tuple-element.173.refs_1_.refs_2_), custom_call_target="tpu_custom_call" | custom-call | flops 2147483648 | tf_op jit(solution)/shard_map/pallas_call | solution.py:135
  79.8 6.7 %shard_map.27.refs_0_.refs_5_.refs_3_ = bf16[2,1024,256]{2,1,0:T(8,128)(2,1)} custom-call(s32[1]{0:T(128)} %get-tuple-element.103.where, bf16[512,2048]{1,0:T(8,128)(2,1)} %get-tuple-element.174.refs_0_.refs_2_, bf16[512,2048]{1,0:T(8,128)(2,1)} %get-tuple-element.173.refs_1_.refs_2_, bf16[1024,2048]{1,0:T(8,128)(2,1)} %all-gather.15.cloned.1.call-done.refs_2_.refs_3_), custom_call_target="tpu_custom_call" | custom-call | flops 2147483648 | tf_op jit(solution)/shard_map/pallas_call | solution.py:135
  88.7 3.9 %shard_map.28 = (bf16[1024,256]{1,0:T(8,128)(2,1)}, bf16[1024,256]{1,0:T(8,128)(2,1)}, bf16[1024,1024]{1,0:T(8,128)(2,1)}, f32[8,128]{1,0:T(8,128)}) custom-call(s32[2]{0:T(128)} %pad_add_fusion.where, bf16[2,1024,256]{2,1,0:T(8,128)(2,1)} %shard_map.27.refs_0_.refs_5_.refs_3_, ...), custom_call_target="tpu_custom_call", output_to_operand_aliasing={{3}: (9, {})} | custom-call | flops 40000000000 | tf_op jit(solution)/shard_map/pallas_call | solution.py:223
  92.6 4.6 %collective-permute-start.13 = (bf16[1024,256]{1,0:T(8,128)(2,1)}, bf16[1024,256]{1,0:T(8,128)(2,1)S(1)}, u32[]{:S(2)}, u32[]{:S(2)}) collective-permute-start(bf16[1024,256]{1,0:T(8,128)(2,1)} %get-tuple-element.112.refs_6_.refs_1_), channel_id=1, source_target_pairs={{0,1},{1,0},{2,3},{3,2},{4,5},{5,4},{6,7},{7,6},{8,9},{9,8},{10,11... | collective-permute-start | bytes 1572872 | tf_op jit(solution)/shard_map/ppermute | solution.py:260
  104.6 8.7 %shard_map.25.refs_0_.refs_5_.refs_3_ = bf16[4,1024,256]{2,1,0:T(8,128)(2,1)} custom-call(s32[1]{0:T(128)} %constant.30.clone.1.where, bf16[512,2048]{1,0:T(8,128)(2,1)} %get-tuple-element.174.refs_0_.refs_2_, bf16[512,2048]{1,0:T(8,128)(2,1)} %get-tuple-element.173.refs_1_.refs_2_, bf16[1024,2048]{1,0:T(8,128)(2,1)} %all-gather.13.cloned.1.call-done.refs_2_.refs_5_), custom_call_target="tpu_custom_call" | custom-call | flops 4294967296 | tf_op jit(solution)/shard_map/pallas_call | solution.py:135
  118.8 4.6 %collective-permute-start.18 = (bf16[1024,256]{1,0:T(8,128)(2,1)S(1)}, bf16[1024,256]{1,0:T(8,128)(2,1)}, u32[]{:S(2)}, u32[]{:S(2)}) collective-permute-start(bf16[1024,256]{1,0:T(8,128)(2,1)S(1)} %copy-done.3), channel_id=1, source_target_pairs={{0,1},{1,0},{2,3},{3,2},{4,5},{5,4},{6,7},{7,6},{8,9},{9,8},{10,11... | collective-permute-start | bytes 1572872 | tf_op jit(solution)/shard_map/ppermute | solution.py:260
  125.8 3.8 %shard_map.31 = (bf16[1024,256]{1,0:T(8,128)(2,1)}, bf16[1024,256]{1,0:T(8,128)(2,1)}, bf16[1024,1024]{1,0:T(8,128)(2,1)}, f32[8,128]{1,0:T(8,128)}) custom-call(s32[2]{0:T(128)} %pad_add_fusion.where, bf16[4,1024,256]{2,1,0:T(8,128)(2,1)} %shard_map.25.refs_0_.refs_5_.refs_3_, ...), custom_call_target="tpu_custom_call", output_to_operand_aliasing={{3}: (9, {}), {2}: (10, {})} | custom-call | flops 40000000000 | tf_op jit(solution)/shard_map/pallas_call | solution.py:223
  138.2 4.3 %collective-permute-start.23 = (bf16[1024,256]{1,0:T(8,128)(2,1)}, bf16[1024,256]{1,0:T(8,128)(2,1)S(1)}, u32[]{:S(2)}, u32[]{:S(2)}) collective-permute-start(bf16[1024,256]{1,0:T(8,128)(2,1)} %get-tuple-element.130.refs_6_.refs_0_), channel_id=1, source_target_pairs={{0,1},{1,0},{2,3},{3,2},{4,5},{5,4},{6,7},{7,6},{8,9},{9,8},{10,11... | collective-permute-start | bytes 1572872 | tf_op jit(solution)/shard_map/ppermute | solution.py:260
  155.2 8.7 %shard_map.34.refs_0_.refs_5_.refs_2_.refs_4_ = bf16[4,1024,256]{2,1,0:T(8,128)(2,1)} custom-call(s32[1]{0:T(128)} %constant.30.clone.1.where, bf16[512,2048]{1,0:T(8,128)(2,1)} %get-tuple-element.174.refs_0_.refs_2_, bf16[512,2048]{1,0:T(8,128)(2,1)} %get-tuple-element.173.refs_1_.refs_2_, bf16[1024,2048]{1,0:T(8,128)(2,1)} %all-gather.17.cloned.1.call-done.refs_2_.refs_7_), custom_call_target="tpu_custom_call" | custom-call | flops 4294967296 | tf_op jit(solution)/shard_map/pallas_call | solution.py:135
  190.6 3.8 %collective-permute-done.25.refs_2_.refs_5_ = bf16[1024,256]{1,0:T(8,128)(2,1)S(1)} collective-permute-done((bf16[1024,256]{1,0:T(8,128)(2,1)}, bf16[1024,256]{1,0:T(8,128)(2,1)S(1)}, u32[]{:S(2)}, u32[]{:S(2)}) %collective-permute-start.25) | collective-permute-done | bytes 524320 | tf_op jit(solution)/shard_map/ppermute | solution.py:260
  195.4 3.6 %shard_map.38 = (bf16[1024,256]{1,0:T(8,128)(2,1)}, bf16[1024,256]{1,0:T(8,128)(2,1)}, bf16[1024,1024]{1,0:T(8,128)(2,1)}, f32[8,128]{1,0:T(8,128)}) custom-call(s32[2]{0:T(128)} %pad_add_fusion.where, bf16[4,1024,256]{2,1,0:T(8,128)(2,1)} %shard_map.34.refs_0_.refs_5_.refs_2_.refs_4_, ...), custom_call_target="tpu_custom_call", output_to_operand_aliasing={{3}: (9, {}), {2}: (10, {})} | custom-call | flops 40000000000 | tf_op jit(solution)/shard_map/pallas_call | solution.py:223
  198.9 4.1 %collective-permute-start.29 = (bf16[1024,256]{1,0:T(8,128)(2,1)}, bf16[1024,256]{1,0:T(8,128)(2,1)S(1)}, u32[]{:S(2)}, u32[]{:S(2)}) collective-permute-start(bf16[1024,256]{1,0:T(8,128)(2,1)} %get-tuple-element.144.refs_5_.refs_0_), channel_id=1, source_target_pairs={{0,1},{1,0},{2,3},{3,2},{4,5},{5,4},{6,7},{7,6},{8,9},{9,8},{10,11... | collective-permute-start | bytes 1572872 | tf_op jit(solution)/shard_map/ppermute | solution.py:260
  221.0 3.5 %collective-permute-start.33 = (bf16[1024,256]{1,0:T(8,128)(2,1)}, bf16[1024,256]{1,0:T(8,128)(2,1)S(1)}, u32[]{:S(2)}, u32[]{:S(2)}) collective-permute-start(bf16[1024,256]{1,0:T(8,128)(2,1)} %get-tuple-element.154.refs_4_), channel_id=1, source_target_pairs={{0,1},{1,0},{2,3},{3,2},{4,5},{5,4},{6,7},{7,6},{8,9},{9,8},{10,11... | collective-permute-start | bytes 1572872 | tf_op jit(solution)/shard_map/ppermute | solution.py:260
  235.4 7.2 %collective-permute-done.35.refs_6_ = bf16[1024,1024]{1,0:T(8,128)(2,1)} collective-permute-done((bf16[1024,1024]{1,0:T(8,128)(2,1)S(1)}, bf16[1024,1024]{1,0:T(8,128)(2,1)}, u32[]{:S(2)}, u32[]{:S(2)}) %collective-permute-start.35) | collective-permute-done | bytes 2097184 | tf_op jit(solution)/shard_map/ppermute | solution.py:248
  248.1 16.0 %shard_map.43.refs_4_ = f32[1024,2048]{1,0:T(8,128)} custom-call(bf16[1024,1024]{1,0:T(8,128)(2,1)} %get-tuple-element.129.refs_0_.refs_4_.refs_8_.refs_10_, bf16[2048,1024]{1,0:T(8,128)(2,1)} %get-tuple-element.164.refs_1_, bf16[1024,1024]{1,0:T(8,128)(2,1)} %get-tuple-element.156.refs_2_.refs_5_.refs_12_.refs_14_, ...), custom_call_target="tpu_custom_call" | custom-call | flops 8589934592 | tf_op jit(solution)/shard_map/pallas_call | solution.py:103
  271.4 15.0 %shard_map.47.refs_4_ = bf16[1024,1024]{1,0:T(8,128)(2,1)} custom-call(bf16[1024,1024]{1,0:T(8,128)(2,1)} %get-tuple-element.153.refs_0_.refs_2_.refs_16_, bf16[2048,1024]{1,0:T(8,128)(2,1)} %get-tuple-element.171.refs_1_.refs_3_.refs_5_.refs_7_, bf16[1024,1024]{1,0:T(8,128)(2,1)} %get-tuple-element.153.refs_0_.refs_2_.refs_16_, ...), custom_call_target="tpu_custom_call" | custom-call | flops 8589934592 | tf_op jit(solution)/shard_map/pallas_call | solution.py:103
  286.5 15.0 %shard_map.48.refs_6_ = bf16[1024,1024]{1,0:T(8,128)(2,1)} custom-call(bf16[1024,1024]{1,0:T(8,128)(2,1)} %get-tuple-element.153.refs_0_.refs_2_.refs_16_, bf16[2048,1024]{1,0:T(8,128)(2,1)} %all-gather.29.cloned.1.call-done.refs_1_.refs_3_.refs_5_.refs_7_, bf16[1024,1024]{1,0:T(8,128)(2,1)} %get-tuple-element.153.refs_0_.refs_2_.refs_16_, ...), custom_call_target="tpu_custom_call" | custom-call | flops 8589934592 | tf_op jit(solution)/shard_map/pallas_call | solution.py:103
  301.4 14.7 %shard_map.46.refs_0_.refs_2_ = bf16[1024,2048]{1,0:T(8,128)(2,1)} custom-call(bf16[1024,1024]{1,0:T(8,128)(2,1)} %get-tuple-element.153.refs_0_.refs_2_.refs_16_, bf16[2048,1024]{1,0:T(8,128)(2,1)} %all-gather.23.cloned.1.call-done.refs_1_.refs_9_.refs_11_.refs_13_.refs_15_, bf16[1024,1024]{1,0:T(8,128)(2,1)} %get-tuple-element.169.refs_2_.refs_4_.refs_6_.refs_16_, ...), custom_call_target="tpu_custom_call" | custom-call | flops 8589934592 | tf_op jit(solution)/shard_map/pallas_call | solution.py:103
  316.2 24.8 %shard_map.49 = f32[1024,2048]{1,0:T(8,128)} custom-call(bf16[1024,2048]{1,0:T(8,128)(2,1)} %shard_map.46.refs_0_.refs_2_, bf16[1024,2048]{1,0:T(8,128)(2,1)} %all-gather.11.cloned.1.call-done.refs_2_.refs_1_, bf16[1024,2048]{1,0:T(8,128)(2,1)} %shard_map.46.refs_0_.refs_2_, bf16[1024,2048]{1,0:T(8,128)(2,1)} %all-gather.15.cloned.1.call-done.refs_2_.refs_3_, ...), custom_call_target="tpu_custom_call" | custom-call | flops 17179869184 | tf_op jit(solution)/shard_map/pallas_call | solution.py:103
  (184 shorter events, 149.4 us)
Async XLA Ops:
  6.5 26.1 %all-gather.11.cloned.1.call-start = ((), (), s32[]{:S(2)}) async-start(), calls=%async_computation | async-start | bytes 6291456 | tf_op jit(solution)/shard_map/all_gather | solution.py:252
  12.9 66.9 %all-gather.15.cloned.1.call-start = ((), (), s32[]{:S(2)}) async-start(), calls=%async_computation.2 | async-start | bytes 6291456 | tf_op jit(solution)/shard_map/all_gather | solution.py:252
  12.9 54.6 %collective-permute-start.3 = (bf16[512,2048]{1,0:T(8,128)(2,1)}, bf16[512,2048]{1,0:T(8,128)(2,1)}, u32[]{:S(2)}, u32[]{:S(2)}) collective-permute-start(bf16[512,2048]{1,0:T(8,128)(2,1)} %get-tuple-element.174.refs_0_.refs_2_), channel_id=1, source_target_pairs={{0,8},{4,12},{8,0},{12,4},{1,9},{5,13},{9,1},{13,5},{2,10},{6,14},... | collective-permute-start | bytes 6291464 | tf_op jit(solution)/shard_map/ppermute | solution.py:248
  29.7 22.3 %collective-permute-start.4 = (bf16[1024,256]{1,0:T(8,128)(2,1)}, bf16[1024,256]{1,0:T(8,128)(2,1)S(1)}, u32[]{:S(2)}, u32[]{:S(2)}) collective-permute-start(bf16[1024,256]{1,0:T(8,128)(2,1)} %get-tuple-element.95.refs_1_), channel_id=1, source_target_pairs={{0,1},{1,0},{2,3},{3,2},{4,5},{5,4},{6,7},{7,6},{8,9},{9,8},{10,11... | collective-permute-start | bytes 1572872 | tf_op jit(solution)/shard_map/ppermute | solution.py:260
  30.3 74.3 %all-gather.13.cloned.1.call-start = ((), (), s32[]{:S(2)}) async-start(), calls=%async_computation.1 | async-start | bytes 6291456 | tf_op jit(solution)/shard_map/all_gather | solution.py:252
  44.6 23.5 %collective-permute-start.1 = (bf16[1024,256]{1,0:T(8,128)(2,1)}, bf16[1024,256]{1,0:T(8,128)(2,1)S(1)}, u32[]{:S(2)}, u32[]{:S(2)}) collective-permute-start(bf16[1024,256]{1,0:T(8,128)(2,1)} %get-tuple-element.93), channel_id=1, source_target_pairs={{1,2},{2,1},{5,6},{6,5},{9,10},{10,9},{13,14},{14,13},{17,18},{18,... | collective-permute-start | bytes 1572872 | tf_op jit(solution)/shard_map/ppermute | solution.py:260
  45.3 22.8 %collective-permute-start.2 = (bf16[1024,256]{1,0:T(8,128)(2,1)}, bf16[1024,256]{1,0:T(8,128)(2,1)S(1)}, u32[]{:S(2)}, u32[]{:S(2)}) collective-permute-start(bf16[1024,256]{1,0:T(8,128)(2,1)} %get-tuple-element.94.refs_1_), channel_id=1, source_target_pairs={{0,1},{1,0},{2,3},{3,2},{4,5},{5,4},{6,7},{7,6},{8,9},{9,8},{10,11... | collective-permute-start | bytes 1572872 | tf_op jit(solution)/shard_map/ppermute | solution.py:260
  67.6 45.7 %collective-permute-start.15 = (bf16[512,2048]{1,0:T(8,128)(2,1)}, bf16[512,2048]{1,0:T(8,128)(2,1)}, u32[]{:S(2)}, u32[]{:S(2)}) collective-permute-start(bf16[512,2048]{1,0:T(8,128)(2,1)} %get-tuple-element.114), channel_id=1, source_target_pairs={{0,8},{4,12},{8,0},{12,4},{1,9},{5,13},{9,1},{13,5},{2,10},{6,14},... | collective-permute-start | bytes 6291464 | tf_op jit(solution)/shard_map/ppermute | solution.py:248
  79.7 75.4 %all-gather.17.cloned.1.call-start = ((), (), s32[]{:S(2)}) async-start(), calls=%async_computation.3 | async-start | bytes 6291456 | tf_op jit(solution)/shard_map/all_gather | solution.py:252
  102.4 22.4 %collective-permute-start.11 = (bf16[1024,256]{1,0:T(8,128)(2,1)}, bf16[1024,256]{1,0:T(8,128)(2,1)S(1)}, u32[]{:S(2)}, u32[]{:S(2)}) collective-permute-start(bf16[1024,256]{1,0:T(8,128)(2,1)} %get-tuple-element.110.refs_6_.refs_1_), channel_id=1, source_target_pairs={{0,1},{1,0},{2,3},{3,2},{4,5},{5,4},{6,7},{7,6},{8,9},{9,8},{10,11... | collective-permute-start | bytes 1572872 | tf_op jit(solution)/shard_map/ppermute | solution.py:260
  103.8 21.0 %collective-permute-start.12 = (bf16[1024,256]{1,0:T(8,128)(2,1)}, bf16[1024,256]{1,0:T(8,128)(2,1)S(1)}, u32[]{:S(2)}, u32[]{:S(2)}) collective-permute-start(bf16[1024,256]{1,0:T(8,128)(2,1)} %get-tuple-element.111), channel_id=1, source_target_pairs={{1,2},{2,1},{5,6},{6,5},{9,10},{10,9},{13,14},{14,13},{17,18},{18,... | collective-permute-start | bytes 1572872 | tf_op jit(solution)/shard_map/ppermute | solution.py:260
  117.8 56.3 %all-gather.19.cloned.1.call-start = ((), (), s32[]{:S(2)}) async-start(), calls=%async_computation.4 | async-start | bytes 6291456 | tf_op jit(solution)/shard_map/all_gather | solution.py:252
  131.9 42.1 %collective-permute-start.22 = (bf16[1024,1024]{1,0:T(8,128)(2,1)}, bf16[1024,1024]{1,0:T(8,128)(2,1)S(1)}, u32[]{:S(2)}, u32[]{:S(2)}) collective-permute-start(bf16[1024,1024]{1,0:T(8,128)(2,1)} %get-tuple-element.129.refs_0_.refs_4_.refs_8_.refs_10_), channel_id=1, source_target_pairs={{0,8},{4,12},{8,0},{12,4},{1,9},{5,13},{9,1},{13,5},{2,10},{6,14},... | collective-permute-start | bytes 6291464 | tf_op jit(solution)/shard_map/ppermute | solution.py:248
  133.5 83.4 %all-gather.21.cloned.1.call-start = ((), (), s32[]{:S(2)}) async-start(), calls=%async_computation.5 | async-start | bytes 6291456 | tf_op jit(solution)/shard_map/all_gather | solution.py:252
  138.2 25.7 %collective-permute-start.23 = (bf16[1024,256]{1,0:T(8,128)(2,1)}, bf16[1024,256]{1,0:T(8,128)(2,1)S(1)}, u32[]{:S(2)}, u32[]{:S(2)}) collective-permute-start(bf16[1024,256]{1,0:T(8,128)(2,1)} %get-tuple-element.130.refs_6_.refs_0_), channel_id=1, source_target_pairs={{0,1},{1,0},{2,3},{3,2},{4,5},{5,4},{6,7},{7,6},{8,9},{9,8},{10,11... | collective-permute-start | bytes 1572872 | tf_op jit(solution)/shard_map/ppermute | solution.py:260
  142.4 21.4 %collective-permute-start.24 = (bf16[1024,256]{1,0:T(8,128)(2,1)}, bf16[1024,256]{1,0:T(8,128)(2,1)}, u32[]{:S(2)}, u32[]{:S(2)}) collective-permute-start(bf16[1024,256]{1,0:T(8,128)(2,1)} %get-tuple-element.131), channel_id=1, source_target_pairs={{1,2},{2,1},{5,6},{6,5},{9,10},{10,9},{13,14},{14,13},{17,18},{18,... | collective-permute-start | bytes 1572872 | tf_op jit(solution)/shard_map/ppermute | solution.py:260
  182.1 46.0 %all-gather.25.cloned.1.call-start = ((), (), s32[]{:S(2)}) async-start(), calls=%async_computation.7 | async-start | bytes 6291456 | tf_op jit(solution)/shard_map/all_gather | solution.py:252
  204.4 38.1 %collective-permute-start.35 = (bf16[1024,1024]{1,0:T(8,128)(2,1)S(1)}, bf16[1024,1024]{1,0:T(8,128)(2,1)}, u32[]{:S(2)}, u32[]{:S(2)}) collective-permute-start(bf16[1024,1024]{1,0:T(8,128)(2,1)S(1)} %copy-done.1), channel_id=1, source_target_pairs={{0,8},{4,12},{8,0},{12,4},{1,9},{5,13},{9,1},{13,5},{2,10},{6,14},... | collective-permute-start | bytes 6291464 | tf_op jit(solution)/shard_map/ppermute | solution.py:248
  207.2 64.2 %all-gather.23.cloned.1.call-start = ((), (), s32[]{:S(2)}) async-start(), calls=%async_computation.6 | async-start | bytes 6291456 | tf_op jit(solution)/shard_map/all_gather | solution.py:252
  221.0 21.6 %collective-permute-start.33 = (bf16[1024,256]{1,0:T(8,128)(2,1)}, bf16[1024,256]{1,0:T(8,128)(2,1)S(1)}, u32[]{:S(2)}, u32[]{:S(2)}) collective-permute-start(bf16[1024,256]{1,0:T(8,128)(2,1)} %get-tuple-element.154.refs_4_), channel_id=1, source_target_pairs={{0,1},{1,0},{2,3},{3,2},{4,5},{5,4},{6,7},{7,6},{8,9},{9,8},{10,11... | collective-permute-start | bytes 1572872 | tf_op jit(solution)/shard_map/ppermute | solution.py:260
  226.0 60.4 %all-gather.29.cloned.1.call-start = ((), (), s32[]{:S(2)}) async-start(), calls=%async_computation.9 | async-start | bytes 6291456 | tf_op jit(solution)/shard_map/all_gather | solution.py:252
  232.0 32.1 %collective-permute-start.39 = (bf16[1024,256]{1,0:T(8,128)(2,1)}, bf16[1024,256]{1,0:T(8,128)(2,1)S(1)}, u32[]{:S(2)}, u32[]{:S(2)}) collective-permute-start(bf16[1024,256]{1,0:T(8,128)(2,1)} %get-tuple-element.163.refs_2_), channel_id=1, source_target_pairs={{0,1},{1,0},{2,3},{3,2},{4,5},{5,4},{6,7},{7,6},{8,9},{9,8},{10,11... | collective-permute-start | bytes 1572872 | tf_op jit(solution)/shard_map/ppermute | solution.py:260
  246.4 21.3 %collective-permute-start.38 = (bf16[1024,256]{1,0:T(8,128)(2,1)}, bf16[1024,256]{1,0:T(8,128)(2,1)S(1)}, u32[]{:S(2)}, u32[]{:S(2)}) collective-permute-start(bf16[1024,256]{1,0:T(8,128)(2,1)} %get-tuple-element.162.refs_2_), channel_id=1, source_target_pairs={{0,1},{1,0},{2,3},{3,2},{4,5},{5,4},{6,7},{7,6},{8,9},{9,8},{10,11... | collective-permute-start | bytes 1572872 | tf_op jit(solution)/shard_map/ppermute | solution.py:260
  248.1 38.4 %all-gather.27.cloned.1.call-start = ((), (), s32[]{:S(2)}) async-start(), calls=%async_computation.8 | async-start | bytes 6291456 | tf_op jit(solution)/shard_map/all_gather | solution.py:252
  (56 other events, 467.5 us)
Sparse Core Ops, SparseCore 0:
  13.0 16.3 all-gather.10
  30.9 14.8 all-gather.14
  79.8 15.8 all-gather.12
  117.9 15.9 all-gather.16
  135.2 14.8 all-gather.18
  182.2 13.0 all-gather.20
  207.3 12.3 all-gather.24
  226.1 14.4 all-gather.22
  248.2 13.5 all-gather.28
  271.5 13.3 all-gather.26
